TPU v7x, 32 devices: a whole 2x2x4 slice. The times are simulated.
32 devices in a mesh: row: 8 (over y, x, core), col: 4 (over z).
Axes of the slice: x: 2, y: 2, z: 4, core: 2. Of those that a mesh axis runs over, the one named last changes fastest.
Arguments:
- a_blocks: bfloat16 [64, 16, 128, 128], P('row', 'col'), may hold values from -0.125 to 0.125
- a_mask: int32 [64, 16], P('row', 'col'), may hold values 0 or 1
- b_blocks: bfloat16 [32, 32, 128, 128], P('row', 'col'), may hold values from -6 to 6
- b_mask: int32 [32, 32], P('row', 'col'), may hold values 0 or 1
- c_mask: int32 [64, 32], P('row', 'col'), may hold values 0 or 1
Outputs:
- product: bfloat16 [64, 32, 128, 128], P('row', 'col')
All inputs are finite; a program needn't handle non-finite values. No bound on the sum of `a_mask` or of `b_mask` or of `c_mask` on one device may be relied on, other than what follows from the above.
Results may differ from a plain program's by a relative error of at most 0.001.
Values may be sent and summed in bfloat16 or wider, within the bound.
No kernel may reach another device: no remote copies, remote signals or barrier semaphores. Data moves between devices by JAX's collectives and lax.ppermute only.
A program may use at most 64 MiB of HBM per device.

v0:
```python
import jax
import jax.numpy as jnp
from jax import lax
from jax.sharding import PartitionSpec as P

STEPS = 4


def from_behind(array, axis, by):
    size = lax.axis_size(axis)
    return lax.ppermute(array, axis, [(i, (i + by) % size) for i in range(size)])


def on_device(a_blocks, a_mask, b_blocks, b_mask, c_mask):
    a_live = a_blocks * a_mask[:, :, None, None].astype(jnp.bfloat16)
    b_live = b_blocks * b_mask[:, :, None, None].astype(jnp.bfloat16)
    left_slabs = [a_live]
    right_slabs = [b_live]
    a_current = a_live
    b_current = b_live
    for step in range(1, STEPS):
        a_current = from_behind(a_current, "col", -1)
        b_current = from_behind(b_current, "row", -1)
        left_slabs.append(a_current)
        right_slabs.append(b_current)
    left_all = jnp.concatenate(left_slabs, axis=1)
    right_all = jnp.concatenate(right_slabs, axis=0)
    total = jnp.einsum("ikxy,kjyz->ijxz", left_all, right_all, preferred_element_type=jnp.float32)
    keep = c_mask[:, :, None, None].astype(jnp.float32)
    return (total * keep).astype(jnp.bfloat16)


def solution(mesh):
    return jax.shard_map(
        on_device,
        mesh=mesh,
        in_specs=(
            P("row", "col", None, None),
            P("row", "col"),
            P("row", "col", None, None),
            P("row", "col"),
            P("row", "col"),
        ),
        out_specs=P("row", "col", None, None),
        check_vma=False,
    )
```

profile of v0, /device:TPU:26, one launch (start us, length us, event | category | flops | bytes accessed | tf_op | source)
XLA Modules:
  0.0 93.0 jit_solution(1472094370663768043)
XLA Ops:
  0.0 0.7 convert_element_type.15
  0.7 0.1 copy.6
  0.8 0.0 copy-start.3
  0.8 0.0 copy-start
  0.8 1.7 %copy.7 = bf16[4,8,128,128]{2,3,0,1:T(8,128)(2,1)S(1)} copy(bf16[4,8,128,128]{3,2,1,0:T(8,128)(2,1)} %param.7) | data formatting | bytes 2097152 | tf_op args[2]
  2.5 0.0 copy-start.2
  2.5 0.1 broadcast_multiply_fusion.1
  2.7 0.1 collective-permute-start
  2.7 0.0 copy-done.3
  2.8 0.1 copy.8
  2.8 0.0 copy-done
  2.9 0.1 broadcast_multiply_fusion
  3.0 0.0 copy-start.1
  3.0 0.5 collective-permute-start.3
  3.5 11.5 %collective-permute-done = bf16[4,8,128,128]{2,3,0,1:T(8,128)(2,1)} collective-permute-done((bf16[4,8,128,128]{2,3,0,1:T(8,128)(2,1)S(1)}, bf16[4,8,128,128]{2,3,0,1:T(8,128)(2,1)}, u32[]{:S(2)}, u32[]{:S(2)}) %collective-permute-start) | collective-permute-done | bytes 1048608 | tf_op jit(solution)/shard_map/ppermute | solution.py:11
  15.0 0.0 copy-done.1
  15.0 2.2 %collective-permute-start.1 = (bf16[4,8,128,128]{2,3,0,1:T(8,128)(2,1)}, bf16[4,8,128,128]{2,3,0,1:T(8,128)(2,1)S(1)}, u32[]{:S(2)}, u32[]{:S(2)}) collective-permute-start(bf16[4,8,128,128]{2,3,0,1:T(8,128)(2,1)} %collective-permute-done), channel_id=1, source_target_pairs={{0,28},{4,0},{8,4},{12,8},{16,12},{20,16},{24,20},{28,24},{1,29},{... | collective-permute-start | bytes 3145736 | tf_op jit(solution)/shard_map/ppermute | solution.py:11
  17.2 13.2 %collective-permute-done.3 = bf16[8,4,128,128]{3,2,1,0:T(8,128)(2,1)S(1)} collective-permute-done((bf16[8,4,128,128]{3,2,1,0:T(8,128)(2,1)S(1)}, bf16[8,4,128,128]{3,2,1,0:T(8,128)(2,1)S(1)}, u32[]{:S(2)}, u32[]{:S(2)}) %collective-permute-start.3) | collective-permute-done | bytes 1048608 | tf_op jit(solution)/shard_map/ppermute | solution.py:11
  30.4 0.0 copy-start.4
  30.4 0.0 collective-permute-start.4
  30.4 0.0 collective-permute-done.1
  30.4 0.0 copy-start.5
  30.4 1.3 %collective-permute-start.2 = (bf16[4,8,128,128]{2,3,0,1:T(8,128)(2,1)S(1)}, bf16[4,8,128,128]{2,3,0,1:T(8,128)(2,1)}, u32[]{:S(2)}, u32[]{:S(2)}) collective-permute-start(bf16[4,8,128,128]{2,3,0,1:T(8,128)(2,1)S(1)} %collective-permute-done.1), channel_id=1, source_target_pairs={{0,28},{4,0},{8,4},{12,8},{16,12},{20,16},{24,20},{28,24},{1,29},{... | collective-permute-start | bytes 3145736 | tf_op jit(solution)/shard_map/ppermute | solution.py:11
  31.7 25.3 %collective-permute-done.4 = bf16[8,4,128,128]{3,2,1,0:T(8,128)(2,1)S(1)} collective-permute-done((bf16[8,4,128,128]{3,2,1,0:T(8,128)(2,1)S(1)}, bf16[8,4,128,128]{3,2,1,0:T(8,128)(2,1)S(1)}, u32[]{:S(2)}, u32[]{:S(2)}) %collective-permute-start.4) | collective-permute-done | bytes 1048608 | tf_op jit(solution)/shard_map/ppermute | solution.py:11
  57.0 0.0 copy-done.4
  57.0 0.0 copy-start.6
  57.0 0.0 collective-permute-start.5
  57.0 0.0 copy-done.2
  57.0 0.1 copy.9
  57.1 0.0 collective-permute-done.2
  57.1 0.0 copy-done.5
  57.1 0.9 copy-done.6
  57.9 24.8 %collective-permute-done.5 = bf16[8,4,128,128]{3,2,1,0:T(8,128)(2,1)} collective-permute-done((bf16[8,4,128,128]{3,2,1,0:T(8,128)(2,1)S(1)}, bf16[8,4,128,128]{3,2,1,0:T(8,128)(2,1)}, u32[]{:S(2)}, u32[]{:S(2)}) %collective-permute-start.5) | collective-permute-done | bytes 1048608 | tf_op jit(solution)/shard_map/ppermute | solution.py:11
  82.8 7.6 %fusion.13 = bf16[8,8,128,128]{2,3,0,1:T(8,128)(2,1)S(1)} fusion(bf16[8,4,128,128]{3,2,1,0:T(8,128)(2,1)} %collective-permute-done.5, bf16[8,4,128,128]{3,2,1,0:T(8,128)(2,1)} %copy-done.6, bf16[8,4,128,128]{3,2,1,0:T(8,128)(2,1)} %copy-done.4, bf16[8,4,128,128]{3,2,1,0:T(8,128)(2,1)} %copy-done.1, bf16[4,8,128,128]{2,3,0,1:T(8,128)(2,1)} %collective-permute-done.2, ...), kind=kOutput, calls=%fused_computation.16 | convolution fusion | flops 4330618880 | bytes 10486016 | tf_op jit(solution)/shard_map/ikxy,kjyz->ijxz/dot_general | solution.py:28
  90.4 2.6 %copy.10 = bf16[8,8,128,128]{3,2,1,0:T(8,128)(2,1)} copy(bf16[8,8,128,128]{2,3,0,1:T(8,128)(2,1)S(1)} %fusion.13) | data formatting | bytes 4194304 | tf_op jit(solution)/shard_map/convert_element_type | solution.py:30
  (2 shorter events, 0.0 us)
Async XLA Ops:
  0.8 2.0 %copy-start.3 = (s32[8,4]{0,1:T(4,128)S(1)}, s32[8,4]{0,1:T(4,128)}, u32[]{:S(2)}) copy-start(s32[8,4]{0,1:T(4,128)} %param.6) | copy-start | bytes 388
  0.8 2.1 %copy-start = (bf16[8,4,128,128]{3,2,1,0:T(8,128)(2,1)S(1)}, bf16[8,4,128,128]{3,2,1,0:T(8,128)(2,1)}, u32[]{:S(2)}) copy-start(bf16[8,4,128,128]{3,2,1,0:T(8,128)(2,1)} %param.5) | copy-start | bytes 3145732
  2.5 54.5 %copy-start.2 = (s32[8,8]{1,0:T(8,128)S(1)}, s32[8,8]{1,0:T(8,128)}, u32[]{:S(2)}) copy-start(s32[8,8]{1,0:T(8,128)} %param.9) | copy-start | bytes 772
  2.7 12.4 %collective-permute-start = (bf16[4,8,128,128]{2,3,0,1:T(8,128)(2,1)S(1)}, bf16[4,8,128,128]{2,3,0,1:T(8,128)(2,1)}, u32[]{:S(2)}, u32[]{:S(2)}) collective-permute-start(bf16[4,8,128,128]{2,3,0,1:T(8,128)(2,1)S(1)} %broadcast_multiply_fusion.1), channel_id=1, source_target_pairs={{0,28},{4,0},{8,4},{12,8},{16,12},{20,16},{24,20},{28,24},{1,29},{... | collective-permute-start | bytes 3145736 | tf_op jit(solution)/shard_map/ppermute | solution.py:11
  3.0 12.0 %copy-start.1 = (bf16[8,4,128,128]{3,2,1,0:T(8,128)(2,1)}, bf16[8,4,128,128]{3,2,1,0:T(8,128)(2,1)S(1)}, u32[]{:S(2)}) copy-start(bf16[8,4,128,128]{3,2,1,0:T(8,128)(2,1)S(1)} %broadcast_multiply_fusion) | copy-start | bytes 3145732
  3.0 27.4 %collective-permute-start.3 = (bf16[8,4,128,128]{3,2,1,0:T(8,128)(2,1)S(1)}, bf16[8,4,128,128]{3,2,1,0:T(8,128)(2,1)S(1)}, u32[]{:S(2)}, u32[]{:S(2)}) collective-permute-start(bf16[8,4,128,128]{3,2,1,0:T(8,128)(2,1)S(1)} %broadcast_multiply_fusion), channel_id=1, source_target_pairs={{0,3},{1,0},{2,1},{3,2},{4,7},{5,4},{6,5},{7,6},{8,11},{9,8},{10,9... | collective-permute-start | bytes 3145736 | tf_op jit(solution)/shard_map/ppermute | solution.py:11
  15.0 15.4 %collective-permute-start.1 = (bf16[4,8,128,128]{2,3,0,1:T(8,128)(2,1)}, bf16[4,8,128,128]{2,3,0,1:T(8,128)(2,1)S(1)}, u32[]{:S(2)}, u32[]{:S(2)}) collective-permute-start(bf16[4,8,128,128]{2,3,0,1:T(8,128)(2,1)} %collective-permute-done), channel_id=1, source_target_pairs={{0,28},{4,0},{8,4},{12,8},{16,12},{20,16},{24,20},{28,24},{1,29},{... | collective-permute-start | bytes 3145736 | tf_op jit(solution)/shard_map/ppermute | solution.py:11
  30.4 26.6 %copy-start.4 = (bf16[8,4,128,128]{3,2,1,0:T(8,128)(2,1)}, bf16[8,4,128,128]{3,2,1,0:T(8,128)(2,1)S(1)}, u32[]{:S(2)}) copy-start(bf16[8,4,128,128]{3,2,1,0:T(8,128)(2,1)S(1)} %collective-permute-done.3) | copy-start | bytes 3145732
  30.4 26.6 %collective-permute-start.4 = (bf16[8,4,128,128]{3,2,1,0:T(8,128)(2,1)S(1)}, bf16[8,4,128,128]{3,2,1,0:T(8,128)(2,1)S(1)}, u32[]{:S(2)}, u32[]{:S(2)}) collective-permute-start(bf16[8,4,128,128]{3,2,1,0:T(8,128)(2,1)S(1)} %collective-permute-done.3), channel_id=1, source_target_pairs={{0,3},{1,0},{2,1},{3,2},{4,7},{5,4},{6,5},{7,6},{8,11},{9,8},{10,9... | collective-permute-start | bytes 3145736 | tf_op jit(solution)/shard_map/ppermute | solution.py:11
  30.4 26.7 %copy-start.5 = (bf16[4,8,128,128]{2,3,0,1:T(8,128)(2,1)}, bf16[4,8,128,128]{2,3,0,1:T(8,128)(2,1)S(1)}, u32[]{:S(2)}) copy-start(bf16[4,8,128,128]{2,3,0,1:T(8,128)(2,1)S(1)} %collective-permute-done.1) | copy-start | bytes 3145732
  30.4 26.7 %collective-permute-start.2 = (bf16[4,8,128,128]{2,3,0,1:T(8,128)(2,1)S(1)}, bf16[4,8,128,128]{2,3,0,1:T(8,128)(2,1)}, u32[]{:S(2)}, u32[]{:S(2)}) collective-permute-start(bf16[4,8,128,128]{2,3,0,1:T(8,128)(2,1)S(1)} %collective-permute-done.1), channel_id=1, source_target_pairs={{0,28},{4,0},{8,4},{12,8},{16,12},{20,16},{24,20},{28,24},{1,29},{... | collective-permute-start | bytes 3145736 | tf_op jit(solution)/shard_map/ppermute | solution.py:11
  57.0 1.0 %copy-start.6 = (bf16[8,4,128,128]{3,2,1,0:T(8,128)(2,1)}, bf16[8,4,128,128]{3,2,1,0:T(8,128)(2,1)S(1)}, u32[]{:S(2)}) copy-start(bf16[8,4,128,128]{3,2,1,0:T(8,128)(2,1)S(1)} %collective-permute-done.4) | copy-start | bytes 3145732
  57.0 25.8 %collective-permute-start.5 = (bf16[8,4,128,128]{3,2,1,0:T(8,128)(2,1)S(1)}, bf16[8,4,128,128]{3,2,1,0:T(8,128)(2,1)}, u32[]{:S(2)}, u32[]{:S(2)}) collective-permute-start(bf16[8,4,128,128]{3,2,1,0:T(8,128)(2,1)S(1)} %collective-permute-done.4), channel_id=1, source_target_pairs={{0,3},{1,0},{2,1},{3,2},{4,7},{5,4},{6,5},{7,6},{8,11},{9,8},{10,9... | collective-permute-start | bytes 3145736 | tf_op jit(solution)/shard_map/ppermute | solution.py:11
where the time goes:
time: 93.1 us; the launch traced here: 93 us
  waiting for transfers between devices  74.8 us (80%)
  matrix products  7.62 us (8%)
  local copies, waits for them, and re-layouts  5.47 us (6%)
  starting transfers between devices  4.03 us (4%)
  other arithmetic  0.96 us (1%)
    ppermute x6, waiting for transfers between devices, from_behind(): lax.ppermute(array, axis, [(i, (i + by) % size) for i in range(size)])  74.8 us
    dot_general x1, matrix products, on_device(): jnp.einsum('ikxy,kjyz->ijxz', left_all, right_all, preferred_element_type...  7.62 us
    ppermute x6, starting transfers between devices, from_behind(): lax.ppermute(array, axis, [(i, (i + by) % size) for i in range(size)])  4.03 us
    unnamed x15, local copies, waits for them, and re-layouts  2.61 us
    convert_element_type x1, local copies, waits for them, and re-layouts, on_device(): return (total * keep).astype(jnp.bfloat16)  2.6 us
  transfers between devices with their start and end apart: 6, of which 4 were waited for; matrix products, arithmetic and copies ran while one was open for 0% of the time, Pallas kernels for 0%

commit v1 on v0

v1 whole, which is shorter than its diff:
```python
import functools

import jax
import jax.numpy as jnp
from jax import lax
from jax.experimental import pallas as pl
from jax.experimental.pallas import tpu as pltpu
from jax.sharding import PartitionSpec as P

STEPS = 4
HALVES = 2


def from_behind(array, axis, by):
    size = lax.axis_size(axis)
    return lax.ppermute(array, axis, [(i, (i + by) % size) for i in range(size)])


def wide(a_refs, rows):
    kb = a_refs[0].shape[1]
    blk = a_refs[0].shape[-1]
    columns = []
    for k in range(kb):
        columns.append(jnp.concatenate([a[:, k].reshape(-1, blk) for a in a_refs], axis=0))
    return jnp.concatenate(columns, axis=1)


def tall(b_ref):
    kb, bc = b_ref.shape[:2]
    return jnp.concatenate(
        [jnp.concatenate([b_ref[k, j] for j in range(bc)], axis=1) for k in range(kb)], axis=0
    )


def first_kernel(steps, *refs):
    a_refs, b_refs, acc_ref = refs[: HALVES * steps], refs[HALVES * steps : -1], refs[-1]
    total = None
    for t in range(steps):
        part = jnp.dot(
            wide(a_refs[HALVES * t : HALVES * (t + 1)], None), tall(b_refs[t]), preferred_element_type=jnp.float32
        )
        total = part if total is None else total + part
    acc_ref[...] = total


def last_kernel(c_ref, acc_ref, *refs):
    a_refs, b_ref, out_ref = refs[:HALVES], refs[HALVES], refs[-1]
    blk = out_ref.shape[-1]
    total = acc_ref[...] + jnp.dot(wide(a_refs, None), tall(b_ref), preferred_element_type=jnp.float32)
    j0 = pl.program_id(0) * out_ref.shape[1]
    for i in range(out_ref.shape[0]):
        for j in range(out_ref.shape[1]):
            keep = c_ref[i, j0 + j].astype(jnp.float32)
            out_ref[i, j] = (total[i * blk : (i + 1) * blk, j * blk : (j + 1) * blk] * keep).astype(out_ref.dtype)


def on_device(a_blocks, a_mask, b_blocks, b_mask, c_mask):
    br, kb, blk, _ = a_blocks.shape
    bc = b_blocks.shape[1]
    a_live = a_blocks * a_mask[:, :, None, None].astype(jnp.bfloat16)
    b_live = b_blocks * b_mask[:, :, None, None].astype(jnp.bfloat16)
    size = br // HALVES
    left = [[a_live[h * size : (h + 1) * size] for h in range(HALVES)]]
    right = [b_live]
    for step in range(1, STEPS):
        left.append([from_behind(part, "col", -1) for part in left[-1]])
        right.append(from_behind(right[-1], "row", -1))

    wide_j = 2
    grid = (bc // wide_j,)
    a_spec = pl.BlockSpec((size, kb, blk, blk), lambda g: (0, 0, 0, 0))
    b_spec = pl.BlockSpec((kb, wide_j, blk, blk), lambda g: (0, g, 0, 0))
    acc_spec = pl.BlockSpec((br * blk, wide_j * blk), lambda g: (0, g))
    done = STEPS - 1
    acc = pl.pallas_call(
        functools.partial(first_kernel, done),
        grid=grid,
        in_specs=[a_spec] * (HALVES * done) + [b_spec] * done,
        out_specs=acc_spec,
        out_shape=jax.ShapeDtypeStruct((br * blk, bc * blk), jnp.float32),
        compiler_params=pltpu.CompilerParams(vmem_limit_bytes=40 * 1024 * 1024),
        cost_estimate=pl.CostEstimate(flops=2 * br * blk * bc * blk * kb * blk * done, bytes_accessed=10 << 20, transcendentals=0),
    )(*[part for parts in left[:done] for part in parts], *right[:done])
    return pl.pallas_call(
        last_kernel,
        grid=grid,
        in_specs=[pl.BlockSpec(memory_space=pltpu.SMEM), acc_spec] + [a_spec] * HALVES + [b_spec],
        out_specs=pl.BlockSpec((br, wide_j, blk, blk), lambda g: (0, g, 0, 0)),
        out_shape=jax.ShapeDtypeStruct((br, bc, blk, blk), jnp.bfloat16),
        compiler_params=pltpu.CompilerParams(vmem_limit_bytes=40 * 1024 * 1024),
        cost_estimate=pl.CostEstimate(flops=2 * br * blk * bc * blk * kb * blk, bytes_accessed=8 << 20, transcendentals=0),
    )(c_mask, acc, *left[done], right[done])


def solution(mesh):
    return jax.shard_map(
        on_device,
        mesh=mesh,
        in_specs=(
            P("row", "col", None, None),
            P("row", "col"),
            P("row", "col", None, None),
            P("row", "col"),
            P("row", "col"),
        ),
        out_specs=P("row", "col", None, None),
        check_vma=False,
    )
```

time: 93.1 us -> 95 us (1.020)
  the two profiles are of different devices: /device:TPU:26 before, /device:TPU:0 now
where the time goes in v1:
time: 95 us; the launch traced here: 94.7 us
  waiting for transfers between devices  54.7 us (58%)
  starting transfers between devices  27.4 us (29%)
  Pallas kernels  8.28 us (9%)
  other arithmetic  4.08 us (4%)
    ppermute x9, waiting for transfers between devices, from_behind(): lax.ppermute(array, axis, [(i, (i + by) % size) for i in range(size)])  54.7 us
    ppermute x9, starting transfers between devices, from_behind(): lax.ppermute(array, axis, [(i, (i + by) % size) for i in range(size)])  27.4 us
    pallas_call x1, Pallas kernels, on_device(): pl.pallas_call(functools.partial(first_kernel, done), grid=grid, in_specs...  4.46 us
    pallas_call x1, Pallas kernels, on_device(): pl.pallas_call(last_kernel, grid=grid, in_specs=[pl.BlockSpec(memory_spac...  3.82 us
  transfers between devices with their start and end apart: 9, of which 7 were waited for; matrix products, arithmetic and copies ran while one was open for 2% of the time, Pallas kernels for 5%

profile of v1, /device:TPU:0, one launch (start us, length us, event | category | flops | bytes accessed | tf_op | source)
XLA Modules:
  0.0 94.7 jit_solution(7655225708288648622)
XLA Ops:
  0.0 0.7 convert_element_type.9
  0.7 1.4 %broadcast_multiply_fusion.refs_6_ = bf16[4,8,128,128]{3,2,1,0:T(8,128)(2,1)S(1)} fusion(bf16[4,8,128,128]{3,2,1,0:T(8,128)(2,1)} %param.7, bf16[4,8]{1,0:T(4,128)(2,1)S(1)} %convert_element_type.9), kind=kLoop, calls=%fused_computation | loop fusion | flops 524288 | bytes 2097216 | tf_op jit(solution)/shard_map/mul | solution.py:61
  2.1 3.4 %collective-permute-start.4 = (bf16[4,8,128,128]{3,2,1,0:T(8,128)(2,1)S(1)}, bf16[4,8,128,128]{3,2,1,0:T(8,128)(2,1)S(1)}, u32[]{:S(2)}, u32[]{:S(2)}) collective-permute-start(bf16[4,8,128,128]{3,2,1,0:T(8,128)(2,1)S(1)} %broadcast_multiply_fusion.refs_6_), channel_id=1, source_target_pairs={{0,28},{4,0},{8,4},{12,8},{16,12},{20,16},{24,20},{28,24},{1,29},{... | collective-permute-start | bytes 3145736 | tf_op jit(solution)/shard_map/ppermute | solution.py:16
  5.4 0.7 convert_element_type.8
  6.1 0.1 copy.6
  6.2 11.5 %collective-permute-done.4.refs_7_ = bf16[4,8,128,128]{3,2,1,0:T(8,128)(2,1)S(1)} collective-permute-done((bf16[4,8,128,128]{3,2,1,0:T(8,128)(2,1)S(1)}, bf16[4,8,128,128]{3,2,1,0:T(8,128)(2,1)S(1)}, u32[]{:S(2)}, u32[]{:S(2)}) %collective-permute-start.4) | collective-permute-done | bytes 1048608 | tf_op jit(solution)/shard_map/ppermute | solution.py:16
  17.8 2.8 %collective-permute-start.5 = (bf16[4,8,128,128]{3,2,1,0:T(8,128)(2,1)S(1)}, bf16[4,8,128,128]{3,2,1,0:T(8,128)(2,1)S(1)}, u32[]{:S(2)}, u32[]{:S(2)}) collective-permute-start(bf16[4,8,128,128]{3,2,1,0:T(8,128)(2,1)S(1)} %collective-permute-done.4.refs_7_), channel_id=1, source_target_pairs={{0,28},{4,0},{8,4},{12,8},{16,12},{20,16},{24,20},{28,24},{1,29},{... | collective-permute-start | bytes 3145736 | tf_op jit(solution)/shard_map/ppermute | solution.py:16
  20.6 1.4 %broadcast_multiply_fusion.1 = bf16[8,4,128,128]{3,2,1,0:T(8,128)(2,1)S(1)} fusion(bf16[8,4,128,128]{3,2,1,0:T(8,128)(2,1)} %param.5, bf16[8,4]{1,0:T(8,128)(2,1)S(1)} %copy.6), kind=kLoop, calls=%fused_computation.1 | loop fusion | flops 524288 | bytes 2097216 | tf_op jit(solution)/shard_map/mul | solution.py:60
  21.9 0.1 fusion
  22.0 3.7 %collective-permute-start = (bf16[4,4,128,128]{3,2,1,0:T(8,128)(2,1)S(1)}, bf16[4,4,128,128]{3,2,1,0:T(8,128)(2,1)S(1)}, u32[]{:S(2)}, u32[]{:S(2)}) collective-permute-start(bf16[4,4,128,128]{3,2,1,0:T(8,128)(2,1)S(1)} %get-tuple-element.6.refs_0_), channel_id=1, source_target_pairs={{0,3},{1,0},{2,1},{3,2},{4,7},{5,4},{6,5},{7,6},{8,11},{9,8},{10,9... | collective-permute-start | bytes 1572872 | tf_op jit(solution)/shard_map/ppermute | solution.py:16
  25.7 0.0 copy-start
  25.7 0.4 collective-permute-start.1
  26.1 11.9 %collective-permute-done.refs_2_ = bf16[4,4,128,128]{3,2,1,0:T(8,128)(2,1)S(1)} collective-permute-done((bf16[4,4,128,128]{3,2,1,0:T(8,128)(2,1)S(1)}, bf16[4,4,128,128]{3,2,1,0:T(8,128)(2,1)S(1)}, u32[]{:S(2)}, u32[]{:S(2)}) %collective-permute-start) | collective-permute-done | bytes 524320 | tf_op jit(solution)/shard_map/ppermute | solution.py:16
  38.1 4.3 %collective-permute-start.2 = (bf16[4,4,128,128]{3,2,1,0:T(8,128)(2,1)S(1)}, bf16[4,4,128,128]{3,2,1,0:T(8,128)(2,1)S(1)}, u32[]{:S(2)}, u32[]{:S(2)}) collective-permute-start(bf16[4,4,128,128]{3,2,1,0:T(8,128)(2,1)S(1)} %collective-permute-done.refs_2_), channel_id=1, source_target_pairs={{0,3},{1,0},{2,1},{3,2},{4,7},{5,4},{6,5},{7,6},{8,11},{9,8},{10,9... | collective-permute-start | bytes 1572872 | tf_op jit(solution)/shard_map/ppermute | solution.py:16
  42.4 7.0 %collective-permute-done.1.refs_3_ = bf16[4,4,128,128]{3,2,1,0:T(8,128)(2,1)S(1)} collective-permute-done((bf16[4,4,128,128]{3,2,1,0:T(8,128)(2,1)S(1)}, bf16[4,4,128,128]{3,2,1,0:T(8,128)(2,1)S(1)}, u32[]{:S(2)}, u32[]{:S(2)}) %collective-permute-start.1) | collective-permute-done | bytes 524320 | tf_op jit(solution)/shard_map/ppermute | solution.py:16
  49.3 4.3 %collective-permute-start.3 = (bf16[4,4,128,128]{3,2,1,0:T(8,128)(2,1)S(1)}, bf16[4,4,128,128]{3,2,1,0:T(8,128)(2,1)S(1)}, u32[]{:S(2)}, u32[]{:S(2)}) collective-permute-start(bf16[4,4,128,128]{3,2,1,0:T(8,128)(2,1)S(1)} %collective-permute-done.1.refs_3_), channel_id=1, source_target_pairs={{0,3},{1,0},{2,1},{3,2},{4,7},{5,4},{6,5},{7,6},{8,11},{9,8},{10,9... | collective-permute-start | bytes 1572872 | tf_op jit(solution)/shard_map/ppermute | solution.py:16
  53.6 0.0 collective-permute-done.5.refs_8_
  53.6 0.0 collective-permute-start.8
  53.6 6.9 %collective-permute-done.2.refs_4_ = bf16[4,4,128,128]{3,2,1,0:T(8,128)(2,1)S(1)} collective-permute-done((bf16[4,4,128,128]{3,2,1,0:T(8,128)(2,1)S(1)}, bf16[4,4,128,128]{3,2,1,0:T(8,128)(2,1)S(1)}, u32[]{:S(2)}, u32[]{:S(2)}) %collective-permute-start.2) | collective-permute-done | bytes 524320 | tf_op jit(solution)/shard_map/ppermute | solution.py:16
  60.5 4.3 %collective-permute-start.6 = (bf16[4,4,128,128]{3,2,1,0:T(8,128)(2,1)S(1)}, bf16[4,4,128,128]{3,2,1,0:T(8,128)(2,1)S(1)}, u32[]{:S(2)}, u32[]{:S(2)}) collective-permute-start(bf16[4,4,128,128]{3,2,1,0:T(8,128)(2,1)S(1)} %collective-permute-done.2.refs_4_), channel_id=1, source_target_pairs={{0,3},{1,0},{2,1},{3,2},{4,7},{5,4},{6,5},{7,6},{8,11},{9,8},{10,9... | collective-permute-start | bytes 1572872 | tf_op jit(solution)/shard_map/ppermute | solution.py:16
  64.8 7.0 %collective-permute-done.3.refs_5_ = bf16[4,4,128,128]{3,2,1,0:T(8,128)(2,1)S(1)} collective-permute-done((bf16[4,4,128,128]{3,2,1,0:T(8,128)(2,1)S(1)}, bf16[4,4,128,128]{3,2,1,0:T(8,128)(2,1)S(1)}, u32[]{:S(2)}, u32[]{:S(2)}) %collective-permute-start.3) | collective-permute-done | bytes 524320 | tf_op jit(solution)/shard_map/ppermute | solution.py:16
  71.8 4.3 %collective-permute-start.7 = (bf16[4,4,128,128]{3,2,1,0:T(8,128)(2,1)S(1)}, bf16[4,4,128,128]{3,2,1,0:T(8,128)(2,1)S(1)}, u32[]{:S(2)}, u32[]{:S(2)}) collective-permute-start(bf16[4,4,128,128]{3,2,1,0:T(8,128)(2,1)S(1)} %collective-permute-done.3.refs_5_), channel_id=1, source_target_pairs={{0,3},{1,0},{2,1},{3,2},{4,7},{5,4},{6,5},{7,6},{8,11},{9,8},{10,9... | collective-permute-start | bytes 1572872 | tf_op jit(solution)/shard_map/ppermute | solution.py:16
  76.1 4.5 %shard_map.55.acc_ref = f32[1024,1024]{1,0:T(8,128)S(1)} custom-call(bf16[4,4,128,128]{3,2,1,0:T(8,128)(2,1)S(1)} %get-tuple-element.6.refs_0_, bf16[4,4,128,128]{3,2,1,0:T(8,128)(2,1)S(1)} %get-tuple-element.5.refs_1_, bf16[4,4,128,128]{3,2,1,0:T(8,128)(2,1)S(1)} %collective-permute-done.refs_2_, ...), custom_call_target="tpu_custom_call" | custom-call | flops 3221225472 | bytes 10485760 | tf_op jit(solution)/shard_map/pallas_call | solution.py:75
  80.5 2.5 %collective-permute-done.6.refs_0_ = bf16[4,4,128,128]{3,2,1,0:T(8,128)(2,1)S(1)} collective-permute-done((bf16[4,4,128,128]{3,2,1,0:T(8,128)(2,1)S(1)}, bf16[4,4,128,128]{3,2,1,0:T(8,128)(2,1)S(1)}, u32[]{:S(2)}, u32[]{:S(2)}) %collective-permute-start.6) | collective-permute-done | bytes 524320 | tf_op jit(solution)/shard_map/ppermute | solution.py:16
  83.0 7.9 %collective-permute-done.7.refs_1_ = bf16[4,4,128,128]{3,2,1,0:T(8,128)(2,1)S(1)} collective-permute-done((bf16[4,4,128,128]{3,2,1,0:T(8,128)(2,1)S(1)}, bf16[4,4,128,128]{3,2,1,0:T(8,128)(2,1)S(1)}, u32[]{:S(2)}, u32[]{:S(2)}) %collective-permute-start.7) | collective-permute-done | bytes 524320 | tf_op jit(solution)/shard_map/ppermute | solution.py:16
  90.9 0.0 collective-permute-done.8.refs_2_
  90.9 0.0 copy-done
  90.9 3.8 %shard_map.56 = bf16[8,8,128,128]{3,2,1,0:T(8,128)(2,1)} custom-call(s32[8,8]{1,0:T(8,128)S(1)} %copy-done, f32[1024,1024]{1,0:T(8,128)S(1)} %shard_map.55.acc_ref, bf16[4,4,128,128]{3,2,1,0:T(8,128)(2,1)S(1)} %collective-permute-done.6.refs_0_, bf16[4,4,128,128]{3,2,1,0:T(8,128)(2,1)S(1)} %collective-permute-done.7.refs_1_, ...), custom_call_target="tpu_custom_call" | custom-call | flops 1073741824 | bytes 8388608 | tf_op jit(solution)/shard_map/pallas_call | solution.py:84
Async XLA Ops:
  2.1 15.7 %collective-permute-start.4 = (bf16[4,8,128,128]{3,2,1,0:T(8,128)(2,1)S(1)}, bf16[4,8,128,128]{3,2,1,0:T(8,128)(2,1)S(1)}, u32[]{:S(2)}, u32[]{:S(2)}) collective-permute-start(bf16[4,8,128,128]{3,2,1,0:T(8,128)(2,1)S(1)} %broadcast_multiply_fusion.refs_6_), channel_id=1, source_target_pairs={{0,28},{4,0},{8,4},{12,8},{16,12},{20,16},{24,20},{28,24},{1,29},{... | collective-permute-start | bytes 3145736 | tf_op jit(solution)/shard_map/ppermute | solution.py:16
  17.8 35.8 %collective-permute-start.5 = (bf16[4,8,128,128]{3,2,1,0:T(8,128)(2,1)S(1)}, bf16[4,8,128,128]{3,2,1,0:T(8,128)(2,1)S(1)}, u32[]{:S(2)}, u32[]{:S(2)}) collective-permute-start(bf16[4,8,128,128]{3,2,1,0:T(8,128)(2,1)S(1)} %collective-permute-done.4.refs_7_), channel_id=1, source_target_pairs={{0,28},{4,0},{8,4},{12,8},{16,12},{20,16},{24,20},{28,24},{1,29},{... | collective-permute-start | bytes 3145736 | tf_op jit(solution)/shard_map/ppermute | solution.py:16
  22.0 16.0 %collective-permute-start = (bf16[4,4,128,128]{3,2,1,0:T(8,128)(2,1)S(1)}, bf16[4,4,128,128]{3,2,1,0:T(8,128)(2,1)S(1)}, u32[]{:S(2)}, u32[]{:S(2)}) collective-permute-start(bf16[4,4,128,128]{3,2,1,0:T(8,128)(2,1)S(1)} %get-tuple-element.6.refs_0_), channel_id=1, source_target_pairs={{0,3},{1,0},{2,1},{3,2},{4,7},{5,4},{6,5},{7,6},{8,11},{9,8},{10,9... | collective-permute-start | bytes 1572872 | tf_op jit(solution)/shard_map/ppermute | solution.py:16
  25.7 65.2 %copy-start = (s32[8,8]{1,0:T(8,128)S(1)}, s32[8,8]{1,0:T(8,128)}, u32[]{:S(2)}) copy-start(s32[8,8]{1,0:T(8,128)} %c_ref.1) | copy-start | bytes 772
  25.7 23.6 %collective-permute-start.1 = (bf16[4,4,128,128]{3,2,1,0:T(8,128)(2,1)S(1)}, bf16[4,4,128,128]{3,2,1,0:T(8,128)(2,1)S(1)}, u32[]{:S(2)}, u32[]{:S(2)}) collective-permute-start(bf16[4,4,128,128]{3,2,1,0:T(8,128)(2,1)S(1)} %get-tuple-element.5.refs_1_), channel_id=1, source_target_pairs={{0,3},{1,0},{2,1},{3,2},{4,7},{5,4},{6,5},{7,6},{8,11},{9,8},{10,9... | collective-permute-start | bytes 1572872 | tf_op jit(solution)/shard_map/ppermute | solution.py:16
  38.1 22.5 %collective-permute-start.2 = (bf16[4,4,128,128]{3,2,1,0:T(8,128)(2,1)S(1)}, bf16[4,4,128,128]{3,2,1,0:T(8,128)(2,1)S(1)}, u32[]{:S(2)}, u32[]{:S(2)}) collective-permute-start(bf16[4,4,128,128]{3,2,1,0:T(8,128)(2,1)S(1)} %collective-permute-done.refs_2_), channel_id=1, source_target_pairs={{0,3},{1,0},{2,1},{3,2},{4,7},{5,4},{6,5},{7,6},{8,11},{9,8},{10,9... | collective-permute-start | bytes 1572872 | tf_op jit(solution)/shard_map/ppermute | solution.py:16
  49.3 22.5 %collective-permute-start.3 = (bf16[4,4,128,128]{3,2,1,0:T(8,128)(2,1)S(1)}, bf16[4,4,128,128]{3,2,1,0:T(8,128)(2,1)S(1)}, u32[]{:S(2)}, u32[]{:S(2)}) collective-permute-start(bf16[4,4,128,128]{3,2,1,0:T(8,128)(2,1)S(1)} %collective-permute-done.1.refs_3_), channel_id=1, source_target_pairs={{0,3},{1,0},{2,1},{3,2},{4,7},{5,4},{6,5},{7,6},{8,11},{9,8},{10,9... | collective-permute-start | bytes 1572872 | tf_op jit(solution)/shard_map/ppermute | solution.py:16
  53.6 37.3 %collective-permute-start.8 = (bf16[4,8,128,128]{3,2,1,0:T(8,128)(2,1)S(1)}, bf16[4,8,128,128]{3,2,1,0:T(8,128)(2,1)S(1)}, u32[]{:S(2)}, u32[]{:S(2)}) collective-permute-start(bf16[4,8,128,128]{3,2,1,0:T(8,128)(2,1)S(1)} %collective-permute-done.5.refs_8_), channel_id=1, source_target_pairs={{0,28},{4,0},{8,4},{12,8},{16,12},{20,16},{24,20},{28,24},{1,29},{... | collective-permute-start | bytes 3145736 | tf_op jit(solution)/shard_map/ppermute | solution.py:16
  60.5 22.5 %collective-permute-start.6 = (bf16[4,4,128,128]{3,2,1,0:T(8,128)(2,1)S(1)}, bf16[4,4,128,128]{3,2,1,0:T(8,128)(2,1)S(1)}, u32[]{:S(2)}, u32[]{:S(2)}) collective-permute-start(bf16[4,4,128,128]{3,2,1,0:T(8,128)(2,1)S(1)} %collective-permute-done.2.refs_4_), channel_id=1, source_target_pairs={{0,3},{1,0},{2,1},{3,2},{4,7},{5,4},{6,5},{7,6},{8,11},{9,8},{10,9... | collective-permute-start | bytes 1572872 | tf_op jit(solution)/shard_map/ppermute | solution.py:16
  71.8 19.1 %collective-permute-start.7 = (bf16[4,4,128,128]{3,2,1,0:T(8,128)(2,1)S(1)}, bf16[4,4,128,128]{3,2,1,0:T(8,128)(2,1)S(1)}, u32[]{:S(2)}, u32[]{:S(2)}) collective-permute-start(bf16[4,4,128,128]{3,2,1,0:T(8,128)(2,1)S(1)} %collective-permute-done.3.refs_5_), channel_id=1, source_target_pairs={{0,3},{1,0},{2,1},{3,2},{4,7},{5,4},{6,5},{7,6},{8,11},{9,8},{10,9... | collective-permute-start | bytes 1572872 | tf_op jit(solution)/shard_map/ppermute | solution.py:16

commit v2 on v0

v2 whole, which is shorter than its diff:
```python
import functools

import jax
import jax.numpy as jnp
from jax import lax
from jax.experimental import pallas as pl
from jax.experimental.pallas import tpu as pltpu
from jax.sharding import PartitionSpec as P

STEPS = 4
END_CHUNKS = 9
MID_CHUNKS = 7
VMEM = 48 * 1024 * 1024


def from_behind(array, axis, by):
    size = lax.axis_size(axis)
    return lax.ppermute(array, axis, [(i, (i + by) % size) for i in range(size)])


def smem():
    return pl.BlockSpec(memory_space=pltpu.SMEM)


def whole():
    return pl.BlockSpec(memory_space=pltpu.VMEM)


def params():
    return pltpu.CompilerParams(vmem_limit_bytes=VMEM)


def cost(flops, nbytes):
    return pl.CostEstimate(flops=int(flops), bytes_accessed=int(nbytes), transcendentals=0)


def wide(a_ref):
    kb, blk = a_ref.shape[1], a_ref.shape[-1]
    return jnp.concatenate([a_ref[:, k].reshape(-1, blk) for k in range(kb)], axis=1)


def tall(b_ref):
    kb, bc = b_ref.shape[:2]
    return jnp.concatenate(
        [jnp.concatenate([b_ref[k, j] for j in range(bc)], axis=1) for k in range(kb)], axis=0
    )


def dense_kernel(c_ref, *refs):
    a_refs, b_refs, out_ref = refs[:STEPS], refs[STEPS:-1], refs[-1]
    total = None
    for a_ref, b_ref in zip(a_refs, b_refs):
        part = jnp.dot(wide(a_ref), tall(b_ref), preferred_element_type=jnp.float32)
        total = part if total is None else total + part
    blk = out_ref.shape[-1]
    j0 = pl.program_id(0) * out_ref.shape[1]
    for i in range(out_ref.shape[0]):
        for j in range(out_ref.shape[1]):
            keep = c_ref[i, j0 + j].astype(jnp.float32)
            out_ref[i, j] = (total[i * blk : (i + 1) * blk, j * blk : (j + 1) * blk] * keep).astype(out_ref.dtype)


def dense_product(a_live, right, c_mask):
    br, kb, blk, _ = a_live.shape
    bc = right[0].shape[1]
    left = [a_live]
    for _ in range(1, STEPS):
        left.append(from_behind(left[-1], "col", -1))
    wide_j = 2 if bc % 2 == 0 else 1
    return pl.pallas_call(
        dense_kernel,
        grid=(bc // wide_j,),
        in_specs=[smem()]
        + [pl.BlockSpec((br, kb, blk, blk), lambda g: (0, 0, 0, 0))] * STEPS
        + [pl.BlockSpec((kb, wide_j, blk, blk), lambda g: (0, g, 0, 0))] * STEPS,
        out_specs=pl.BlockSpec((br, wide_j, blk, blk), lambda g: (0, g, 0, 0)),
        out_shape=jax.ShapeDtypeStruct((br, bc, blk, blk), jnp.bfloat16),
        compiler_params=params(),
        cost_estimate=cost(2 * STEPS * br * bc * kb * blk**3, 10 << 20),
    )(c_mask, *left, *right)


def compact_kernel(mask_ref, a_ref, head0_ref, head1_ref, tail_ref, n_ref, list_ref):
    br, kb = a_ref.shape[:2]
    quarter = br * kb // 4
    count = jnp.int32(0)
    for k in range(kb):
        for i in range(br):
            list_ref[count] = a_ref[i, k]
            count = count + mask_ref[i, k]
    head0_ref[...] = list_ref[0:quarter]
    head1_ref[...] = list_ref[quarter : 2 * quarter]
    tail_ref[...] = list_ref[2 * quarter : 4 * quarter]
    n_ref[0] = jnp.maximum(count, 2 * quarter)


def relay_own_kernel(chunk, sides, n_ref, tail_ref, *refs):
    ins, outs, line = refs[: sides * (chunk - 1)], refs[sides * (chunk - 1) : -1], refs[-1]
    quarter = outs[0].shape[0]
    at = n_ref[0] - 2 * quarter
    for side, out_ref in enumerate(outs):
        line[0 : 2 * quarter] = tail_ref[...]
        for c, ref in enumerate(ins[side * (chunk - 1) : (side + 1) * (chunk - 1)]):
            line[pl.ds(at + c * quarter, quarter)] = ref[...]
        out_ref[...] = line[(chunk - 2) * quarter : (chunk - 1) * quarter]


def relay_kernel(sides, n_ref, *refs):
    ins, outs, line = refs[: 3 * sides], refs[3 * sides : -1], refs[-1]
    quarter = outs[0].shape[0]
    at = 4 * quarter - n_ref[0]
    for side, out_ref in enumerate(outs):
        for c in range(3):
            line[c * quarter : (c + 1) * quarter] = ins[3 * side + c][...]
        out_ref[...] = line[pl.ds(at, quarter)]


def table_kernel(where_ref, mask_ref, end_ref, mid_ref, over_ref):
    blocks = mask_ref.shape[1]
    none = STEPS * blocks
    z = where_ref[0]
    at_end = jnp.logical_or(z == 0, z == 3)
    near = 1 + 2 * (z % 2)

    def clear(ref):
        def body(p, carry):
            ref[p] = none
            return carry

        lax.fori_loop(0, ref.shape[0], body, 0)

    def fill(ref, base, step, there):
        def body(b, count):
            ref[count] = step * blocks + b
            return count + mask_ref[step, b]

        count = lax.fori_loop(0, jnp.where(there, blocks, 0), body, base)
        ref[count] = none
        return jnp.where(there, jnp.maximum(count, base + blocks // 2), base)

    clear(end_ref)
    clear(mid_ref)
    base = fill(end_ref, jnp.int32(0), near, True)
    base = fill(end_ref, base, 2, at_end)
    fill(end_ref, base, 4 - near, at_end)
    base = fill(mid_ref, jnp.int32(0), 4 - near, jnp.logical_not(at_end))
    fill(mid_ref, base, 2, jnp.logical_not(at_end))

    def count_of(slab):
        step = (slab - z + 4) % 4
        total = lax.fori_loop(0, blocks, lambda b, total: total + mask_ref[step, b], jnp.int32(0))
        return jnp.maximum(total, blocks // 2)

    n = [count_of(slab) for slab in range(4)]
    end = n[0] + n[1] + n[2] + n[3] - jnp.minimum(n[0], n[3])
    mid = jnp.maximum(n[0] + n[1], n[2] + n[3])
    quarter = blocks // 4
    over = jnp.logical_or(end > END_CHUNKS * quarter, mid > MID_CHUNKS * quarter)
    over_ref[0] = jnp.where(over, 1, 0).astype(jnp.int32)


def early_kernel(n_end, n_mid, mask_ref, end_ref, mid_ref, a_ref, *refs):
    ends, refs = refs[:n_end], refs[n_end:]
    mids, refs = refs[:n_mid], refs[n_mid:]
    b_refs, acc_ref, left_ref = refs[:STEPS], refs[STEPS], refs[STEPS + 1]
    br, kb, blk, _ = a_ref.shape
    quarter = ends[0].shape[0]

    @pl.when(pl.program_id(0) == 0)
    def _():
        for k in range(kb):
            for i in range(br):
                left_ref[i * blk : (i + 1) * blk, k * blk : (k + 1) * blk] = a_ref[i, k] * mask_ref[i, k].astype(
                    jnp.float32
                ).astype(jnp.bfloat16)
        left_ref[:, kb * blk :] = jnp.zeros((br * blk, left_ref.shape[1] - kb * blk), jnp.bfloat16)
        for table, chunks in ((end_ref, ends), (mid_ref, mids)):
            for c, chunk in enumerate(chunks):
                for b in range(quarter):
                    place = table[c * quarter + b]
                    row = pl.multiple_of((place % br) * blk, blk)
                    column = pl.multiple_of((place // br) * blk, blk)
                    left_ref[pl.ds(row, blk), pl.ds(column, blk)] = chunk[b]

    total = None
    for t in range(STEPS):
        part = jnp.dot(
            left_ref[:, t * kb * blk : (t + 1) * kb * blk], tall(b_refs[t]), preferred_element_type=jnp.float32
        )
        total = part if total is None else total + part
    acc_ref[...] = total


def late_kernel(first, where_ref, c_ref, end_ref, late_ref, acc_ref, b1_ref, b3_ref, out_ref, b_ref, sum_ref, sem):
    i = pl.program_id(0)
    bc, blk = out_ref.shape[1], out_ref.shape[-1]
    kb = b_ref.shape[0]
    br = pl.num_programs(0)
    z = where_ref[0]

    @pl.when(i == 0)
    def _():
        @pl.when(z < 2)
        def _():
            copy = pltpu.make_async_copy(b3_ref, b_ref, sem)
            copy.start()
            copy.wait()

        @pl.when(z >= 2)
        def _():
            copy = pltpu.make_async_copy(b1_ref, b_ref, sem)
            copy.start()
            copy.wait()

    sum_ref[...] = acc_ref[...]
    for b in range(late_ref.shape[0]):
        place = end_ref[first + b]

        @pl.when(jnp.logical_and(place < STEPS * kb * br, place % br == i))
        def _():
            k = (place // br) % kb
            row = jnp.concatenate([b_ref[k, j] for j in range(bc)], axis=1)
            sum_ref[...] += jnp.dot(late_ref[b], row, preferred_element_type=jnp.float32)

    for j in range(bc):
        keep = c_ref[i, j].astype(jnp.float32)
        out_ref[0, j] = (sum_ref[:, j * blk : (j + 1) * blk] * keep).astype(out_ref.dtype)


def sparse_product(a_blocks, a_mask, right, c_mask):
    br, kb, blk, _ = a_blocks.shape
    bc = right[0].shape[1]
    blocks = br * kb
    quarter = blocks // 4
    z = lax.axis_index("col").astype(jnp.int32).reshape(1)
    chunk_shape = jax.ShapeDtypeStruct((quarter, blk, blk), a_blocks.dtype)
    chunk_bytes = quarter * blk * blk * 2

    def end_swap(x):
        return lax.ppermute(x, "col", [(0, 1), (1, 0), (2, 3), (3, 2)])

    def mid_swap(x):
        return lax.ppermute(x, "col", [(1, 2), (2, 1)])

    head0, head1, tail, n = pl.pallas_call(
        compact_kernel,
        in_specs=[smem(), whole()],
        out_specs=[whole(), whole(), whole(), smem()],
        out_shape=[
            chunk_shape,
            chunk_shape,
            jax.ShapeDtypeStruct((2 * quarter, blk, blk), a_blocks.dtype),
            jax.ShapeDtypeStruct((1,), jnp.int32),
        ],
        scratch_shapes=[pltpu.VMEM((blocks, blk, blk), a_blocks.dtype)],
        compiler_params=params(),
        cost_estimate=cost(0, 8 * chunk_bytes),
        name="compact",
    )(a_mask, a_blocks)

    ends = [end_swap(head0)]
    mids = [mid_swap(head0)]
    ends.append(end_swap(head1))
    mids.append(mid_swap(head1))

    masks = [a_mask] + [from_behind(a_mask, "col", -t) for t in range(1, STEPS)]
    by_column = jnp.stack([m.T.reshape(blocks) for m in masks])
    end_table, mid_table, over = pl.pallas_call(
        table_kernel,
        in_specs=[smem(), smem()],
        out_specs=[smem(), smem(), smem()],
        out_shape=[
            jax.ShapeDtypeStruct((3 * blocks + 8,), jnp.int32),
            jax.ShapeDtypeStruct((2 * blocks + 8,), jnp.int32),
            jax.ShapeDtypeStruct((1,), jnp.int32),
        ],
        compiler_params=params(),
        name="table",
    )(z, by_column)
    rows = lax.axis_size("row")
    bit = 1
    while bit < rows:
        over = jnp.maximum(over, lax.ppermute(over, "row", [(i, i ^ bit) for i in range(rows)]))
        bit *= 2

    for chunk in range(2, END_CHUNKS):
        to_mid = chunk < MID_CHUNKS
        sides = 2 if to_mid else 1
        if chunk < 4:
            kernel = functools.partial(relay_own_kernel, chunk, sides)
            ins = [tail] + mids[: chunk - 1] + (ends[: chunk - 1] if to_mid else [])
            length = 2 + chunk - 1
        else:
            kernel = functools.partial(relay_kernel, sides)
            ins = mids[chunk - 4 : chunk - 1] + (ends[chunk - 4 : chunk - 1] if to_mid else [])
            length = 3
        outs = pl.pallas_call(
            kernel,
            in_specs=[smem()] + [whole()] * len(ins),
            out_specs=[whole()] * sides,
            out_shape=[chunk_shape] * sides,
            scratch_shapes=[pltpu.VMEM((length * quarter, blk, blk), a_blocks.dtype)],
            compiler_params=params(),
            cost_estimate=cost(0, (len(ins) + sides) * chunk_bytes),
            name=f"relay{chunk}",
        )(n, *ins)
        ends.append(end_swap(outs[0]))
        if to_mid:
            mids.append(mid_swap(outs[1]))

    wide_j = 2 if bc % 2 == 0 else 1
    chunk_spec = pl.BlockSpec(chunk_shape.shape, lambda g: (0, 0, 0))
    acc = pl.pallas_call(
        functools.partial(early_kernel, END_CHUNKS - 1, MID_CHUNKS),
        grid=(bc // wide_j,),
        in_specs=[smem(), smem(), smem(), pl.BlockSpec(a_blocks.shape, lambda g: (0, 0, 0, 0))]
        + [chunk_spec] * (END_CHUNKS - 1 + MID_CHUNKS)
        + [pl.BlockSpec((kb, wide_j, blk, blk), lambda g: (0, g, 0, 0))] * STEPS,
        out_specs=pl.BlockSpec((br * blk, wide_j * blk), lambda g: (0, g)),
        out_shape=jax.ShapeDtypeStruct((br * blk, bc * blk), jnp.float32),
        scratch_shapes=[pltpu.VMEM((br * blk, (STEPS * kb + 1) * blk), a_blocks.dtype)],
        compiler_params=params(),
        cost_estimate=cost(2 * STEPS * br * bc * kb * blk**3, 14 << 20),
        name="early",
    )(a_mask, end_table, mid_table, a_blocks, *ends[:-1], *mids, *right)

    def rest(late, acc, right):
        return pl.pallas_call(
            functools.partial(late_kernel, (END_CHUNKS - 1) * quarter),
            grid=(br,),
            in_specs=[
                smem(),
                smem(),
                smem(),
                pl.BlockSpec(late.shape, lambda g: (0, 0, 0)),
                pl.BlockSpec((blk, bc * blk), lambda g: (g, 0)),
                pl.BlockSpec(memory_space=pl.ANY),
                pl.BlockSpec(memory_space=pl.ANY),
            ],
            out_specs=pl.BlockSpec((1, bc, blk, blk), lambda g: (g, 0, 0, 0)),
            out_shape=jax.ShapeDtypeStruct((br, bc, blk, blk), jnp.bfloat16),
            scratch_shapes=[
                pltpu.VMEM((kb, bc, blk, blk), jnp.bfloat16),
                pltpu.VMEM((blk, bc * blk), jnp.float32),
                pltpu.SemaphoreType.DMA,
            ],
            compiler_params=params(),
            cost_estimate=cost(0, 8 << 20),
            name="late",
        )(z, c_mask, end_table, late, acc, right[1], right[3])

    def everything(late, acc, right):
        a_live = a_blocks * a_mask[:, :, None, None].astype(a_blocks.dtype)
        return dense_product(a_live, right, c_mask)

    return lax.cond(over[0] > 0, everything, rest, ends[-1], acc, right)


def on_device(a_blocks, a_mask, b_blocks, b_mask, c_mask):
    b_live = b_blocks * b_mask[:, :, None, None].astype(jnp.bfloat16)
    right = [b_live]
    for _ in range(1, STEPS):
        right.append(from_behind(right[-1], "row", -1))
    blocks = a_blocks.shape[0] * a_blocks.shape[1]
    rows = lax.axis_size("row")
    if lax.axis_size("col") == STEPS and blocks % 4 == 0 and rows & (rows - 1) == 0:
        return sparse_product(a_blocks, a_mask, right, c_mask)
    a_live = a_blocks * a_mask[:, :, None, None].astype(jnp.bfloat16)
    return dense_product(a_live, right, c_mask)


def solution(mesh):
    return jax.shard_map(
        on_device,
        mesh=mesh,
        in_specs=(
            P("row", "col", None, None),
            P("row", "col"),
            P("row", "col", None, None),
            P("row", "col"),
            P("row", "col"),
        ),
        out_specs=P("row", "col", None, None),
        check_vma=False,
    )
```

time: 93.1 us -> 123 us (1.32)
  the two profiles are of different devices: /device:TPU:26 before, /device:TPU:0 now
where the time goes in v2:
time: 123 us
  starting transfers between devices  49 us (40%)
  waiting for transfers between devices  42.8 us (35%)
  Pallas kernels  23.7 us (19%)
  other arithmetic  3.04 us (2%)
  between operations  2.63 us (2%)
  local copies, waits for them, and re-layouts  1.73 us (1%)
    ppermute x9, starting transfers between devices, end_swap(): return lax.ppermute(x, 'col', [(0, 1), (1, 0), (2, 3), (3, 2)])  24 us
    ppermute x6, waiting for transfers between devices, from_behind(): lax.ppermute(array, axis, [(i, (i + by) % size) for i in range(size)])  22.9 us
    ppermute x9, waiting for transfers between devices, end_swap(): return lax.ppermute(x, 'col', [(0, 1), (1, 0), (2, 3), (3, 2)])  16.8 us
    ppermute x6, starting transfers between devices, from_behind(): lax.ppermute(array, axis, [(i, (i + by) % size) for i in range(size)])  16.4 us
    pallas_call x1, Pallas kernels, sparse_product(): pl.pallas_call(functools.partial(early_kernel, END_CHUNKS - 1, MID_CHUNKS...  8.41 us
    pallas_call x7, Pallas kernels, sparse_product(): pl.pallas_call(kernel, in_specs=[smem()] + [whole()] * len(ins), out_spec...  6.24 us
    ppermute x7, starting transfers between devices, mid_swap(): return lax.ppermute(x, 'col', [(1, 2), (2, 1)])  4.69 us
    pallas_call x1, Pallas kernels, sparse_product(): pl.pallas_call(table_kernel, in_specs=[smem(), smem()], out_specs=[smem()...  3.89 us
  transfers between devices with their start and end apart: 25, of which 11 were waited for; matrix products, arithmetic and copies ran while one was open for 0% of the time, Pallas kernels for 17%

profile of v2, /device:TPU:0, one launch (start us, length us, event | category | flops | bytes accessed | tf_op | source)
XLA Modules:
  0.0 122.9 jit_solution(1744726136574968728)
XLA Ops:
  0.0 0.7 convert_element_type.16
  0.7 2.3 %broadcast_multiply_fusion.1.refs_15_ = bf16[4,8,128,128]{3,2,1,0:T(8,128)(2,1)} fusion(bf16[4,8,128,128]{3,2,1,0:T(8,128)(2,1)} %param.9, bf16[4,8]{1,0:T(4,128)(2,1)S(1)} %convert_element_type.16), kind=kLoop, calls=%fused_computation.1 | loop fusion | flops 524288 | bytes 2097216 | tf_op jit(solution)/shard_map/mul | solution.py:360
  3.0 3.3 %collective-permute-start.25 = (bf16[4,8,128,128]{3,2,1,0:T(8,128)(2,1)}, bf16[4,8,128,128]{3,2,1,0:T(8,128)(2,1)}, u32[]{:S(2)}, u32[]{:S(2)}) collective-permute-start(bf16[4,8,128,128]{3,2,1,0:T(8,128)(2,1)} %broadcast_multiply_fusion.1.refs_15_), channel_id=1, source_target_pairs={{0,28},{4,0},{8,4},{12,8},{16,12},{20,16},{24,20},{28,24},{1,29},{... | collective-permute-start | bytes 3145736 | tf_op jit(solution)/shard_map/ppermute | solution.py:18
  6.4 12.6 %collective-permute-done.25.refs_16_ = bf16[4,8,128,128]{3,2,1,0:T(8,128)(2,1)} collective-permute-done((bf16[4,8,128,128]{3,2,1,0:T(8,128)(2,1)}, bf16[4,8,128,128]{3,2,1,0:T(8,128)(2,1)}, u32[]{:S(2)}, u32[]{:S(2)}) %collective-permute-start.25) | collective-permute-done | bytes 1048608 | tf_op jit(solution)/shard_map/ppermute | solution.py:18
  19.0 2.8 %collective-permute-start.26 = (bf16[4,8,128,128]{3,2,1,0:T(8,128)(2,1)}, bf16[4,8,128,128]{3,2,1,0:T(8,128)(2,1)}, u32[]{:S(2)}, u32[]{:S(2)}) collective-permute-start(bf16[4,8,128,128]{3,2,1,0:T(8,128)(2,1)} %collective-permute-done.25.refs_16_), channel_id=1, source_target_pairs={{0,28},{4,0},{8,4},{12,8},{16,12},{20,16},{24,20},{28,24},{1,29},{... | collective-permute-start | bytes 3145736 | tf_op jit(solution)/shard_map/ppermute | solution.py:18
  21.9 1.8 %compact.1 = (bf16[8,128,128]{2,1,0:T(8,128)(2,1)S(1)}, bf16[8,128,128]{2,1,0:T(8,128)(2,1)S(1)}, bf16[16,128,128]{2,1,0:T(8,128)(2,1)S(1)}, s32[1]{0:T(128)}) custom-call(s32[8,4]{1,0:T(8,128)S(1)} %copy.8.mask_ref, bf16[8,4,128,128]{3,2,1,0:T(8,128)(2,1)} %a_ref.3), custom_call_target="tpu_custom_call" | custom-call | bytes 2097152 | tf_op jit(solution)/shard_map/compact/pallas_call | solution.py:245
  23.7 1.6 %collective-permute-start.11 = (bf16[8,128,128]{2,1,0:T(8,128)(2,1)S(1)}, bf16[8,128,128]{2,1,0:T(8,128)(2,1)S(1)}, u32[]{:S(2)}, u32[]{:S(2)}) collective-permute-start(bf16[8,128,128]{2,1,0:T(8,128)(2,1)S(1)} %get-tuple-element.70), channel_id=1, source_target_pairs={{0,1},{1,0},{2,3},{3,2},{4,5},{5,4},{6,7},{7,6},{8,9},{9,8},{10,11... | collective-permute-start | bytes 786440 | tf_op jit(solution)/shard_map/ppermute | solution.py:240
  25.3 0.7 collective-permute-start.9
  26.0 4.4 %collective-permute-start.13 = (bf16[8,128,128]{2,1,0:T(8,128)(2,1)S(1)}, bf16[8,128,128]{2,1,0:T(8,128)(2,1)S(1)}, u32[]{:S(2)}, u32[]{:S(2)}) collective-permute-start(bf16[8,128,128]{2,1,0:T(8,128)(2,1)S(1)} %get-tuple-element.71), channel_id=1, source_target_pairs={{0,1},{1,0},{2,3},{3,2},{4,5},{5,4},{6,7},{7,6},{8,9},{9,8},{10,11... | collective-permute-start | bytes 786440 | tf_op jit(solution)/shard_map/ppermute | solution.py:240
  30.5 0.7 collective-permute-start.10
  31.1 3.3 %collective-permute-done.26.refs_17_ = bf16[4,8,128,128]{3,2,1,0:T(8,128)(2,1)} collective-permute-done((bf16[4,8,128,128]{3,2,1,0:T(8,128)(2,1)}, bf16[4,8,128,128]{3,2,1,0:T(8,128)(2,1)}, u32[]{:S(2)}, u32[]{:S(2)}) %collective-permute-start.26) | collective-permute-done | bytes 1048608 | tf_op jit(solution)/shard_map/ppermute | solution.py:18
  34.4 2.8 %collective-permute-start.27 = (bf16[4,8,128,128]{3,2,1,0:T(8,128)(2,1)}, bf16[4,8,128,128]{3,2,1,0:T(8,128)(2,1)}, u32[]{:S(2)}, u32[]{:S(2)}) collective-permute-start(bf16[4,8,128,128]{3,2,1,0:T(8,128)(2,1)} %collective-permute-done.26.refs_17_), channel_id=1, source_target_pairs={{0,28},{4,0},{8,4},{12,8},{16,12},{20,16},{24,20},{28,24},{1,29},{... | collective-permute-start | bytes 3145736 | tf_op jit(solution)/shard_map/ppermute | solution.py:18
  37.3 0.7 relay2.1
  38.0 0.7 collective-permute-start.12
  38.6 4.4 %collective-permute-start.14 = (bf16[8,128,128]{2,1,0:T(8,128)(2,1)S(1)}, bf16[8,128,128]{2,1,0:T(8,128)(2,1)S(1)}, u32[]{:S(2)}, u32[]{:S(2)}) collective-permute-start(bf16[8,128,128]{2,1,0:T(8,128)(2,1)S(1)} %get-tuple-element.74), channel_id=1, source_target_pairs={{0,1},{1,0},{2,3},{3,2},{4,5},{5,4},{6,7},{7,6},{8,9},{9,8},{10,11... | collective-permute-start | bytes 786440 | tf_op jit(solution)/shard_map/ppermute | solution.py:240
  43.1 0.7 relay3.1
  43.8 0.7 collective-permute-start.16
  44.5 1.8 %collective-permute-start.17 = (bf16[8,128,128]{2,1,0:T(8,128)(2,1)S(1)}, bf16[8,128,128]{2,1,0:T(8,128)(2,1)S(1)}, u32[]{:S(2)}, u32[]{:S(2)}) collective-permute-start(bf16[8,128,128]{2,1,0:T(8,128)(2,1)S(1)} %get-tuple-element.77), channel_id=1, source_target_pairs={{0,1},{1,0},{2,3},{3,2},{4,5},{5,4},{6,7},{7,6},{8,9},{9,8},{10,11... | collective-permute-start | bytes 786440 | tf_op jit(solution)/shard_map/ppermute | solution.py:240
  46.3 3.6 %collective-permute-done.14.refs_5_.refs_4_.refs_3_.refs_2_ = bf16[8,128,128]{2,1,0:T(8,128)(2,1)S(1)} collective-permute-done((bf16[8,128,128]{2,1,0:T(8,128)(2,1)S(1)}, bf16[8,128,128]{2,1,0:T(8,128)(2,1)S(1)}, u32[]{:S(2)}, u32[]{:S(2)}) %collective-permute-start.14) | collective-permute-done | bytes 262176 | tf_op jit(solution)/shard_map/ppermute | solution.py:240
  49.9 1.4 %relay4.1 = (bf16[8,128,128]{2,1,0:T(8,128)(2,1)S(1)}, bf16[8,128,128]{2,1,0:T(8,128)(2,1)}) custom-call(s32[1]{0:T(128)} %get-tuple-element.69.n_ref, bf16[8,128,128]{2,1,0:T(8,128)(2,1)S(1)} %collective-permute-done.9.refs_0_.refs_8_, bf16[8,128,128]{2,1,0:T(8,128)(2,1)S(1)} %collective-permute-done.10.refs_1_.refs_0_.refs_9_, ...), custom_call_target="tpu_custom_call" | custom-call | bytes 2097152 | tf_op jit(solution)/shard_map/relay4/pallas_call | solution.py:297
  51.3 0.7 collective-permute-start.15
  52.0 3.6 %collective-permute-start.19 = (bf16[8,128,128]{2,1,0:T(8,128)(2,1)S(1)}, bf16[8,128,128]{2,1,0:T(8,128)(2,1)S(1)}, u32[]{:S(2)}, u32[]{:S(2)}) collective-permute-start(bf16[8,128,128]{2,1,0:T(8,128)(2,1)S(1)} %get-tuple-element.79), channel_id=1, source_target_pairs={{0,1},{1,0},{2,3},{3,2},{4,5},{5,4},{6,7},{7,6},{8,9},{9,8},{10,11... | collective-permute-start | bytes 786440 | tf_op jit(solution)/shard_map/ppermute | solution.py:240
  55.7 1.4 %relay5.1 = (bf16[8,128,128]{2,1,0:T(8,128)(2,1)S(1)}, bf16[8,128,128]{2,1,0:T(8,128)(2,1)}) custom-call(s32[1]{0:T(128)} %get-tuple-element.69.n_ref, bf16[8,128,128]{2,1,0:T(8,128)(2,1)S(1)} %collective-permute-done.10.refs_1_.refs_0_.refs_9_, bf16[8,128,128]{2,1,0:T(8,128)(2,1)S(1)} %collective-permute-done.12.refs_2_.refs_1_.refs_0_.refs_10_, ...), custom_call_target="tpu_custom_call" | custom-call | bytes 2097152 | tf_op jit(solution)/shard_map/relay5/pallas_call | solution.py:297
  57.1 0.7 collective-permute-start.18
  57.8 2.8 %collective-permute-start.5 = (s32[8,4]{0,1:T(4,128)S(1)}, s32[8,4]{0,1:T(4,128)S(1)}, u32[]{:S(2)}, u32[]{:S(2)}) collective-permute-start(s32[8,4]{0,1:T(4,128)S(1)} %copy-done.1), channel_id=1, source_target_pairs={{0,1},{1,2},{2,3},{3,0},{4,5},{5,6},{6,7},{7,4},{8,9},{9,10},{10,1... | collective-permute-start | bytes 392 | tf_op jit(solution)/shard_map/ppermute | solution.py:18
  60.7 2.5 %collective-permute-done.5 = s32[8,4]{0,1:T(4,128)S(1)} collective-permute-done((s32[8,4]{0,1:T(4,128)S(1)}, s32[8,4]{0,1:T(4,128)S(1)}, u32[]{:S(2)}, u32[]{:S(2)}) %collective-permute-start.5) | collective-permute-done | bytes 160 | tf_op jit(solution)/shard_map/ppermute | solution.py:18
  63.2 4.1 %collective-permute-start.4 = (s32[8,4]{0,1:T(4,128)S(1)}, s32[8,4]{0,1:T(4,128)S(1)}, u32[]{:S(2)}, u32[]{:S(2)}) collective-permute-start(s32[8,4]{0,1:T(4,128)S(1)} %copy-done.1), channel_id=1, source_target_pairs={{0,2},{1,3},{2,0},{3,1},{4,6},{5,7},{6,4},{7,5},{8,10},{9,11},{10,... | collective-permute-start | bytes 392 | tf_op jit(solution)/shard_map/ppermute | solution.py:18
  67.4 1.5 %collective-permute-done.4 = s32[8,4]{0,1:T(4,128)S(1)} collective-permute-done((s32[8,4]{0,1:T(4,128)S(1)}, s32[8,4]{0,1:T(4,128)S(1)}, u32[]{:S(2)}, u32[]{:S(2)}) %collective-permute-start.4) | collective-permute-done | bytes 160 | tf_op jit(solution)/shard_map/ppermute | solution.py:18
  69.5 3.0 %collective-permute-done.3 = s32[8,4]{0,1:T(4,128)S(1)} collective-permute-done((s32[8,4]{0,1:T(4,128)S(1)}, s32[8,4]{0,1:T(4,128)S(1)}, u32[]{:S(2)}, u32[]{:S(2)}) %collective-permute-start.3) | collective-permute-done | bytes 160 | tf_op jit(solution)/shard_map/ppermute | solution.py:18
  72.5 3.9 %table.1 = (s32[104]{0:T(128)S(1)}, s32[72]{0:T(128)S(1)}, s32[1]{0:T(128)}) custom-call(s32[1]{0:T(128)} %bitcast.where_ref, s32[4,32]{1,0:T(4,128)S(1)} %pad_add_fusion.mask_ref), custom_call_target="tpu_custom_call" | custom-call | tf_op jit(solution)/shard_map/table/pallas_call | solution.py:268
  76.5 1.3 %collective-permute-done.6 = s32[1]{0:T(128)} collective-permute-done((s32[1]{0:T(128)}, s32[1]{0:T(128)}, u32[]{:S(2)}, u32[]{:S(2)}) %collective-permute-start.6) | collective-permute-done | bytes 36 | tf_op jit(solution)/shard_map/ppermute | solution.py:283
  79.1 1.9 %collective-permute-start.7 = (s32[1]{0:T(128)}, s32[1]{0:T(128)}, u32[]{:S(2)}, u32[]{:S(2)}) collective-permute-start(s32[1]{0:T(128)} %max.9), channel_id=1, source_target_pairs={{0,8},{4,12},{8,0},{12,4},{16,24},{20,28},{24,16},{28,20},{1,9},{5... | collective-permute-start | bytes 20 | tf_op jit(solution)/shard_map/ppermute | solution.py:283
  81.0 1.8 %collective-permute-done.7 = s32[1]{0:T(128)} collective-permute-done((s32[1]{0:T(128)}, s32[1]{0:T(128)}, u32[]{:S(2)}, u32[]{:S(2)}) %collective-permute-start.7) | collective-permute-done | bytes 36 | tf_op jit(solution)/shard_map/ppermute | solution.py:283
  83.4 1.9 %collective-permute-start.8 = (s32[1]{0:T(128)}, s32[1]{0:T(128)}, u32[]{:S(2)}, u32[]{:S(2)}) collective-permute-start(s32[1]{0:T(128)} %max.10), channel_id=1, source_target_pairs={{0,16},{4,20},{8,24},{12,28},{16,0},{20,4},{24,8},{28,12},{1,17},{... | collective-permute-start | bytes 20 | tf_op jit(solution)/shard_map/ppermute | solution.py:283
  85.2 0.7 relay6.1
  86.0 0.7 collective-permute-start.20
  86.7 4.8 %collective-permute-start.22 = (bf16[8,128,128]{2,1,0:T(8,128)(2,1)S(1)}, bf16[8,128,128]{2,1,0:T(8,128)(2,1)S(1)}, u32[]{:S(2)}, u32[]{:S(2)}) collective-permute-start(bf16[8,128,128]{2,1,0:T(8,128)(2,1)S(1)} %get-tuple-element.82), channel_id=1, source_target_pairs={{0,1},{1,0},{2,3},{3,2},{4,5},{5,4},{6,7},{7,6},{8,9},{9,8},{10,11... | collective-permute-start | bytes 786440 | tf_op jit(solution)/shard_map/ppermute | solution.py:240
  91.5 0.6 relay7.1
  92.2 2.0 %collective-permute-start.23 = (bf16[8,128,128]{2,1,0:T(8,128)(2,1)S(1)}, bf16[8,128,128]{2,1,0:T(8,128)(2,1)S(1)}, u32[]{:S(2)}, u32[]{:S(2)}) collective-permute-start(bf16[8,128,128]{2,1,0:T(8,128)(2,1)S(1)} %get-tuple-element.83), channel_id=1, source_target_pairs={{0,1},{1,0},{2,3},{3,2},{4,5},{5,4},{6,7},{7,6},{8,9},{9,8},{10,11... | collective-permute-start | bytes 786440 | tf_op jit(solution)/shard_map/ppermute | solution.py:240
  94.8 0.6 relay8.1
  95.4 1.2 collective-permute-start.21
  96.6 2.1 %collective-permute-done.22.refs_5_ = bf16[8,128,128]{2,1,0:T(8,128)(2,1)S(1)} collective-permute-done((bf16[8,128,128]{2,1,0:T(8,128)(2,1)S(1)}, bf16[8,128,128]{2,1,0:T(8,128)(2,1)S(1)}, u32[]{:S(2)}, u32[]{:S(2)}) %collective-permute-start.22) | collective-permute-done | bytes 262176 | tf_op jit(solution)/shard_map/ppermute | solution.py:240
  98.7 5.6 %collective-permute-done.24.refs_7_ = bf16[8,128,128]{2,1,0:T(8,128)(2,1)S(1)} collective-permute-done((bf16[8,128,128]{2,1,0:T(8,128)(2,1)S(1)}, bf16[8,128,128]{2,1,0:T(8,128)(2,1)S(1)}, u32[]{:S(2)}, u32[]{:S(2)}) %collective-permute-start.24) | collective-permute-done | bytes 262176 | tf_op jit(solution)/shard_map/ppermute | solution.py:240
  104.3 5.5 %collective-permute-done.23.refs_6_ = bf16[8,128,128]{2,1,0:T(8,128)(2,1)S(1)} collective-permute-done((bf16[8,128,128]{2,1,0:T(8,128)(2,1)S(1)}, bf16[8,128,128]{2,1,0:T(8,128)(2,1)S(1)}, u32[]{:S(2)}, u32[]{:S(2)}) %collective-permute-start.23) | collective-permute-done | bytes 262176 | tf_op jit(solution)/shard_map/ppermute | solution.py:240
  109.8 8.4 %early.1 = f32[1024,1024]{1,0:T(8,128)S(1)} custom-call(s32[8,4]{1,0:T(8,128)S(1)} %copy.8.mask_ref, s32[104]{0:T(128)S(1)} %get-tuple-element.68.end_ref, s32[72]{0:T(128)S(1)} %get-tuple-element.81.mid_ref, bf16[8,4,128,128]{3,2,1,0:T(8,128)(2,1)} %a_ref.3, bf16[8,128,128]{2,1,0:T(8,128)(2,1)S(1)} %collective-permute-done.11.refs_1_.refs_3_.refs_2_.refs_0_, ...), custom_call_target="tpu_custom_call" | custom-call | flops 4294967296 | bytes 14680064 | tf_op jit(solution)/shard_map/early/pallas_call | solution.py:313
  118.2 3.4 %conditional.1 = (bf16[8,8,128,128]{3,2,1,0:T(8,128)(2,1)S(1)}) conditional(s32[]{:T(128)} %bitcast.5, (s32[1]{0:T(128)}, s32[8,8]{1,0:T(8,128)S(1)}, s32[104]{0:T(128)S(1)}, bf16[8,128,128]{2,1,0:T(8,128)(2,1)S(1)}, f32[1024,1024]{1,0:T(8,128)S(1)}, /*index=5*/bf16[4,8,128,128]{3,2,1,0:T(8,128)(2,1)}, bf16[4,8,128,128]{3,2,1,0:T(8,128)(2,1)}) %tuple.20, ...), branch_computations={%region_0.0_spmd, %region_1.0_spmd} | conditional | flops 4295491584 | bytes 25166464 | solution.py:356
  118.2 3.4 %late.1 = bf16[8,8,128,128]{3,2,1,0:T(8,128)(2,1)S(1)} custom-call(s32[1]{0:T(128)} %get-tuple-element.36.where_ref, s32[8,8]{1,0:T(8,128)S(1)} %get-tuple-element.37.c_ref, s32[104]{0:T(128)S(1)} %get-tuple-element.38.end_ref, bf16[8,128,128]{2,1,0:T(8,128)(2,1)S(1)} %get-tuple-element.39.late_ref, f32[1024,1024]{1,0:T(8,128)S(1)} %get-tuple-element.40.acc_ref, ...), custom_call_target="tpu_custom_call" | custom-call | bytes 8388608 | tf_op jit(solution)/shard_map/cond/branch_0_fun/late/pallas_call | solution.py:328
  121.6 1.3 %copy-done = bf16[8,8,128,128]{3,2,1,0:T(8,128)(2,1)} copy-done((bf16[8,8,128,128]{3,2,1,0:T(8,128)(2,1)}, bf16[8,8,128,128]{3,2,1,0:T(8,128)(2,1)S(1)}, u32[]{:S(2)}) %copy-start) | copy-done | bytes 2097176
  (28 shorter events, 1.2 us)
Async XLA Ops:
  0.0 21.8 %copy-start.1 = (s32[8,4]{0,1:T(4,128)S(1)}, s32[8,4]{0,1:T(4,128)}, u32[]{:S(2)}) copy-start(s32[8,4]{0,1:T(4,128)} %param.8) | copy-start | bytes 388
  3.0 16.0 %collective-permute-start.25 = (bf16[4,8,128,128]{3,2,1,0:T(8,128)(2,1)}, bf16[4,8,128,128]{3,2,1,0:T(8,128)(2,1)}, u32[]{:S(2)}, u32[]{:S(2)}) collective-permute-start(bf16[4,8,128,128]{3,2,1,0:T(8,128)(2,1)} %broadcast_multiply_fusion.1.refs_15_), channel_id=1, source_target_pairs={{0,28},{4,0},{8,4},{12,8},{16,12},{20,16},{24,20},{28,24},{1,29},{... | collective-permute-start | bytes 3145736 | tf_op jit(solution)/shard_map/ppermute | solution.py:18
  19.0 15.4 %collective-permute-start.26 = (bf16[4,8,128,128]{3,2,1,0:T(8,128)(2,1)}, bf16[4,8,128,128]{3,2,1,0:T(8,128)(2,1)}, u32[]{:S(2)}, u32[]{:S(2)}) collective-permute-start(bf16[4,8,128,128]{3,2,1,0:T(8,128)(2,1)} %collective-permute-done.25.refs_16_), channel_id=1, source_target_pairs={{0,28},{4,0},{8,4},{12,8},{16,12},{20,16},{24,20},{28,24},{1,29},{... | collective-permute-start | bytes 3145736 | tf_op jit(solution)/shard_map/ppermute | solution.py:18
  23.7 13.6 %collective-permute-start.11 = (bf16[8,128,128]{2,1,0:T(8,128)(2,1)S(1)}, bf16[8,128,128]{2,1,0:T(8,128)(2,1)S(1)}, u32[]{:S(2)}, u32[]{:S(2)}) collective-permute-start(bf16[8,128,128]{2,1,0:T(8,128)(2,1)S(1)} %get-tuple-element.70), channel_id=1, source_target_pairs={{0,1},{1,0},{2,3},{3,2},{4,5},{5,4},{6,7},{7,6},{8,9},{9,8},{10,11... | collective-permute-start | bytes 786440 | tf_op jit(solution)/shard_map/ppermute | solution.py:240
  25.3 11.9 %collective-permute-start.9 = (bf16[8,128,128]{2,1,0:T(8,128)(2,1)S(1)}, bf16[8,128,128]{2,1,0:T(8,128)(2,1)S(1)}, u32[]{:S(2)}, u32[]{:S(2)}) collective-permute-start(bf16[8,128,128]{2,1,0:T(8,128)(2,1)S(1)} %get-tuple-element.70), channel_id=1, source_target_pairs={{1,2},{2,1},{5,6},{6,5},{9,10},{10,9},{13,14},{14,13},{17,18},{18,... | collective-permute-start | bytes 786440 | tf_op jit(solution)/shard_map/ppermute | solution.py:243
  26.0 17.1 %collective-permute-start.13 = (bf16[8,128,128]{2,1,0:T(8,128)(2,1)S(1)}, bf16[8,128,128]{2,1,0:T(8,128)(2,1)S(1)}, u32[]{:S(2)}, u32[]{:S(2)}) collective-permute-start(bf16[8,128,128]{2,1,0:T(8,128)(2,1)S(1)} %get-tuple-element.71), channel_id=1, source_target_pairs={{0,1},{1,0},{2,3},{3,2},{4,5},{5,4},{6,7},{7,6},{8,9},{9,8},{10,11... | collective-permute-start | bytes 786440 | tf_op jit(solution)/shard_map/ppermute | solution.py:240
  30.5 12.6 %collective-permute-start.10 = (bf16[8,128,128]{2,1,0:T(8,128)(2,1)S(1)}, bf16[8,128,128]{2,1,0:T(8,128)(2,1)S(1)}, u32[]{:S(2)}, u32[]{:S(2)}) collective-permute-start(bf16[8,128,128]{2,1,0:T(8,128)(2,1)S(1)} %get-tuple-element.71), channel_id=1, source_target_pairs={{1,2},{2,1},{5,6},{6,5},{9,10},{10,9},{13,14},{14,13},{17,18},{18,... | collective-permute-start | bytes 786440 | tf_op jit(solution)/shard_map/ppermute | solution.py:243
  34.4 62.2 %collective-permute-start.27 = (bf16[4,8,128,128]{3,2,1,0:T(8,128)(2,1)}, bf16[4,8,128,128]{3,2,1,0:T(8,128)(2,1)}, u32[]{:S(2)}, u32[]{:S(2)}) collective-permute-start(bf16[4,8,128,128]{3,2,1,0:T(8,128)(2,1)} %collective-permute-done.26.refs_17_), channel_id=1, source_target_pairs={{0,28},{4,0},{8,4},{12,8},{16,12},{20,16},{24,20},{28,24},{1,29},{... | collective-permute-start | bytes 3145736 | tf_op jit(solution)/shard_map/ppermute | solution.py:18
  38.0 8.3 %collective-permute-start.12 = (bf16[8,128,128]{2,1,0:T(8,128)(2,1)S(1)}, bf16[8,128,128]{2,1,0:T(8,128)(2,1)S(1)}, u32[]{:S(2)}, u32[]{:S(2)}) collective-permute-start(bf16[8,128,128]{2,1,0:T(8,128)(2,1)S(1)} %get-tuple-element.73), channel_id=1, source_target_pairs={{1,2},{2,1},{5,6},{6,5},{9,10},{10,9},{13,14},{14,13},{17,18},{18,... | collective-permute-start | bytes 786440 | tf_op jit(solution)/shard_map/ppermute | solution.py:243
  38.6 11.3 %collective-permute-start.14 = (bf16[8,128,128]{2,1,0:T(8,128)(2,1)S(1)}, bf16[8,128,128]{2,1,0:T(8,128)(2,1)S(1)}, u32[]{:S(2)}, u32[]{:S(2)}) collective-permute-start(bf16[8,128,128]{2,1,0:T(8,128)(2,1)S(1)} %get-tuple-element.74), channel_id=1, source_target_pairs={{0,1},{1,0},{2,3},{3,2},{4,5},{5,4},{6,7},{7,6},{8,9},{9,8},{10,11... | collective-permute-start | bytes 786440 | tf_op jit(solution)/shard_map/ppermute | solution.py:240
  43.8 11.8 %collective-permute-start.16 = (bf16[8,128,128]{2,1,0:T(8,128)(2,1)S(1)}, bf16[8,128,128]{2,1,0:T(8,128)(2,1)S(1)}, u32[]{:S(2)}, u32[]{:S(2)}) collective-permute-start(bf16[8,128,128]{2,1,0:T(8,128)(2,1)S(1)} %get-tuple-element.76), channel_id=1, source_target_pairs={{1,2},{2,1},{5,6},{6,5},{9,10},{10,9},{13,14},{14,13},{17,18},{18,... | collective-permute-start | bytes 786440 | tf_op jit(solution)/shard_map/ppermute | solution.py:243
  44.5 11.2 %collective-permute-start.17 = (bf16[8,128,128]{2,1,0:T(8,128)(2,1)S(1)}, bf16[8,128,128]{2,1,0:T(8,128)(2,1)S(1)}, u32[]{:S(2)}, u32[]{:S(2)}) collective-permute-start(bf16[8,128,128]{2,1,0:T(8,128)(2,1)S(1)} %get-tuple-element.77), channel_id=1, source_target_pairs={{0,1},{1,0},{2,3},{3,2},{4,5},{5,4},{6,7},{7,6},{8,9},{9,8},{10,11... | collective-permute-start | bytes 786440 | tf_op jit(solution)/shard_map/ppermute | solution.py:240
  51.3 33.9 %collective-permute-start.15 = (bf16[8,128,128]{2,1,0:T(8,128)(2,1)}, bf16[8,128,128]{2,1,0:T(8,128)(2,1)S(1)}, u32[]{:S(2)}, u32[]{:S(2)}) collective-permute-start(bf16[8,128,128]{2,1,0:T(8,128)(2,1)} %get-tuple-element.75), channel_id=1, source_target_pairs={{1,2},{2,1},{5,6},{6,5},{9,10},{10,9},{13,14},{14,13},{17,18},{18,... | collective-permute-start | bytes 786440 | tf_op jit(solution)/shard_map/ppermute | solution.py:243
  52.0 33.2 %collective-permute-start.19 = (bf16[8,128,128]{2,1,0:T(8,128)(2,1)S(1)}, bf16[8,128,128]{2,1,0:T(8,128)(2,1)S(1)}, u32[]{:S(2)}, u32[]{:S(2)}) collective-permute-start(bf16[8,128,128]{2,1,0:T(8,128)(2,1)S(1)} %get-tuple-element.79), channel_id=1, source_target_pairs={{0,1},{1,0},{2,3},{3,2},{4,5},{5,4},{6,7},{7,6},{8,9},{9,8},{10,11... | collective-permute-start | bytes 786440 | tf_op jit(solution)/shard_map/ppermute | solution.py:240
  57.1 34.4 %collective-permute-start.18 = (bf16[8,128,128]{2,1,0:T(8,128)(2,1)}, bf16[8,128,128]{2,1,0:T(8,128)(2,1)S(1)}, u32[]{:S(2)}, u32[]{:S(2)}) collective-permute-start(bf16[8,128,128]{2,1,0:T(8,128)(2,1)} %get-tuple-element.78), channel_id=1, source_target_pairs={{1,2},{2,1},{5,6},{6,5},{9,10},{10,9},{13,14},{14,13},{17,18},{18,... | collective-permute-start | bytes 786440 | tf_op jit(solution)/shard_map/ppermute | solution.py:243
  57.8 5.4 %collective-permute-start.5 = (s32[8,4]{0,1:T(4,128)S(1)}, s32[8,4]{0,1:T(4,128)S(1)}, u32[]{:S(2)}, u32[]{:S(2)}) collective-permute-start(s32[8,4]{0,1:T(4,128)S(1)} %copy-done.1), channel_id=1, source_target_pairs={{0,1},{1,2},{2,3},{3,0},{4,5},{5,6},{6,7},{7,4},{8,9},{9,10},{10,1... | collective-permute-start | bytes 392 | tf_op jit(solution)/shard_map/ppermute | solution.py:18
  63.2 5.6 %collective-permute-start.4 = (s32[8,4]{0,1:T(4,128)S(1)}, s32[8,4]{0,1:T(4,128)S(1)}, u32[]{:S(2)}, u32[]{:S(2)}) collective-permute-start(s32[8,4]{0,1:T(4,128)S(1)} %copy-done.1), channel_id=1, source_target_pairs={{0,2},{1,3},{2,0},{3,1},{4,6},{5,7},{6,4},{7,5},{8,10},{9,11},{10,... | collective-permute-start | bytes 392 | tf_op jit(solution)/shard_map/ppermute | solution.py:18
  68.8 3.6 %collective-permute-start.3 = (s32[8,4]{0,1:T(4,128)S(1)}, s32[8,4]{0,1:T(4,128)S(1)}, u32[]{:S(2)}, u32[]{:S(2)}) collective-permute-start(s32[8,4]{0,1:T(4,128)S(1)} %copy-done.1), channel_id=1, source_target_pairs={{0,3},{1,0},{2,1},{3,2},{4,7},{5,4},{6,5},{7,6},{8,11},{9,8},{10,9... | collective-permute-start | bytes 392 | tf_op jit(solution)/shard_map/ppermute | solution.py:18
  76.4 1.4 %collective-permute-start.6 = (s32[1]{0:T(128)}, s32[1]{0:T(128)}, u32[]{:S(2)}, u32[]{:S(2)}) collective-permute-start(s32[1]{0:T(128)} %get-tuple-element.67), channel_id=1, source_target_pairs={{0,4},{4,0},{8,12},{12,8},{16,20},{20,16},{24,28},{28,24},{1,5},{5... | collective-permute-start | bytes 20 | tf_op jit(solution)/shard_map/ppermute | solution.py:283
  79.1 3.7 %collective-permute-start.7 = (s32[1]{0:T(128)}, s32[1]{0:T(128)}, u32[]{:S(2)}, u32[]{:S(2)}) collective-permute-start(s32[1]{0:T(128)} %max.9), channel_id=1, source_target_pairs={{0,8},{4,12},{8,0},{12,4},{16,24},{20,28},{24,16},{28,20},{1,9},{5... | collective-permute-start | bytes 20 | tf_op jit(solution)/shard_map/ppermute | solution.py:283
  83.4 8.8 %collective-permute-start.8 = (s32[1]{0:T(128)}, s32[1]{0:T(128)}, u32[]{:S(2)}, u32[]{:S(2)}) collective-permute-start(s32[1]{0:T(128)} %max.10), channel_id=1, source_target_pairs={{0,16},{4,20},{8,24},{12,28},{16,0},{20,4},{24,8},{28,12},{1,17},{... | collective-permute-start | bytes 20 | tf_op jit(solution)/shard_map/ppermute | solution.py:283
  86.0 8.8 %collective-permute-start.20 = (bf16[8,128,128]{2,1,0:T(8,128)(2,1)S(1)}, bf16[8,128,128]{2,1,0:T(8,128)(2,1)S(1)}, u32[]{:S(2)}, u32[]{:S(2)}) collective-permute-start(bf16[8,128,128]{2,1,0:T(8,128)(2,1)S(1)} %get-tuple-element.80), channel_id=1, source_target_pairs={{1,2},{2,1},{5,6},{6,5},{9,10},{10,9},{13,14},{14,13},{17,18},{18,... | collective-permute-start | bytes 786440 | tf_op jit(solution)/shard_map/ppermute | solution.py:243
  86.7 12.0 %collective-permute-start.22 = (bf16[8,128,128]{2,1,0:T(8,128)(2,1)S(1)}, bf16[8,128,128]{2,1,0:T(8,128)(2,1)S(1)}, u32[]{:S(2)}, u32[]{:S(2)}) collective-permute-start(bf16[8,128,128]{2,1,0:T(8,128)(2,1)S(1)} %get-tuple-element.82), channel_id=1, source_target_pairs={{0,1},{1,0},{2,3},{3,2},{4,5},{5,4},{6,7},{7,6},{8,9},{9,8},{10,11... | collective-permute-start | bytes 786440 | tf_op jit(solution)/shard_map/ppermute | solution.py:240
  92.1 12.2 %collective-permute-start.24 = (bf16[8,128,128]{2,1,0:T(8,128)(2,1)S(1)}, bf16[8,128,128]{2,1,0:T(8,128)(2,1)S(1)}, u32[]{:S(2)}, u32[]{:S(2)}) collective-permute-start(bf16[8,128,128]{2,1,0:T(8,128)(2,1)S(1)} %relay7.1), channel_id=1, source_target_pairs={{0,1},{1,0},{2,3},{3,2},{4,5},{5,4},{6,7},{7,6},{8,9},{9,8},{10,11... | collective-permute-start | bytes 786440 | tf_op jit(solution)/shard_map/ppermute | solution.py:240
  92.2 17.6 %collective-permute-start.23 = (bf16[8,128,128]{2,1,0:T(8,128)(2,1)S(1)}, bf16[8,128,128]{2,1,0:T(8,128)(2,1)S(1)}, u32[]{:S(2)}, u32[]{:S(2)}) collective-permute-start(bf16[8,128,128]{2,1,0:T(8,128)(2,1)S(1)} %get-tuple-element.83), channel_id=1, source_target_pairs={{0,1},{1,0},{2,3},{3,2},{4,5},{5,4},{6,7},{7,6},{8,9},{9,8},{10,11... | collective-permute-start | bytes 786440 | tf_op jit(solution)/shard_map/ppermute | solution.py:240
  95.4 22.8 %collective-permute-start.21 = (bf16[8,128,128]{2,1,0:T(8,128)(2,1)S(1)}, bf16[8,128,128]{2,1,0:T(8,128)(2,1)S(1)}, u32[]{:S(2)}, u32[]{:S(2)}) collective-permute-start(bf16[8,128,128]{2,1,0:T(8,128)(2,1)S(1)} %relay8.1), channel_id=1, source_target_pairs={{0,1},{1,0},{2,3},{3,2},{4,5},{5,4},{6,7},{7,6},{8,9},{9,8},{10,11... | collective-permute-start | bytes 786440 | tf_op jit(solution)/shard_map/ppermute | solution.py:240
  109.8 8.4 %copy-start.2 = (s32[8,8]{1,0:T(8,128)S(1)}, s32[8,8]{1,0:T(8,128)}, u32[]{:S(2)}) copy-start(s32[8,8]{1,0:T(8,128)} %param.11) | copy-start | bytes 772
  121.6 1.3 %copy-start = (bf16[8,8,128,128]{3,2,1,0:T(8,128)(2,1)}, bf16[8,8,128,128]{3,2,1,0:T(8,128)(2,1)S(1)}, u32[]{:S(2)}) copy-start(bf16[8,8,128,128]{3,2,1,0:T(8,128)(2,1)S(1)} %get-tuple-element.129) | copy-start | bytes 6291460

commit v3 on v0

v3 whole, which is shorter than its diff:
```python
import functools

import jax
import jax.numpy as jnp
from jax import lax
from jax.experimental import pallas as pl
from jax.experimental.pallas import tpu as pltpu
from jax.sharding import PartitionSpec as P

STEPS = 4
T_SECOND, T_RIGHT = 5, 0
NOTE = 16
MIB = 1024 * 1024


def slots(blocks):
    return blocks // 2, 3 * blocks // 4, 3 * blocks // 8, 9 * blocks // 16


def from_behind(array, axis, by):
    size = lax.axis_size(axis)
    return lax.ppermute(array, axis, [(i, (i + by) % size) for i in range(size)])


def smem():
    return pl.BlockSpec(memory_space=pltpu.SMEM)


def whole():
    return pl.BlockSpec(memory_space=pltpu.VMEM)


def anywhere():
    return pl.BlockSpec(memory_space=pl.ANY)


def in_hbm():
    return pl.BlockSpec(memory_space=pltpu.HBM)


def params(mib=8):
    return pltpu.CompilerParams(vmem_limit_bytes=mib * MIB)


def cost(flops, nbytes):
    return pl.CostEstimate(flops=int(flops), bytes_accessed=int(nbytes), transcendentals=0)


def wide(a_ref):
    kb, blk = a_ref.shape[1], a_ref.shape[-1]
    return jnp.concatenate([a_ref[:, k].reshape(-1, blk) for k in range(kb)], axis=1)


def tall(b_ref):
    kb, bc = b_ref.shape[:2]
    return jnp.concatenate(
        [jnp.concatenate([b_ref[k, j] for j in range(bc)], axis=1) for k in range(kb)], axis=0
    )


def filtered(c_ref, i, j, block):
    return (block * c_ref[i, j].astype(jnp.float32)).astype(jnp.bfloat16)


def token_kernel(*refs):
    refs[-1][...] = jnp.zeros_like(refs[-1])


def token(seen, us):
    return pl.pallas_call(
        token_kernel,
        in_specs=[anywhere()] * len(seen),
        out_specs=whole(),
        out_shape=jax.ShapeDtypeStruct((8, 128), jnp.float32),
        compiler_params=params(),
        cost_estimate=cost(us * 1.1e9, 0),
        name="token",
    )(*seen)


def passed(x, seen):
    return pl.pallas_call(
        lambda *refs: None,
        in_specs=[anywhere()] * (1 + len(seen)),
        out_specs=anywhere(),
        out_shape=jax.ShapeDtypeStruct(x.shape, x.dtype),
        input_output_aliases={0: 0},
        compiler_params=params(),
        cost_estimate=cost(0, 0),
        name="passed",
    )(x, *seen)


def live_kernel(by_column, mask_ref, x_ref, *refs):
    out_ref = refs[-1]
    i = pl.program_id(0)
    for j in range(x_ref.shape[1]):
        keep = mask_ref[j, i] if by_column else mask_ref[i, j]
        out_ref[0, j] = x_ref[0, j] * keep.astype(jnp.float32).astype(x_ref.dtype)


def live(blocks, mask, by_column=False, after=()):
    shape = (1,) + blocks.shape[1:]
    return pl.pallas_call(
        functools.partial(live_kernel, by_column),
        grid=(blocks.shape[0],),
        in_specs=[smem(), pl.BlockSpec(shape, lambda g: (g, 0, 0, 0))] + [anywhere()] * len(after),
        out_specs=pl.BlockSpec(shape, lambda g: (g, 0, 0, 0)),
        out_shape=jax.ShapeDtypeStruct(blocks.shape, blocks.dtype),
        compiler_params=params(),
        cost_estimate=cost(0, 4 * blocks.size),
        name="live",
    )(mask, blocks, *after)


def dense_kernel(*refs):
    a_refs, b_refs, acc_ref = refs[:STEPS], refs[STEPS:-1], refs[-1]
    total = None
    for a_ref, b_ref in zip(a_refs, b_refs):
        part = jnp.dot(wide(a_ref), tall(b_ref), preferred_element_type=jnp.float32)
        total = part if total is None else total + part
    acc_ref[...] = total


def dense_sum(left, right):
    br, kb, blk, _ = left[0].shape
    bc = right[0].shape[1]
    wide_j = 2 if bc % 2 == 0 else 1
    return pl.pallas_call(
        dense_kernel,
        grid=(bc // wide_j,),
        in_specs=[pl.BlockSpec((br, kb, blk, blk), lambda g: (0, 0, 0, 0))] * STEPS
        + [pl.BlockSpec((kb, wide_j, blk, blk), lambda g: (0, g, 0, 0))] * STEPS,
        out_specs=pl.BlockSpec((br * blk, wide_j * blk), lambda g: (0, g)),
        out_shape=jax.ShapeDtypeStruct((br * blk, bc * blk), jnp.float32),
        compiler_params=params(32),
        cost_estimate=cost(2 * STEPS * br * bc * kb * blk**3, 12 << 20),
        name="dense",
    )(*left, *right)


def filter_kernel(c_ref, acc_ref, out_ref):
    blk = out_ref.shape[-1]
    for j in range(out_ref.shape[1]):
        out_ref[0, j] = filtered(c_ref, pl.program_id(0), j, acc_ref[:, j * blk : (j + 1) * blk])


def filter_sum(total, c_mask, blk):
    br, bc = c_mask.shape
    return pl.pallas_call(
        filter_kernel,
        grid=(br,),
        in_specs=[smem(), pl.BlockSpec((blk, bc * blk), lambda g: (g, 0))],
        out_specs=pl.BlockSpec((1, bc, blk, blk), lambda g: (g, 0, 0, 0)),
        out_shape=jax.ShapeDtypeStruct((br, bc, blk, blk), jnp.bfloat16),
        compiler_params=params(),
        name="filter",
    )(c_mask, total)


def dense_product(a_blocks, a_mask, b_blocks, b_mask, c_mask):
    left = [live(a_blocks, a_mask.T, by_column=True)]
    right = [live(b_blocks, b_mask)]
    for _ in range(1, STEPS):
        left.append(from_behind(left[-1], "col", -1))
        right.append(from_behind(right[-1], "row", -1))
    return filter_sum(dense_sum(left, right), c_mask, a_blocks.shape[-1])


def compact_kernel(mask_ref, a_ref, lead_ref, head_ref, inner_ref, tail_ref, n_ref, list_ref):
    br, kb, blk = a_ref.shape[:3]
    head, lead, inner, _ = slots(br * kb)
    lanes = lax.broadcasted_iota(jnp.int32, (NOTE, blk), 1)
    note = jnp.zeros((NOTE, blk), jnp.int32)
    count = jnp.int32(0)
    for k in range(kb):
        for i in range(br):
            list_ref[pl.ds(pl.multiple_of(count * blk, blk), blk), :] = a_ref[i, k]
            note = jnp.where(lanes == k * br + i, mask_ref[k, i], note)
            count = count + mask_ref[k, i]
    note = note.astype(jnp.float32).astype(jnp.bfloat16)
    lead_ref[0 : lead * blk, :] = list_ref[0 : lead * blk, :]
    lead_ref[lead * blk :, :] = note
    head_ref[0 : head * blk, :] = list_ref[0 : head * blk, :]
    head_ref[head * blk :, :] = note
    inner_ref[...] = list_ref[head * blk : (head + inner) * blk, :]
    tail_ref[...] = list_ref[head * blk :, :]
    n_ref[0] = count


def pool_kernel(skip, n_ref, tail_ref, more_ref, *refs):
    out_ref, line = refs[-2:]
    blk = out_ref.shape[1]
    first = skip * blk - tail_ref.shape[0]
    own = tail_ref.shape[0] - first
    line[0:own, :] = tail_ref[first:, :]
    at = pl.multiple_of(jnp.maximum(n_ref[0] - skip, 0) * blk, blk)
    line[pl.ds(at, more_ref.shape[0]), :] = more_ref[...]
    out_ref[...] = line[0 : out_ref.shape[0], :]


def table_kernel(blocks, where_ref, own_ref, *refs):
    notes, (table_ref, over_ref, note_ref, wide_ref, mask_ref, sems, sem) = refs[:6], refs[6:]
    copies = [
        pltpu.make_async_copy(
            ref.at[pl.ds(ref.shape[0] - NOTE, NOTE), :], note_ref.at[pl.ds(m * NOTE, NOTE), :], sems.at[m]
        )
        for m, ref in enumerate(notes)
    ]
    for copy in copies:
        copy.start()
    for copy in copies:
        copy.wait()
    wide_ref[...] = note_ref[...].astype(jnp.float32).astype(jnp.int32)
    down = pltpu.make_async_copy(wide_ref, mask_ref, sem)
    down.start()
    down.wait()

    none, apart = STEPS * blocks, blocks + 8
    head, lead, inner, pool = slots(blocks)
    z = where_ref[0]
    at_end = jnp.logical_or(z == 0, z == 3)
    near = 1 + 2 * (z % 2)
    flip = where_ref[1] % 2 == 1

    def place_of(step):
        return jnp.where(flip, 4 - step, step)

    def fill(base, place, m):
        count = jnp.int32(base)
        for b in range(blocks):
            table_ref[count] = place * blocks + b
            count = count + mask_ref[m * NOTE, b]

        def pad(p, carry):
            table_ref[p] = none
            return carry

        lax.fori_loop(count, base + blocks, pad, 0)
        return count - base

    first = fill(0, place_of(near), jnp.where(at_end, 0, 3))
    second = fill(apart, jnp.where(at_end, 2, place_of(4 - near)), jnp.where(at_end, 1, 4))
    third = fill(2 * apart, jnp.where(at_end, place_of(4 - near), 2), jnp.where(at_end, 2, 5))

    def append(base, begin, length, at):
        def body(p, at):
            table_ref[at] = table_ref[base + p]
            return at + 1

        return lax.fori_loop(begin, length, body, at)

    at = append(0, jnp.where(at_end, lead, blocks), first, jnp.int32(3 * apart))
    at = append(apart, head, second, at)
    at = append(2 * apart, head, third, at)

    def pad(p, carry):
        table_ref[p] = none
        return carry

    lax.fori_loop(at, 3 * apart + pool, pad, 0)

    own = jnp.int32(0)
    for k in range(own_ref.shape[0]):
        for i in range(own_ref.shape[1]):
            own = own + own_ref[k, i]

    def past(n, by):
        return jnp.maximum(n - by, 0)

    def overflows(next_one, middle, far):
        pooled = past(next_one, lead) + past(middle, head) + past(far, head)
        return jnp.logical_or(pooled > pool, far > head + inner)

    ends_view = jnp.logical_or(overflows(first, second, third), overflows(second, first, own))
    middles_view = jnp.logical_or(overflows(own, second, third), overflows(second, own, first))
    over_ref[0] = jnp.where(jnp.where(at_end, ends_view, middles_view), 1, 0).astype(jnp.int32)


def masked_tall(mask_ref, b_ref, j0):
    kb, bc = b_ref.shape[:2]

    def block(k, j):
        return b_ref[k, j] * mask_ref[k, j0 + j].astype(jnp.float32).astype(b_ref.dtype)

    return jnp.concatenate([jnp.concatenate([block(k, j) for j in range(bc)], axis=1) for k in range(kb)], axis=0)


def early_kernel(where_ref, mask_ref, c_ref, table_ref, *refs):
    b_masks, a_ref, refs = refs[:STEPS], refs[STEPS], refs[STEPS + 1 :]
    outs, mids, b_refs, (acc_ref, out_ref, left_ref) = refs[:3], refs[3:8], refs[8:12], refs[12:]
    br, kb, blk, _ = a_ref.shape
    blocks = br * kb
    apart = blocks + 8
    head, lead, inner, pool = slots(blocks)
    z = where_ref[0]
    at_end = jnp.logical_or(z == 0, z == 3)

    def scatter(ref, first, length):
        for b in range(length):
            place = table_ref[first + b]
            row = pl.multiple_of((place % br) * blk, blk)
            column = pl.multiple_of((place // br) * blk, blk)
            left_ref[pl.ds(row, blk), pl.ds(column, blk)] = ref[b * blk : (b + 1) * blk, :]

    @pl.when(pl.program_id(0) == 0)
    def _():
        for k in range(kb):
            for i in range(br):
                left_ref[i * blk : (i + 1) * blk, k * blk : (k + 1) * blk] = a_ref[i, k] * mask_ref[k, i].astype(
                    jnp.float32
                ).astype(jnp.bfloat16)
        left_ref[:, kb * blk :] = jnp.zeros((br * blk, left_ref.shape[1] - kb * blk), jnp.bfloat16)

        @pl.when(at_end)
        def _():
            scatter(outs[0], 0, lead)
            scatter(outs[1], apart, head)
            scatter(outs[2], 2 * apart, head)

        @pl.when(jnp.logical_not(at_end))
        def _():
            scatter(mids[0], 0, head)
            scatter(mids[1], head, inner)
            scatter(mids[2], apart, head)
            scatter(mids[3], 2 * apart, head)
            scatter(mids[4], 3 * apart, pool)

    j0 = pl.program_id(0) * out_ref.shape[1]
    total = None
    for t in range(STEPS):
        part = jnp.dot(
            left_ref[:, t * kb * blk : (t + 1) * kb * blk],
            masked_tall(b_masks[t], b_refs[t], j0),
            preferred_element_type=jnp.float32,
        )
        total = part if total is None else total + part
    acc_ref[...] = total
    for i in range(br):
        for j in range(out_ref.shape[1]):
            out_ref[i, j] = filtered(c_ref, i, j0 + j, total[i * blk : (i + 1) * blk, j * blk : (j + 1) * blk])


def late_kernel(where_ref, c_ref, table_ref, *refs):
    b_masks, refs = refs[: STEPS - 1], refs[STEPS - 1 :]
    late_ref, acc_ref, b_refs, refs = refs[0], refs[1], refs[2 : 1 + STEPS], refs[2 + STEPS :]
    out_ref, row_ref, sems = refs
    br, bc, blk, _ = out_ref.shape
    kb = b_refs[0].shape[0]
    none = STEPS * kb * br
    _, _, _, pool = slots(kb * br)
    first = 3 * (kb * br + 8)
    at_end = jnp.logical_or(where_ref[0] == 0, where_ref[0] == 3)
    places = [jnp.where(at_end, table_ref[first + b], none) for b in range(pool)]

    for b, place in enumerate(places):
        for slab, (b_ref, mask_ref) in enumerate(zip(b_refs, b_masks)):

            @pl.when(place // (kb * br) == slab + 1)
            def _():
                row, k = pl.multiple_of((place % br) * blk, blk), (place // br) % kb
                keep = [mask_ref[k, j].astype(jnp.float32).astype(jnp.bfloat16) for j in range(bc)]
                columns = jnp.concatenate([b_ref[k, j] * keep[j] for j in range(bc)], axis=1)
                acc_ref[pl.ds(row, blk), :] += jnp.dot(
                    late_ref[b * blk : (b + 1) * blk, :], columns, preferred_element_type=jnp.float32
                )

    go = [pltpu.make_async_copy(row_ref.at[i], out_ref.at[i], sems.at[i]) for i in range(br)]
    touched = [
        functools.reduce(jnp.logical_or, [jnp.logical_and(p < none, p % br == i) for p in places]) for i in range(br)
    ]
    for i in range(br):

        @pl.when(touched[i])
        def _():
            for j in range(bc):
                row_ref[i, j] = filtered(c_ref, i, j, acc_ref[i * blk : (i + 1) * blk, j * blk : (j + 1) * blk])
            go[i].start()

    for i in range(br):

        @pl.when(touched[i])
        def _():
            go[i].wait()


def sparse_product(a_blocks, a_mask, b_blocks, b_mask, c_mask):
    br, kb, blk, _ = a_blocks.shape
    bc = b_blocks.shape[1]
    blocks = br * kb
    head, lead, inner, pool = slots(blocks)
    rows = lax.axis_size("row")
    where = jnp.stack([lax.axis_index("col"), lax.axis_index("row")]).astype(jnp.int32)
    by_column = a_mask.T

    def outward(x):
        return lax.ppermute(x, "col", [(1, 0), (2, 3)])

    def inward(x):
        return lax.ppermute(x, "col", [(0, 1), (3, 2)])

    def over_middle(x):
        return lax.ppermute(x, "col", [(1, 2), (2, 1)])

    def two_up(x):
        return from_behind(x, "row", -2)

    def odd_up(x):
        return lax.ppermute(x, "row", [((r + 1 + 2 * (r % 2)) % rows, r) for r in range(rows)])

    def core_swap(x):
        return lax.ppermute(x, "row", [(r, r ^ 1) for r in range(rows)])

    def listed(slot_count, note=0):
        return jax.ShapeDtypeStruct((slot_count * blk + note, blk), a_blocks.dtype)

    with jax.named_scope("right_two_up"):
        second = two_up(b_blocks)
    with jax.named_scope("right_odd_up"):
        odd_one = odd_up(b_blocks)
    with jax.named_scope("right_masks"):
        second_mask, odd_mask = two_up(b_mask), odd_up(b_mask)
        b_masks = [b_mask, odd_mask, second_mask, core_swap(second_mask)]

    own_lead, own_head, own_inner, own_tail, n = pl.pallas_call(
        compact_kernel,
        in_specs=[smem(), whole()],
        out_specs=[whole(), whole(), whole(), whole(), smem()],
        out_shape=[
            listed(lead, NOTE),
            listed(head, NOTE),
            listed(inner),
            listed(blocks - head),
            jax.ShapeDtypeStruct((1,), jnp.int32),
        ],
        scratch_shapes=[pltpu.VMEM((blocks * blk, blk), a_blocks.dtype)],
        compiler_params=params(),
        cost_estimate=cost(0, 6 * blocks * blk * blk),
        name="compact",
    )(by_column, a_blocks)

    def pooled(skip, more, gate, seen):
        own = blocks - skip
        outs = pl.pallas_call(
            functools.partial(pool_kernel, skip),
            in_specs=[smem(), whole(), whole()] + [anywhere()] * (len(gate) + len(seen)),
            out_specs=[anywhere()] * len(gate) + [whole()],
            out_shape=[jax.ShapeDtypeStruct(g.shape, g.dtype) for g in gate] + [listed(pool)],
            scratch_shapes=[pltpu.VMEM((own * blk + more.shape[0], blk), a_blocks.dtype)],
            input_output_aliases={3 + g: g for g in range(len(gate))},
            compiler_params=params(),
            cost_estimate=cost(0, 6 * pool * blk * blk),
            name="pool",
        )(n, own_tail, more, *gate, *seen)
        return outs[-1], outs[:-1]

    with jax.named_scope("lead_outward"):
        near_lead = outward(own_lead)
    with jax.named_scope("head_inward"):
        near_head = inward(own_head)
    with jax.named_scope("head_over_middle"):
        mid_head = over_middle(own_head)
    with jax.named_scope("second_head_outward"):
        mid_head = passed(mid_head, [near_lead])
        second_head = outward(mid_head)
    with jax.named_scope("tail_inward"):
        near_tail = inward(passed(own_inner, [near_lead]))
    with jax.named_scope("end_head_over_middle"):
        end_head = over_middle(near_head)
    with jax.named_scope("third_head_outward"):
        third_head = outward(end_head)
    mid_pool, _ = pooled(head, near_tail, [], [end_head])
    with jax.named_scope("pool_over_middle"):
        mid_pool = over_middle(mid_pool)
    slabs_here = token([second, odd_one], T_RIGHT)
    out_pool, (second, odd_one) = pooled(
        lead, mid_pool, [second, odd_one], [token([second_head], T_SECOND), slabs_here, third_head] + b_masks[1:]
    )
    with jax.named_scope("pool_outward"):
        out_pool = outward(out_pool)
    with jax.named_scope("right_core_swap"):
        right = [b_blocks, odd_one, second, core_swap(second)]

    table, over = pl.pallas_call(
        functools.partial(table_kernel, blocks),
        in_specs=[smem(), smem()] + [anywhere()] * 6,
        out_specs=[smem(), smem()],
        out_shape=[jax.ShapeDtypeStruct((5 * (blocks + 8),), jnp.int32), jax.ShapeDtypeStruct((1,), jnp.int32)],
        scratch_shapes=[
            pltpu.VMEM((6 * NOTE, blk), jnp.bfloat16),
            pltpu.VMEM((6 * NOTE, blk), jnp.int32),
            pltpu.SMEM((6 * NOTE, blk), jnp.int32),
            pltpu.SemaphoreType.DMA((6,)),
            pltpu.SemaphoreType.DMA,
        ],
        compiler_params=params(),
        name="table",
    )(where, by_column, near_lead, second_head, third_head, near_head, mid_head, end_head)

    def fixed(x):
        return pl.BlockSpec(x.shape, lambda g: (0,) * x.ndim)

    wide_j = 2 if bc % 2 == 0 else 1
    arrived = [near_lead, second_head, third_head, near_head, near_tail, mid_head, end_head, mid_pool]
    acc, out = pl.pallas_call(
        early_kernel,
        grid=(bc // wide_j,),
        in_specs=[smem()] * (4 + STEPS)
        + [fixed(x) for x in [a_blocks] + arrived]
        + [pl.BlockSpec((kb, wide_j, blk, blk), lambda g: (0, g, 0, 0))] * STEPS,
        out_specs=[
            pl.BlockSpec((br * blk, wide_j * blk), lambda g: (0, g)),
            pl.BlockSpec((br, wide_j, blk, blk), lambda g: (0, g, 0, 0)),
        ],
        out_shape=[
            jax.ShapeDtypeStruct((br * blk, bc * blk), jnp.float32),
            jax.ShapeDtypeStruct((br, bc, blk, blk), jnp.bfloat16),
        ],
        scratch_shapes=[pltpu.VMEM((br * blk, (STEPS * kb + 1) * blk), a_blocks.dtype)],
        compiler_params=params(32),
        cost_estimate=cost(2 * STEPS * br * bc * kb * blk**3, 14 << 20),
        name="early",
    )(where, by_column, c_mask, table, *b_masks, a_blocks, *arrived, *right)

    out = pl.pallas_call(
        late_kernel,
        in_specs=[smem()] * (3 + STEPS - 1) + [whole()] * (1 + STEPS) + [in_hbm()],
        out_specs=in_hbm(),
        out_shape=jax.ShapeDtypeStruct((br, bc, blk, blk), jnp.bfloat16),
        scratch_shapes=[pltpu.VMEM((br, bc, blk, blk), jnp.bfloat16), pltpu.SemaphoreType.DMA((br,))],
        input_output_aliases={3 + STEPS - 1 + 1 + STEPS: 0},
        compiler_params=params(24),
        cost_estimate=cost(0, 4 << 20),
        name="late",
    )(where, c_mask, table, *b_masks[1:], out_pool, acc, *right[1:], out)

    def again(state):
        before, trips = state
        left = [live(a_blocks, by_column, by_column=True, after=(before,))]
        for _ in range(1, STEPS):
            left.append(from_behind(left[-1], "col", -1))
        odd = lax.axis_index("row") % 2 == 1
        held = [live(slab, mask, after=(before,)) for slab, mask in zip(right, b_masks)]
        ordered = [held[0], jnp.where(odd, held[3], held[1]), held[2], jnp.where(odd, held[1], held[3])]
        return filter_sum(dense_sum(left, ordered), c_mask, blk), trips - 1

    out, _ = lax.while_loop(lambda state: state[1] > 0, again, (out, over[0]))
    return out


def on_device(a_blocks, a_mask, b_blocks, b_mask, c_mask):
    blocks = a_blocks.shape[0] * a_blocks.shape[1]
    fits = blocks % 16 == 0 and blocks <= a_blocks.shape[-1]
    if lax.axis_size("col") == STEPS and lax.axis_size("row") % 2 == 0 and fits:
        return sparse_product(a_blocks, a_mask, b_blocks, b_mask, c_mask)
    return dense_product(a_blocks, a_mask, b_blocks, b_mask, c_mask)


def solution(mesh):
    return jax.shard_map(
        on_device,
        mesh=mesh,
        in_specs=(
            P("row", "col", None, None),
            P("row", "col"),
            P("row", "col", None, None),
            P("row", "col"),
            P("row", "col"),
        ),
        out_specs=P("row", "col", None, None),
        check_vma=False,
    )
```

time: 93.1 us -> 83.8 us (0.900)
  the two profiles are of different devices: /device:TPU:26 before, /device:TPU:0 now
where the time goes in v3:
time: 83.8 us; the launch traced here: 82.9 us
  starting transfers between devices  30.2 us (36%)
  waiting for transfers between devices  25.8 us (31%)
  Pallas kernels  20.3 us (24%)
  local copies, waits for them, and re-layouts  5.27 us (6%)
    ppermute x2, waiting for transfers between devices, inward(): return lax.ppermute(x, 'col', [(0, 1), (3, 2)])  13.8 us
    ppermute x4, waiting for transfers between devices, outward(): return lax.ppermute(x, 'col', [(1, 0), (2, 3)])  11.7 us
    ppermute x2, starting transfers between devices, inward(): return lax.ppermute(x, 'col', [(0, 1), (3, 2)])  10.4 us
    ppermute x2, starting transfers between devices, from_behind(): lax.ppermute(array, axis, [(i, (i + by) % size) for i in range(size)])  9.29 us
    pallas_call x1, Pallas kernels, sparse_product(): pl.pallas_call(early_kernel, grid=(bc // wide_j,), in_specs=[smem()] * (4...  8.19 us
    ppermute x4, starting transfers between devices, outward(): return lax.ppermute(x, 'col', [(1, 0), (2, 3)])  5.28 us
    unnamed x46, local copies, waits for them, and re-layouts  5.27 us
    pallas_call x1, Pallas kernels, sparse_product(): pl.pallas_call(late_kernel, in_specs=[smem()] * (3 + STEPS - 1) + [whole(...  4.52 us
  transfers between devices with their start and end apart: 15, of which 6 were waited for; matrix products, arithmetic and copies ran while one was open for 0% of the time, Pallas kernels for 15%

profile of v3, /device:TPU:0, one launch (start us, length us, event | category | flops | bytes accessed | tf_op | source)
XLA Modules:
  0.0 82.9 jit_solution(17559926419796586328)
XLA Ops:
  0.0 1.8 %compact.1 = (bf16[3088,128]{1,0:T(8,128)(2,1)S(1)}, bf16[2064,128]{1,0:T(8,128)(2,1)S(1)}, bf16[1536,128]{1,0:T(8,128)(2,1)S(1)}, bf16[2048,128]{1,0:T(8,128)(2,1)S(1)}, s32[1]{0:T(128)}) custom-call(s32[4,8]{1,0:T(4,128)} %bitcast.4, bf16[8,4,128,128]{3,2,1,0:T(8,128)(2,1)} %refs_4_.1), custom_call_target="tpu_custom_call" | custom-call | bytes 3145728 | tf_op jit(solution)/shard_map/compact/pallas_call | solution.py:425
  1.8 1.3 %collective-permute-start.3 = (bf16[3088,128]{1,0:T(8,128)(2,1)S(1)}, bf16[3088,128]{1,0:T(8,128)(2,1)S(1)}, u32[]{:S(2)}, u32[]{:S(2)}) collective-permute-start(bf16[3088,128]{1,0:T(8,128)(2,1)S(1)} %get-tuple-element.167), channel_id=1, source_target_pairs={{1,0},{2,3},{5,4},{6,7},{9,8},{10,11},{13,12},{14,15},{17,16},{18,... | collective-permute-start | bytes 2371592 | tf_op jit(solution)/shard_map/lead_outward/ppermute | solution.py:397
  3.1 5.0 %collective-permute-start.6 = (bf16[2064,128]{1,0:T(8,128)(2,1)S(1)}, bf16[2064,128]{1,0:T(8,128)(2,1)S(1)}, u32[]{:S(2)}, u32[]{:S(2)}) collective-permute-start(bf16[2064,128]{1,0:T(8,128)(2,1)S(1)} %get-tuple-element.168), channel_id=1, source_target_pairs={{0,1},{3,2},{4,5},{7,6},{8,9},{11,10},{12,13},{15,14},{16,17},{19,... | collective-permute-start | bytes 1585160 | tf_op jit(solution)/shard_map/head_inward/ppermute | solution.py:400
  8.1 0.7 collective-permute-start.4
  8.8 1.5 %collective-permute-start.15 = (bf16[4,8,128,128]{3,2,1,0:T(8,128)(2,1)}, bf16[4,8,128,128]{3,2,1,0:T(8,128)(2,1)S(1)}, u32[]{:S(2)}, u32[]{:S(2)}) collective-permute-start(bf16[4,8,128,128]{3,2,1,0:T(8,128)(2,1)} %refs_13_.1), channel_id=1, source_target_pairs={{4,0},{16,4},{12,8},{24,12},{20,16},{0,20},{28,24},{8,28},{5,1},{1... | collective-permute-start | bytes 3145736 | tf_op jit(solution)/shard_map/right_odd_up/ppermute | solution.py:409
  10.3 2.1 %collective-permute-start.14 = (bf16[4,8,128,128]{3,2,1,0:T(8,128)(2,1)}, bf16[4,8,128,128]{3,2,1,0:T(8,128)(2,1)}, u32[]{:S(2)}, u32[]{:S(2)}) collective-permute-start(bf16[4,8,128,128]{3,2,1,0:T(8,128)(2,1)} %refs_13_.1), channel_id=1, source_target_pairs={{0,24},{4,28},{8,0},{12,4},{16,8},{20,12},{24,16},{28,20},{1,25},{... | collective-permute-start | bytes 3145736 | tf_op jit(solution)/shard_map/right_two_up/ppermute | solution.py:22
  12.5 6.9 %collective-permute-done.6.refs_3_.refs_8_ = bf16[2064,128]{1,0:T(8,128)(2,1)S(1)} collective-permute-done((bf16[2064,128]{1,0:T(8,128)(2,1)S(1)}, bf16[2064,128]{1,0:T(8,128)(2,1)S(1)}, u32[]{:S(2)}, u32[]{:S(2)}) %collective-permute-start.6) | collective-permute-done | bytes 528416 | tf_op jit(solution)/shard_map/head_inward/ppermute | solution.py:400
  19.4 0.7 collective-permute-start.7
  20.0 0.0 collective-permute-done.4.refs_0_
  20.1 3.7 %collective-permute-done.3.refs_1_.refs_0_.refs_5_ = bf16[3088,128]{1,0:T(8,128)(2,1)S(1)} collective-permute-done((bf16[3088,128]{1,0:T(8,128)(2,1)S(1)}, bf16[3088,128]{1,0:T(8,128)(2,1)S(1)}, u32[]{:S(2)}, u32[]{:S(2)}) %collective-permute-start.3) | collective-permute-done | bytes 790560 | tf_op jit(solution)/shard_map/lead_outward/ppermute | solution.py:397
  23.7 1.4 %collective-permute-start.5 = (bf16[2064,128]{1,0:T(8,128)(2,1)S(1)}, bf16[2064,128]{1,0:T(8,128)(2,1)S(1)}, u32[]{:S(2)}, u32[]{:S(2)}) collective-permute-start(bf16[2064,128]{1,0:T(8,128)(2,1)S(1)} %passed.2.refs_4_.refs_10_), channel_id=1, source_target_pairs={{1,0},{2,3},{5,4},{6,7},{9,8},{10,11},{13,12},{14,15},{17,16},{18,... | collective-permute-start | bytes 1585160 | tf_op jit(solution)/shard_map/second_head_outward/ppermute | solution.py:397
  25.2 5.4 %collective-permute-start.12 = (bf16[1536,128]{1,0:T(8,128)(2,1)S(1)}, bf16[1536,128]{1,0:T(8,128)(2,1)S(1)}, u32[]{:S(2)}, u32[]{:S(2)}) collective-permute-start(bf16[1536,128]{1,0:T(8,128)(2,1)S(1)} %passed.3), channel_id=1, source_target_pairs={{0,1},{3,2},{4,5},{7,6},{8,9},{11,10},{12,13},{15,14},{16,17},{19,... | collective-permute-start | bytes 1179656 | tf_op jit(solution)/shard_map/tail_inward/ppermute | solution.py:400
  30.5 0.0 collective-permute-done.7.refs_5_.refs_0_.refs_11_
  30.6 7.0 %collective-permute-done.12.more_ref.refs_9_ = bf16[1536,128]{1,0:T(8,128)(2,1)S(1)} collective-permute-done((bf16[1536,128]{1,0:T(8,128)(2,1)S(1)}, bf16[1536,128]{1,0:T(8,128)(2,1)S(1)}, u32[]{:S(2)}, u32[]{:S(2)}) %collective-permute-start.12) | collective-permute-done | bytes 393248 | tf_op jit(solution)/shard_map/tail_inward/ppermute | solution.py:400
  37.5 0.8 pool.2
  38.3 0.7 collective-permute-start.13
  39.0 0.0 copy-done.6
  39.0 1.3 %collective-permute-start.8 = (bf16[2064,128]{1,0:T(8,128)(2,1)S(1)}, bf16[2064,128]{1,0:T(8,128)(2,1)S(1)}, u32[]{:S(2)}, u32[]{:S(2)}) collective-permute-start(bf16[2064,128]{1,0:T(8,128)(2,1)S(1)} %collective-permute-done.7.refs_5_.refs_0_.refs_11_), channel_id=1, source_target_pairs={{1,0},{2,3},{5,4},{6,7},{9,8},{10,11},{13,12},{14,15},{17,16},{18,... | collective-permute-start | bytes 1585160 | tf_op jit(solution)/shard_map/third_head_outward/ppermute | solution.py:397
  40.3 0.0 collective-permute-done.15.refs_1_
  40.3 7.2 %collective-permute-start.10 = (s32[4,8]{1,0:T(4,128)S(1)}, s32[4,8]{1,0:T(4,128)S(1)}, u32[]{:S(2)}, u32[]{:S(2)}) collective-permute-start(s32[4,8]{1,0:T(4,128)S(1)} %copy-done.30), channel_id=1, source_target_pairs={{0,24},{4,28},{8,0},{12,4},{16,8},{20,12},{24,16},{28,20},{1,25},{... | collective-permute-start | bytes 392 | tf_op jit(solution)/shard_map/right_masks/ppermute | solution.py:22
  47.5 0.0 collective-permute-done.14.refs_0_
  47.5 1.5 %collective-permute-start.9 = (s32[4,8]{1,0:T(4,128)S(1)}, s32[4,8]{1,0:T(4,128)S(1)}, u32[]{:S(2)}, u32[]{:S(2)}) collective-permute-start(s32[4,8]{1,0:T(4,128)S(1)} %copy-done.30), channel_id=1, source_target_pairs={{4,0},{16,4},{12,8},{24,12},{20,16},{0,20},{28,24},{8,28},{5,1},{1... | collective-permute-start | bytes 392 | tf_op jit(solution)/shard_map/right_masks/ppermute | solution.py:409
  49.0 0.0 collective-permute-done.10.refs_6_.refs_2_.refs_1_
  49.0 0.2 collective-permute-start.11
  49.2 0.0 collective-permute-done.5.refs_1_.refs_0_.refs_6_
  49.2 0.8 copy-done.3
  50.0 0.3 collective-permute-done.9.refs_5_.refs_1_.refs_0_
  50.3 0.0 collective-permute-done.11.refs_7_.refs_3_.refs_2_
  50.4 6.4 %collective-permute-done.8.refs_2_.refs_4_.refs_7_ = bf16[2064,128]{1,0:T(8,128)(2,1)S(1)} collective-permute-done((bf16[2064,128]{1,0:T(8,128)(2,1)S(1)}, bf16[2064,128]{1,0:T(8,128)(2,1)S(1)}, u32[]{:S(2)}, u32[]{:S(2)}) %collective-permute-start.8) | collective-permute-done | bytes 528416 | tf_op jit(solution)/shard_map/third_head_outward/ppermute | solution.py:397
  56.8 0.0 collective-permute-done.13.more_ref.refs_12_
  56.8 1.6 %pool.3 = (bf16[4,8,128,128]{3,2,1,0:T(8,128)(2,1)}, bf16[4,8,128,128]{3,2,1,0:T(8,128)(2,1)S(1)}, bf16[2304,128]{1,0:T(8,128)(2,1)}) custom-call(s32[1]{0:T(128)} %get-tuple-element.170.n_ref, bf16[2048,128]{1,0:T(8,128)(2,1)S(1)} %get-tuple-element.171.tail_ref, ...), custom_call_target="tpu_custom_call", output_to_operand_aliasing={{0}: (3, {}), {1}: (4, {})} | custom-call | bytes 1769472 | tf_op jit(solution)/shard_map/pool/pallas_call | solution.py:444
  58.4 0.0 collective-permute-start.17
  58.4 1.0 %copy-done.10 = bf16[4,8,128,128]{3,2,1,0:T(8,128)(2,1)} copy-done((bf16[4,8,128,128]{3,2,1,0:T(8,128)(2,1)}, bf16[4,8,128,128]{3,2,1,0:T(8,128)(2,1)S(1)}, u32[]{:S(2)}) %copy-start.10) | copy-done | bytes 1048600
  59.4 1.3 %collective-permute-start.16 = (bf16[2304,128]{1,0:T(8,128)(2,1)}, bf16[2304,128]{1,0:T(8,128)(2,1)S(1)}, u32[]{:S(2)}, u32[]{:S(2)}) collective-permute-start(bf16[2304,128]{1,0:T(8,128)(2,1)} %get-tuple-element.173), channel_id=1, source_target_pairs={{1,0},{2,3},{5,4},{6,7},{9,8},{10,11},{13,12},{14,15},{17,16},{18,... | collective-permute-start | bytes 1769480 | tf_op jit(solution)/shard_map/pool_outward/ppermute | solution.py:397
  60.7 0.0 copy-start.16
  60.7 0.1 pad_add_fusion.where_ref
  60.8 1.0 %copy-done.1 = bf16[2064,128]{1,0:T(8,128)(2,1)S(1)} copy-done((bf16[2064,128]{1,0:T(8,128)(2,1)S(1)}, bf16[2064,128]{1,0:T(8,128)(2,1)}, u32[]{:S(2)}) %copy-start.1) | copy-done | bytes 528408
  61.8 1.0 %copy-done.4 = bf16[2064,128]{1,0:T(8,128)(2,1)S(1)} copy-done((bf16[2064,128]{1,0:T(8,128)(2,1)S(1)}, bf16[2064,128]{1,0:T(8,128)(2,1)}, u32[]{:S(2)}) %copy-start.4) | copy-done | bytes 528408
  62.9 0.0 copy-start.27
  62.9 0.0 copy-start.31
  62.9 3.4 %table.1 = (s32[200]{0:T(256)S(1)}, s32[1]{0:T(128)}) custom-call(s32[2]{0:T(128)S(1)} %pad_add_fusion.where_ref, s32[4,8]{1,0:T(4,128)} %bitcast.5, bf16[3088,128]{1,0:T(8,128)(2,1)S(1)} %collective-permute-done.3.refs_1_.refs_0_.refs_5_, bf16[2064,128]{1,0:T(8,128)(2,1)S(1)} %copy-done.4, ...), custom_call_target="tpu_custom_call" | custom-call | tf_op jit(solution)/shard_map/table/pallas_call | solution.py:484
  66.4 0.0 collective-permute-done.17.refs_16_.refs_7_
  66.5 8.2 %early.1 = (f32[1024,1024]{1,0:T(8,128)S(1)}, bf16[8,8,128,128]{3,2,1,0:T(8,128)(2,1)S(1)}) custom-call(s32[2]{0:T(128)S(1)} %pad_add_fusion.where_ref, s32[4,8]{1,0:T(4,128)S(1)} %bitcast.6, s32[8,8]{1,0:T(8,128)S(1)} %copy-done.16, s32[200]{0:T(256)S(1)} %get-tuple-element.169.table_ref, s32[4,8]{1,0:T(4,128)S(1)} %copy-done.31, s32[4,8]{1,0:T(4,128)S(1)} %copy-done.22, ...), custom_call_target="tpu_custom_call" | custom-call | flops 4294967296 | bytes 14680064 | tf_op jit(solution)/shard_map/early/pallas_call | solution.py:505
  74.7 1.5 %collective-permute-done.16.refs_3_ = bf16[2304,128]{1,0:T(8,128)(2,1)S(1)} collective-permute-done((bf16[2304,128]{1,0:T(8,128)(2,1)}, bf16[2304,128]{1,0:T(8,128)(2,1)S(1)}, u32[]{:S(2)}, u32[]{:S(2)}) %collective-permute-start.16) | collective-permute-done | bytes 589856 | tf_op jit(solution)/shard_map/pool_outward/ppermute | solution.py:397
  76.2 4.5 %late.1 = bf16[8,8,128,128]{3,2,1,0:T(8,128)(2,1)S(1)} custom-call(s32[2]{0:T(128)S(1)} %pad_add_fusion.where_ref, s32[8,8]{1,0:T(8,128)S(1)} %copy-done.16, s32[200]{0:T(256)S(1)} %get-tuple-element.169.table_ref, s32[4,8]{1,0:T(4,128)S(1)} %copy-done.22, s32[4,8]{1,0:T(4,128)S(1)} %copy-done.19, ...), custom_call_target="tpu_custom_call", output_to_operand_aliasing={{}: (11, {})} | custom-call | bytes 4194304 | tf_op jit(solution)/shard_map/late/pallas_call | solution.py:525
  80.7 0.0 copy-start.8
  80.8 1.3 %copy-done.8 = bf16[8,8,128,128]{3,2,1,0:T(8,128)(2,1)} copy-done((bf16[8,8,128,128]{3,2,1,0:T(8,128)(2,1)}, bf16[8,8,128,128]{3,2,1,0:T(8,128)(2,1)S(1)}, u32[]{:S(2)}) %copy-start.8) | copy-done | bytes 2097176
  82.1 0.6 while.12
  (40 shorter events, 0.1 us)
Async XLA Ops:
  1.8 21.9 %collective-permute-start.3 = (bf16[3088,128]{1,0:T(8,128)(2,1)S(1)}, bf16[3088,128]{1,0:T(8,128)(2,1)S(1)}, u32[]{:S(2)}, u32[]{:S(2)}) collective-permute-start(bf16[3088,128]{1,0:T(8,128)(2,1)S(1)} %get-tuple-element.167), channel_id=1, source_target_pairs={{1,0},{2,3},{5,4},{6,7},{9,8},{10,11},{13,12},{14,15},{17,16},{18,... | collective-permute-start | bytes 2371592 | tf_op jit(solution)/shard_map/lead_outward/ppermute | solution.py:397
  3.1 16.2 %collective-permute-start.6 = (bf16[2064,128]{1,0:T(8,128)(2,1)S(1)}, bf16[2064,128]{1,0:T(8,128)(2,1)S(1)}, u32[]{:S(2)}, u32[]{:S(2)}) collective-permute-start(bf16[2064,128]{1,0:T(8,128)(2,1)S(1)} %get-tuple-element.168), channel_id=1, source_target_pairs={{0,1},{3,2},{4,5},{7,6},{8,9},{11,10},{12,13},{15,14},{16,17},{19,... | collective-permute-start | bytes 1585160 | tf_op jit(solution)/shard_map/head_inward/ppermute | solution.py:400
  8.1 11.9 %collective-permute-start.4 = (bf16[2064,128]{1,0:T(8,128)(2,1)S(1)}, bf16[2064,128]{1,0:T(8,128)(2,1)S(1)}, u32[]{:S(2)}, u32[]{:S(2)}) collective-permute-start(bf16[2064,128]{1,0:T(8,128)(2,1)S(1)} %get-tuple-element.168), channel_id=1, source_target_pairs={{1,2},{2,1},{5,6},{6,5},{9,10},{10,9},{13,14},{14,13},{17,18},{18,... | collective-permute-start | bytes 1585160 | tf_op jit(solution)/shard_map/head_over_middle/ppermute | solution.py:403
  8.8 31.5 %collective-permute-start.15 = (bf16[4,8,128,128]{3,2,1,0:T(8,128)(2,1)}, bf16[4,8,128,128]{3,2,1,0:T(8,128)(2,1)S(1)}, u32[]{:S(2)}, u32[]{:S(2)}) collective-permute-start(bf16[4,8,128,128]{3,2,1,0:T(8,128)(2,1)} %refs_13_.1), channel_id=1, source_target_pairs={{4,0},{16,4},{12,8},{24,12},{20,16},{0,20},{28,24},{8,28},{5,1},{1... | collective-permute-start | bytes 3145736 | tf_op jit(solution)/shard_map/right_odd_up/ppermute | solution.py:409
  10.3 37.2 %collective-permute-start.14 = (bf16[4,8,128,128]{3,2,1,0:T(8,128)(2,1)}, bf16[4,8,128,128]{3,2,1,0:T(8,128)(2,1)}, u32[]{:S(2)}, u32[]{:S(2)}) collective-permute-start(bf16[4,8,128,128]{3,2,1,0:T(8,128)(2,1)} %refs_13_.1), channel_id=1, source_target_pairs={{0,24},{4,28},{8,0},{12,4},{16,8},{20,12},{24,16},{28,20},{1,25},{... | collective-permute-start | bytes 3145736 | tf_op jit(solution)/shard_map/right_two_up/ppermute | solution.py:22
  19.3 18.9 %copy-start = (bf16[2064,128]{1,0:T(8,128)(2,1)}, bf16[2064,128]{1,0:T(8,128)(2,1)S(1)}, u32[]{:S(2)}) copy-start(bf16[2064,128]{1,0:T(8,128)(2,1)S(1)} %collective-permute-done.6.refs_3_.refs_8_) | copy-start | bytes 1585156
  19.4 11.2 %collective-permute-start.7 = (bf16[2064,128]{1,0:T(8,128)(2,1)S(1)}, bf16[2064,128]{1,0:T(8,128)(2,1)S(1)}, u32[]{:S(2)}, u32[]{:S(2)}) collective-permute-start(bf16[2064,128]{1,0:T(8,128)(2,1)S(1)} %collective-permute-done.6.refs_3_.refs_8_), channel_id=1, source_target_pairs={{1,2},{2,1},{5,6},{6,5},{9,10},{10,9},{13,14},{14,13},{17,18},{18,... | collective-permute-start | bytes 1585160 | tf_op jit(solution)/shard_map/end_head_over_middle/ppermute | solution.py:403
  23.7 16.6 %copy-start.30 = (s32[4,8]{1,0:T(4,128)S(1)}, s32[4,8]{1,0:T(4,128)}, u32[]{:S(2)}) copy-start(s32[4,8]{1,0:T(4,128)} %refs_0_.1) | copy-start | bytes 388
  23.7 25.5 %collective-permute-start.5 = (bf16[2064,128]{1,0:T(8,128)(2,1)S(1)}, bf16[2064,128]{1,0:T(8,128)(2,1)S(1)}, u32[]{:S(2)}, u32[]{:S(2)}) collective-permute-start(bf16[2064,128]{1,0:T(8,128)(2,1)S(1)} %passed.2.refs_4_.refs_10_), channel_id=1, source_target_pairs={{1,0},{2,3},{5,4},{6,7},{9,8},{10,11},{13,12},{14,15},{17,16},{18,... | collective-permute-start | bytes 1585160 | tf_op jit(solution)/shard_map/second_head_outward/ppermute | solution.py:397
  25.2 12.3 %collective-permute-start.12 = (bf16[1536,128]{1,0:T(8,128)(2,1)S(1)}, bf16[1536,128]{1,0:T(8,128)(2,1)S(1)}, u32[]{:S(2)}, u32[]{:S(2)}) collective-permute-start(bf16[1536,128]{1,0:T(8,128)(2,1)S(1)} %passed.3), channel_id=1, source_target_pairs={{0,1},{3,2},{4,5},{7,6},{8,9},{11,10},{12,13},{15,14},{16,17},{19,... | collective-permute-start | bytes 1179656 | tf_op jit(solution)/shard_map/tail_inward/ppermute | solution.py:400
  37.5 1.5 %copy-start.6 = (bf16[1536,128]{1,0:T(8,128)(2,1)}, bf16[1536,128]{1,0:T(8,128)(2,1)S(1)}, u32[]{:S(2)}) copy-start(bf16[1536,128]{1,0:T(8,128)(2,1)S(1)} %collective-permute-done.12.more_ref.refs_9_) | copy-start | bytes 1179652
  38.3 18.5 %collective-permute-start.13 = (bf16[2304,128]{1,0:T(8,128)(2,1)S(1)}, bf16[2304,128]{1,0:T(8,128)(2,1)S(1)}, u32[]{:S(2)}, u32[]{:S(2)}) collective-permute-start(bf16[2304,128]{1,0:T(8,128)(2,1)S(1)} %pool.2), channel_id=1, source_target_pairs={{1,2},{2,1},{5,6},{6,5},{9,10},{10,9},{13,14},{14,13},{17,18},{18,... | collective-permute-start | bytes 1769480 | tf_op jit(solution)/shard_map/pool_over_middle/ppermute | solution.py:403
  39.0 17.8 %collective-permute-start.8 = (bf16[2064,128]{1,0:T(8,128)(2,1)S(1)}, bf16[2064,128]{1,0:T(8,128)(2,1)S(1)}, u32[]{:S(2)}, u32[]{:S(2)}) collective-permute-start(bf16[2064,128]{1,0:T(8,128)(2,1)S(1)} %collective-permute-done.7.refs_5_.refs_0_.refs_11_), channel_id=1, source_target_pairs={{1,0},{2,3},{5,4},{6,7},{9,8},{10,11},{13,12},{14,15},{17,16},{18,... | collective-permute-start | bytes 1585160 | tf_op jit(solution)/shard_map/third_head_outward/ppermute | solution.py:397
  40.3 8.7 %collective-permute-start.10 = (s32[4,8]{1,0:T(4,128)S(1)}, s32[4,8]{1,0:T(4,128)S(1)}, u32[]{:S(2)}, u32[]{:S(2)}) collective-permute-start(s32[4,8]{1,0:T(4,128)S(1)} %copy-done.30), channel_id=1, source_target_pairs={{0,24},{4,28},{8,0},{12,4},{16,8},{20,12},{24,16},{28,20},{1,25},{... | collective-permute-start | bytes 392 | tf_op jit(solution)/shard_map/right_masks/ppermute | solution.py:22
  47.5 2.8 %collective-permute-start.9 = (s32[4,8]{1,0:T(4,128)S(1)}, s32[4,8]{1,0:T(4,128)S(1)}, u32[]{:S(2)}, u32[]{:S(2)}) collective-permute-start(s32[4,8]{1,0:T(4,128)S(1)} %copy-done.30), channel_id=1, source_target_pairs={{4,0},{16,4},{12,8},{24,12},{20,16},{0,20},{28,24},{8,28},{5,1},{1... | collective-permute-start | bytes 392 | tf_op jit(solution)/shard_map/right_masks/ppermute | solution.py:409
  49.0 7.8 %copy-start.18 = (s32[4,8]{1,0:T(4,128)}, s32[4,8]{1,0:T(4,128)S(1)}, u32[]{:S(2)}) copy-start(s32[4,8]{1,0:T(4,128)S(1)} %collective-permute-done.10.refs_6_.refs_2_.refs_1_) | copy-start | bytes 388
  49.0 1.3 %collective-permute-start.11 = (s32[4,8]{1,0:T(4,128)S(1)}, s32[4,8]{1,0:T(4,128)S(1)}, u32[]{:S(2)}, u32[]{:S(2)}) collective-permute-start(s32[4,8]{1,0:T(4,128)S(1)} %collective-permute-done.10.refs_6_.refs_2_.refs_1_), channel_id=1, source_target_pairs={{0,4},{4,0},{8,12},{12,8},{16,20},{20,16},{24,28},{28,24},{1,5},{5... | collective-permute-start | bytes 392 | tf_op jit(solution)/shard_map/right_masks/ppermute | solution.py:412
  49.2 0.8 copy-start.3
  50.3 9.0 %copy-start.21 = (s32[4,8]{1,0:T(4,128)}, s32[4,8]{1,0:T(4,128)S(1)}, u32[]{:S(2)}) copy-start(s32[4,8]{1,0:T(4,128)S(1)} %collective-permute-done.9.refs_5_.refs_1_.refs_0_) | copy-start | bytes 388
  50.4 10.3 %copy-start.24 = (s32[4,8]{1,0:T(4,128)}, s32[4,8]{1,0:T(4,128)S(1)}, u32[]{:S(2)}) copy-start(s32[4,8]{1,0:T(4,128)S(1)} %collective-permute-done.11.refs_7_.refs_3_.refs_2_) | copy-start | bytes 388
  58.4 1.0 %copy-start.10 = (bf16[4,8,128,128]{3,2,1,0:T(8,128)(2,1)}, bf16[4,8,128,128]{3,2,1,0:T(8,128)(2,1)S(1)}, u32[]{:S(2)}) copy-start(bf16[4,8,128,128]{3,2,1,0:T(8,128)(2,1)S(1)} %get-tuple-element.300.refs_14_.refs_5_) | copy-start | bytes 3145732
  58.4 8.0 %collective-permute-start.17 = (bf16[4,8,128,128]{3,2,1,0:T(8,128)(2,1)}, bf16[4,8,128,128]{3,2,1,0:T(8,128)(2,1)}, u32[]{:S(2)}, u32[]{:S(2)}) collective-permute-start(bf16[4,8,128,128]{3,2,1,0:T(8,128)(2,1)} %get-tuple-element.302.refs_15_.refs_6_), channel_id=1, source_target_pairs={{0,4},{4,0},{8,12},{12,8},{16,20},{20,16},{24,28},{28,24},{1,5},{5... | collective-permute-start | bytes 3145736 | tf_op jit(solution)/shard_map/right_core_swap/ppermute | solution.py:412
  59.4 16.8 %collective-permute-start.16 = (bf16[2304,128]{1,0:T(8,128)(2,1)}, bf16[2304,128]{1,0:T(8,128)(2,1)S(1)}, u32[]{:S(2)}, u32[]{:S(2)}) collective-permute-start(bf16[2304,128]{1,0:T(8,128)(2,1)} %get-tuple-element.173), channel_id=1, source_target_pairs={{1,0},{2,3},{5,4},{6,7},{9,8},{10,11},{13,12},{14,15},{17,16},{18,... | collective-permute-start | bytes 1769480 | tf_op jit(solution)/shard_map/pool_outward/ppermute | solution.py:397
  60.7 5.7 %copy-start.16 = (s32[8,8]{1,0:T(8,128)S(1)}, s32[8,8]{1,0:T(8,128)}, u32[]{:S(2)}) copy-start(s32[8,8]{1,0:T(8,128)} %c_ref.3) | copy-start | bytes 772
  60.8 1.0 %copy-start.1 = (bf16[2064,128]{1,0:T(8,128)(2,1)S(1)}, bf16[2064,128]{1,0:T(8,128)(2,1)}, u32[]{:S(2)}) copy-start(bf16[2064,128]{1,0:T(8,128)(2,1)} %copy-done) | copy-start | bytes 1585156
  61.8 1.0 %copy-start.4 = (bf16[2064,128]{1,0:T(8,128)(2,1)S(1)}, bf16[2064,128]{1,0:T(8,128)(2,1)}, u32[]{:S(2)}) copy-start(bf16[2064,128]{1,0:T(8,128)(2,1)} %copy-done.3) | copy-start | bytes 1585156
  62.9 3.5 %copy-start.2 = (bf16[2064,128]{1,0:T(8,128)(2,1)S(1)}, bf16[2064,128]{1,0:T(8,128)(2,1)}, u32[]{:S(2)}) copy-start(bf16[2064,128]{1,0:T(8,128)(2,1)} %copy-done) | copy-start | bytes 1585156
  62.9 3.5 %copy-start.5 = (bf16[2064,128]{1,0:T(8,128)(2,1)S(1)}, bf16[2064,128]{1,0:T(8,128)(2,1)}, u32[]{:S(2)}) copy-start(bf16[2064,128]{1,0:T(8,128)(2,1)} %copy-done.3) | copy-start | bytes 1585156
  62.9 3.5 %copy-start.7 = (bf16[1536,128]{1,0:T(8,128)(2,1)S(1)}, bf16[1536,128]{1,0:T(8,128)(2,1)}, u32[]{:S(2)}) copy-start(bf16[1536,128]{1,0:T(8,128)(2,1)} %copy-done.6) | copy-start | bytes 1179652
  62.9 3.6 %copy-start.11 = (bf16[4,8,128,128]{3,2,1,0:T(8,128)(2,1)S(1)}, bf16[4,8,128,128]{3,2,1,0:T(8,128)(2,1)}, u32[]{:S(2)}) copy-start(bf16[4,8,128,128]{3,2,1,0:T(8,128)(2,1)} %copy-done.10) | copy-start | bytes 3145732
  62.9 3.6 %copy-start.19 = (s32[4,8]{1,0:T(4,128)S(1)}, s32[4,8]{1,0:T(4,128)}, u32[]{:S(2)}) copy-start(s32[4,8]{1,0:T(4,128)} %copy-done.18) | copy-start | bytes 388
  62.9 3.6 %copy-start.22 = (s32[4,8]{1,0:T(4,128)S(1)}, s32[4,8]{1,0:T(4,128)}, u32[]{:S(2)}) copy-start(s32[4,8]{1,0:T(4,128)} %copy-done.21) | copy-start | bytes 388
  62.9 3.6 %copy-start.25 = (s32[4,8]{1,0:T(4,128)S(1)}, s32[4,8]{1,0:T(4,128)}, u32[]{:S(2)}) copy-start(s32[4,8]{1,0:T(4,128)} %copy-done.24) | copy-start | bytes 388
  62.9 3.6 %copy-start.27 = (s32[8,4]{0,1:T(4,128)S(1)}, s32[8,4]{0,1:T(4,128)}, u32[]{:S(2)}) copy-start(s32[8,4]{0,1:T(4,128)} %param.8) | copy-start | bytes 388
  62.9 3.6 %copy-start.31 = (s32[4,8]{1,0:T(4,128)S(1)}, s32[4,8]{1,0:T(4,128)}, u32[]{:S(2)}) copy-start(s32[4,8]{1,0:T(4,128)} %refs_0_.1) | copy-start | bytes 388
  76.2 5.9 %copy-start.13 = (bf16[8,4,128,128]{3,2,1,0:T(8,128)(2,1)S(1)}, bf16[8,4,128,128]{3,2,1,0:T(8,128)(2,1)}, u32[]{:S(2)}) copy-start(bf16[8,4,128,128]{3,2,1,0:T(8,128)(2,1)} %refs_4_.1) | copy-start | bytes 3145732
  76.2 5.9 %copy-start.28 = (s32[8,4]{0,1:T(4,128)S(1)}, s32[8,4]{0,1:T(4,128)}, u32[]{:S(2)}) copy-start(s32[8,4]{0,1:T(4,128)} %param.8) | copy-start | bytes 388
  80.7 1.3 %copy-start.8 = (bf16[8,8,128,128]{3,2,1,0:T(8,128)(2,1)}, bf16[8,8,128,128]{3,2,1,0:T(8,128)(2,1)S(1)}, u32[]{:S(2)}) copy-start(bf16[8,8,128,128]{3,2,1,0:T(8,128)(2,1)S(1)} %late.1) | copy-start | bytes 6291460

commit v4 on v3

--- a/solution.py
+++ b/solution.py
@@ -8,7 +8,7 @@
 from jax.sharding import PartitionSpec as P
 
 STEPS = 4
-T_SECOND, T_RIGHT = 5, 0
+T_TAIL, T_SECOND, T_RIGHT = 7, 5, 2
 NOTE = 16
 MIB = 1024 * 1024
 
@@ -32,10 +32,6 @@
 
 def anywhere():
     return pl.BlockSpec(memory_space=pl.ANY)
-
-
-def in_hbm():
-    return pl.BlockSpec(memory_space=pltpu.HBM)
 
 
 def params(mib=8):
@@ -78,17 +74,17 @@
     )(*seen)
 
 
-def passed(x, seen):
+def passed(arrays, seen=()):
     return pl.pallas_call(
         lambda *refs: None,
-        in_specs=[anywhere()] * (1 + len(seen)),
-        out_specs=anywhere(),
-        out_shape=jax.ShapeDtypeStruct(x.shape, x.dtype),
-        input_output_aliases={0: 0},
+        in_specs=[anywhere()] * (len(arrays) + len(seen)),
+        out_specs=[anywhere()] * len(arrays),
+        out_shape=[jax.ShapeDtypeStruct(x.shape, x.dtype) for x in arrays],
+        input_output_aliases={x: x for x in range(len(arrays))},
         compiler_params=params(),
         cost_estimate=cost(0, 0),
         name="passed",
-    )(x, *seen)
+    )(*arrays, *seen)
 
 
 def live_kernel(by_column, mask_ref, x_ref, *refs):
@@ -133,29 +129,31 @@
         + [pl.BlockSpec((kb, wide_j, blk, blk), lambda g: (0, g, 0, 0))] * STEPS,
         out_specs=pl.BlockSpec((br * blk, wide_j * blk), lambda g: (0, g)),
         out_shape=jax.ShapeDtypeStruct((br * blk, bc * blk), jnp.float32),
-        compiler_params=params(32),
+        compiler_params=params(20),
         cost_estimate=cost(2 * STEPS * br * bc * kb * blk**3, 12 << 20),
         name="dense",
     )(*left, *right)
 
 
-def filter_kernel(c_ref, acc_ref, out_ref):
+def filter_kernel(c_ref, acc_ref, *refs):
+    out_ref = refs[-1]
     blk = out_ref.shape[-1]
     for j in range(out_ref.shape[1]):
         out_ref[0, j] = filtered(c_ref, pl.program_id(0), j, acc_ref[:, j * blk : (j + 1) * blk])
 
 
-def filter_sum(total, c_mask, blk):
+def filter_sum(total, c_mask, blk, *into):
     br, bc = c_mask.shape
     return pl.pallas_call(
         filter_kernel,
         grid=(br,),
-        in_specs=[smem(), pl.BlockSpec((blk, bc * blk), lambda g: (g, 0))],
+        in_specs=[smem(), pl.BlockSpec((blk, bc * blk), lambda g: (g, 0))] + [anywhere()] * len(into),
         out_specs=pl.BlockSpec((1, bc, blk, blk), lambda g: (g, 0, 0, 0)),
         out_shape=jax.ShapeDtypeStruct((br, bc, blk, blk), jnp.bfloat16),
+        input_output_aliases={2: 0} if into else {},
         compiler_params=params(),
         name="filter",
-    )(c_mask, total)
+    )(c_mask, total, *into)
 
 
 def dense_product(a_blocks, a_mask, b_blocks, b_mask, c_mask):
@@ -167,7 +165,7 @@
     return filter_sum(dense_sum(left, right), c_mask, a_blocks.shape[-1])
 
 
-def compact_kernel(mask_ref, a_ref, lead_ref, head_ref, inner_ref, tail_ref, n_ref, list_ref):
+def compact_kernel(mask_ref, a_ref, head_ref, inner_ref, tail_ref, n_ref, list_ref):
     br, kb, blk = a_ref.shape[:3]
     head, lead, inner, _ = slots(br * kb)
     lanes = lax.broadcasted_iota(jnp.int32, (NOTE, blk), 1)
@@ -179,13 +177,19 @@
             note = jnp.where(lanes == k * br + i, mask_ref[k, i], note)
             count = count + mask_ref[k, i]
     note = note.astype(jnp.float32).astype(jnp.bfloat16)
-    lead_ref[0 : lead * blk, :] = list_ref[0 : lead * blk, :]
-    lead_ref[lead * blk :, :] = note
     head_ref[0 : head * blk, :] = list_ref[0 : head * blk, :]
     head_ref[head * blk :, :] = note
     inner_ref[...] = list_ref[head * blk : (head + inner) * blk, :]
     tail_ref[...] = list_ref[head * blk :, :]
     n_ref[0] = count
+
+
+def extend_kernel(head_ref, tail_ref, out_ref):
+    size = head_ref.shape[0] - NOTE
+    more = out_ref.shape[0] - head_ref.shape[0]
+    out_ref[0:size, :] = head_ref[0:size, :]
+    out_ref[size : size + more, :] = tail_ref[0:more, :]
+    out_ref[size + more :, :] = head_ref[size:, :]
 
 
 def pool_kernel(skip, n_ref, tail_ref, more_ref, *refs):
@@ -200,7 +204,7 @@
 
 
 def table_kernel(blocks, where_ref, own_ref, *refs):
-    notes, (table_ref, over_ref, note_ref, wide_ref, mask_ref, sems, sem) = refs[:6], refs[6:]
+    notes, (table_ref, over_ref, note_ref, wide_ref, mask_ref, sems, sem) = refs[:5], refs[5:]
     copies = [
         pltpu.make_async_copy(
             ref.at[pl.ds(ref.shape[0] - NOTE, NOTE), :], note_ref.at[pl.ds(m * NOTE, NOTE), :], sems.at[m]
@@ -227,10 +231,11 @@
         return jnp.where(flip, 4 - step, step)
 
     def fill(base, place, m):
-        count = jnp.int32(base)
-        for b in range(blocks):
+        def body(b, count):
             table_ref[count] = place * blocks + b
-            count = count + mask_ref[m * NOTE, b]
+            return count + mask_ref[m * NOTE, b]
+
+        count = lax.fori_loop(0, blocks, body, jnp.int32(base), unroll=8)
 
         def pad(p, carry):
             table_ref[p] = none
@@ -239,9 +244,9 @@
         lax.fori_loop(count, base + blocks, pad, 0)
         return count - base
 
-    first = fill(0, place_of(near), jnp.where(at_end, 0, 3))
-    second = fill(apart, jnp.where(at_end, 2, place_of(4 - near)), jnp.where(at_end, 1, 4))
-    third = fill(2 * apart, jnp.where(at_end, place_of(4 - near), 2), jnp.where(at_end, 2, 5))
+    first = fill(0, place_of(near), 0)
+    second = fill(apart, jnp.where(at_end, 2, place_of(4 - near)), jnp.where(at_end, 1, 3))
+    third = fill(2 * apart, jnp.where(at_end, place_of(4 - near), 2), jnp.where(at_end, 2, 4))
 
     def append(base, begin, length, at):
         def body(p, at):
@@ -288,7 +293,8 @@
 
 def early_kernel(where_ref, mask_ref, c_ref, table_ref, *refs):
     b_masks, a_ref, refs = refs[:STEPS], refs[STEPS], refs[STEPS + 1 :]
-    outs, mids, b_refs, (acc_ref, out_ref, left_ref) = refs[:3], refs[3:8], refs[8:12], refs[12:]
+    near_ref, outs, mids, refs = refs[0], refs[1:3], refs[3:7], refs[7:]
+    b_refs, (acc_ref, out_ref, left_ref) = refs[:STEPS], refs[STEPS:]
     br, kb, blk, _ = a_ref.shape
     blocks = br * kb
     apart = blocks + 8
@@ -296,12 +302,15 @@
     z = where_ref[0]
     at_end = jnp.logical_or(z == 0, z == 3)
 
-    def scatter(ref, first, length):
-        for b in range(length):
+    def scatter(ref, first, length, at=0):
+        def body(b, carry):
             place = table_ref[first + b]
             row = pl.multiple_of((place % br) * blk, blk)
             column = pl.multiple_of((place // br) * blk, blk)
-            left_ref[pl.ds(row, blk), pl.ds(column, blk)] = ref[b * blk : (b + 1) * blk, :]
+            left_ref[pl.ds(row, blk), pl.ds(column, blk)] = ref[pl.ds(pl.multiple_of((at + b) * blk, blk), blk), :]
+            return carry
+
+        lax.fori_loop(0, length, body, 0, unroll=2)
 
     @pl.when(pl.program_id(0) == 0)
     def _():
@@ -311,20 +320,20 @@
                     jnp.float32
                 ).astype(jnp.bfloat16)
         left_ref[:, kb * blk :] = jnp.zeros((br * blk, left_ref.shape[1] - kb * blk), jnp.bfloat16)
+        scatter(near_ref, 0, head)
 
         @pl.when(at_end)
         def _():
-            scatter(outs[0], 0, lead)
-            scatter(outs[1], apart, head)
-            scatter(outs[2], 2 * apart, head)
+            scatter(outs[0], apart, head)
+            scatter(outs[0], head, lead - head, head)
+            scatter(outs[1], 2 * apart, head)
 
         @pl.when(jnp.logical_not(at_end))
         def _():
-            scatter(mids[0], 0, head)
-            scatter(mids[1], head, inner)
-            scatter(mids[2], apart, head)
-            scatter(mids[3], 2 * apart, head)
-            scatter(mids[4], 3 * apart, pool)
+            scatter(mids[0], head, inner)
+            scatter(mids[1], apart, head)
+            scatter(mids[2], 2 * apart, head)
+            scatter(mids[3], 3 * apart, pool)
 
     j0 = pl.program_id(0) * out_ref.shape[1]
     total = None
@@ -344,44 +353,57 @@
 def late_kernel(where_ref, c_ref, table_ref, *refs):
     b_masks, refs = refs[: STEPS - 1], refs[STEPS - 1 :]
     late_ref, acc_ref, b_refs, refs = refs[0], refs[1], refs[2 : 1 + STEPS], refs[2 + STEPS :]
-    out_ref, row_ref, sems = refs
+    out_ref, row_ref, touched_ref, sems = refs
     br, bc, blk, _ = out_ref.shape
     kb = b_refs[0].shape[0]
-    none = STEPS * kb * br
     _, _, _, pool = slots(kb * br)
     first = 3 * (kb * br + 8)
     at_end = jnp.logical_or(where_ref[0] == 0, where_ref[0] == 3)
-    places = [jnp.where(at_end, table_ref[first + b], none) for b in range(pool)]
-
-    for b, place in enumerate(places):
+
+    def clear(i, carry):
+        touched_ref[i] = 0
+        return carry
+
+    def add(b, carry):
+        place = table_ref[first + b]
         for slab, (b_ref, mask_ref) in enumerate(zip(b_refs, b_masks)):
 
             @pl.when(place // (kb * br) == slab + 1)
             def _():
-                row, k = pl.multiple_of((place % br) * blk, blk), (place // br) % kb
+                i, k = place % br, (place // br) % kb
+                touched_ref[i] = 1
                 keep = [mask_ref[k, j].astype(jnp.float32).astype(jnp.bfloat16) for j in range(bc)]
                 columns = jnp.concatenate([b_ref[k, j] * keep[j] for j in range(bc)], axis=1)
-                acc_ref[pl.ds(row, blk), :] += jnp.dot(
-                    late_ref[b * blk : (b + 1) * blk, :], columns, preferred_element_type=jnp.float32
+                acc_ref[pl.ds(pl.multiple_of(i * blk, blk), blk), :] += jnp.dot(
+                    late_ref[pl.ds(pl.multiple_of(b * blk, blk), blk), :], columns, preferred_element_type=jnp.float32
                 )
 
-    go = [pltpu.make_async_copy(row_ref.at[i], out_ref.at[i], sems.at[i]) for i in range(br)]
-    touched = [
-        functools.reduce(jnp.logical_or, [jnp.logical_and(p < none, p % br == i) for p in places]) for i in range(br)
-    ]
-    for i in range(br):
-
-        @pl.when(touched[i])
+        return carry
+
+    def go(i):
+        return pltpu.make_async_copy(row_ref.at[i], out_ref.at[i], sems.at[i])
+
+    def send(i, carry):
+        @pl.when(touched_ref[i] > 0)
         def _():
+            row = pl.multiple_of(i * blk, blk)
             for j in range(bc):
-                row_ref[i, j] = filtered(c_ref, i, j, acc_ref[i * blk : (i + 1) * blk, j * blk : (j + 1) * blk])
-            go[i].start()
-
-    for i in range(br):
-
-        @pl.when(touched[i])
+                row_ref[i, j] = filtered(c_ref, i, j, acc_ref[pl.ds(row, blk), j * blk : (j + 1) * blk])
+            go(i).start()
+
+        return carry
+
+    def settle(i, carry):
+        @pl.when(touched_ref[i] > 0)
         def _():
-            go[i].wait()
+            go(i).wait()
+
+        return carry
+
+    lax.fori_loop(0, br, clear, 0)
+    lax.fori_loop(0, jnp.where(at_end, pool, 0), add, 0)
+    lax.fori_loop(0, br, send, 0)
+    lax.fori_loop(0, br, settle, 0)
 
 
 def sparse_product(a_blocks, a_mask, b_blocks, b_mask, c_mask):
@@ -396,6 +418,9 @@
     def outward(x):
         return lax.ppermute(x, "col", [(1, 0), (2, 3)])
 
+    def end_swap(x):
+        return lax.ppermute(x, "col", [(0, 1), (1, 0), (2, 3), (3, 2)])
+
     def inward(x):
         return lax.ppermute(x, "col", [(0, 1), (3, 2)])
 
@@ -422,12 +447,11 @@
         second_mask, odd_mask = two_up(b_mask), odd_up(b_mask)
         b_masks = [b_mask, odd_mask, second_mask, core_swap(second_mask)]
 
-    own_lead, own_head, own_inner, own_tail, n = pl.pallas_call(
+    own_head, own_inner, own_tail, n = pl.pallas_call(
         compact_kernel,
         in_specs=[smem(), whole()],
-        out_specs=[whole(), whole(), whole(), whole(), smem()],
+        out_specs=[whole(), whole(), whole(), smem()],
         out_shape=[
-            listed(lead, NOTE),
             listed(head, NOTE),
             listed(inner),
             listed(blocks - head),
@@ -454,28 +478,34 @@
         )(n, own_tail, more, *gate, *seen)
         return outs[-1], outs[:-1]
 
-    with jax.named_scope("lead_outward"):
-        near_lead = outward(own_lead)
-    with jax.named_scope("head_inward"):
-        near_head = inward(own_head)
     with jax.named_scope("head_over_middle"):
         mid_head = over_middle(own_head)
+    with jax.named_scope("head_end_swap"):
+        near_head = end_swap(own_head)
+    with jax.named_scope("tail_inward"):
+        near_tail = inward(own_inner)
+    near_head, mid_head = passed([near_head, mid_head])
     with jax.named_scope("second_head_outward"):
-        mid_head = passed(mid_head, [near_lead])
-        second_head = outward(mid_head)
-    with jax.named_scope("tail_inward"):
-        near_tail = inward(passed(own_inner, [near_lead]))
+        second_head = outward(
+            pl.pallas_call(
+                extend_kernel,
+                in_specs=[whole()] * 2,
+                out_specs=whole(),
+                out_shape=listed(lead, NOTE),
+                compiler_params=params(),
+                cost_estimate=cost(0, 0),
+                name="extend",
+            )(mid_head, own_tail)
+        )
     with jax.named_scope("end_head_over_middle"):
         end_head = over_middle(near_head)
     with jax.named_scope("third_head_outward"):
         third_head = outward(end_head)
-    mid_pool, _ = pooled(head, near_tail, [], [end_head])
+    mid_pool, _ = pooled(head, near_tail, [], [end_head, token([near_tail], T_TAIL)])
     with jax.named_scope("pool_over_middle"):
         mid_pool = over_middle(mid_pool)
-    slabs_here = token([second, odd_one], T_RIGHT)
-    out_pool, (second, odd_one) = pooled(
-        lead, mid_pool, [second, odd_one], [token([second_head], T_SECOND), slabs_here, third_head] + b_masks[1:]
-    )
+    here = [token([second_head], T_SECOND), third_head, token([second], T_RIGHT), odd_one] + b_masks[1:]
+    out_pool, (second,) = pooled(lead, mid_pool, [second], here)
     with jax.named_scope("pool_outward"):
         out_pool = outward(out_pool)
     with jax.named_scope("right_core_swap"):
@@ -483,25 +513,25 @@
 
     table, over = pl.pallas_call(
         functools.partial(table_kernel, blocks),
-        in_specs=[smem(), smem()] + [anywhere()] * 6,
+        in_specs=[smem(), smem()] + [anywhere()] * 5,
         out_specs=[smem(), smem()],
         out_shape=[jax.ShapeDtypeStruct((5 * (blocks + 8),), jnp.int32), jax.ShapeDtypeStruct((1,), jnp.int32)],
         scratch_shapes=[
-            pltpu.VMEM((6 * NOTE, blk), jnp.bfloat16),
-            pltpu.VMEM((6 * NOTE, blk), jnp.int32),
-            pltpu.SMEM((6 * NOTE, blk), jnp.int32),
-            pltpu.SemaphoreType.DMA((6,)),
+            pltpu.VMEM((5 * NOTE, blk), jnp.bfloat16),
+            pltpu.VMEM((5 * NOTE, blk), jnp.int32),
+            pltpu.SMEM((5 * NOTE, blk), jnp.int32),
+            pltpu.SemaphoreType.DMA((5,)),
             pltpu.SemaphoreType.DMA,
         ],
         compiler_params=params(),
         name="table",
-    )(where, by_column, near_lead, second_head, third_head, near_head, mid_head, end_head)
+    )(where, by_column, near_head, second_head, third_head, mid_head, end_head)
 
     def fixed(x):
         return pl.BlockSpec(x.shape, lambda g: (0,) * x.ndim)
 
     wide_j = 2 if bc % 2 == 0 else 1
-    arrived = [near_lead, second_head, third_head, near_head, near_tail, mid_head, end_head, mid_pool]
+    arrived = [near_head, second_head, third_head, near_tail, mid_head, end_head, mid_pool]
     acc, out = pl.pallas_call(
         early_kernel,
         grid=(bc // wide_j,),
@@ -517,19 +547,23 @@
             jax.ShapeDtypeStruct((br, bc, blk, blk), jnp.bfloat16),
         ],
         scratch_shapes=[pltpu.VMEM((br * blk, (STEPS * kb + 1) * blk), a_blocks.dtype)],
-        compiler_params=params(32),
+        compiler_params=params(24),
         cost_estimate=cost(2 * STEPS * br * bc * kb * blk**3, 14 << 20),
         name="early",
     )(where, by_column, c_mask, table, *b_masks, a_blocks, *arrived, *right)
 
     out = pl.pallas_call(
         late_kernel,
-        in_specs=[smem()] * (3 + STEPS - 1) + [whole()] * (1 + STEPS) + [in_hbm()],
-        out_specs=in_hbm(),
+        in_specs=[smem()] * (3 + STEPS - 1) + [whole()] * (1 + STEPS) + [anywhere()],
+        out_specs=anywhere(),
         out_shape=jax.ShapeDtypeStruct((br, bc, blk, blk), jnp.bfloat16),
-        scratch_shapes=[pltpu.VMEM((br, bc, blk, blk), jnp.bfloat16), pltpu.SemaphoreType.DMA((br,))],
+        scratch_shapes=[
+            pltpu.VMEM((br, bc, blk, blk), jnp.bfloat16),
+            pltpu.SMEM((br,), jnp.int32),
+            pltpu.SemaphoreType.DMA((br,)),
+        ],
         input_output_aliases={3 + STEPS - 1 + 1 + STEPS: 0},
-        compiler_params=params(24),
+        compiler_params=params(12),
         cost_estimate=cost(0, 4 << 20),
         name="late",
     )(where, c_mask, table, *b_masks[1:], out_pool, acc, *right[1:], out)
@@ -542,7 +576,7 @@
         odd = lax.axis_index("row") % 2 == 1
         held = [live(slab, mask, after=(before,)) for slab, mask in zip(right, b_masks)]
         ordered = [held[0], jnp.where(odd, held[3], held[1]), held[2], jnp.where(odd, held[1], held[3])]
-        return filter_sum(dense_sum(left, ordered), c_mask, blk), trips - 1
+        return filter_sum(dense_sum(left, ordered), c_mask, blk, before), trips - 1
 
     out, _ = lax.while_loop(lambda state: state[1] > 0, again, (out, over[0]))
     return out

time: 83.8 us -> 79.3 us (0.946)
  waiting for transfers between devices: 25.8 us -> 37.7 us
  starting transfers between devices: 30.2 us -> 18.8 us
  local copies, waits for them, and re-layouts: 5.27 us -> 1.35 us
    ppermute x2 -> x1, waiting for transfers between devices: 13.8 us -> 4.9 us  [inward(): return lax.ppermute(x, 'col', [(0, 1), (3, 2)])]
    ppermute x4 -> x3, waiting for transfers between devices: 11.7 us -> 20.3 us  [outward(): return lax.ppermute(x, 'col', [(1, 0), (2, 3)])]
    ppermute x2 -> x1, starting transfers between devices: 10.4 us -> 1.94 us  [inward(): return lax.ppermute(x, 'col', [(0, 1), (3, 2)])]
    ppermute x0 -> x1, waiting for transfers between devices: none -> 8 us  [end_swap(): return lax.ppermute(x, 'col', [(0, 1), (1, 0), (2, 3), (3, 2)])]
    ppermute x0 -> x1, starting transfers between devices: none -> 5.88 us  [end_swap(): return lax.ppermute(x, 'col', [(0, 1), (1, 0), (2, 3), (3, 2)])]
    ppermute x2, starting transfers between devices: 9.29 us -> 4.95 us  [from_behind(): lax.ppermute(array, axis, [(i, (i + by) % size) for i in range(size)])]
    unnamed x46 -> x22, local copies, waits for them, and re-layouts: 5.27 us -> 1.35 us
    ppermute x2, waiting for transfers between devices: 0.01 us -> 3.37 us  [from_behind(): lax.ppermute(array, axis, [(i, (i + by) % size) for i in range(size)])]
  transfers between devices with their start and end apart: 15 -> 14, of which waited for: 6 -> 7; matrix products, arithmetic and copies ran while one was open for 0% -> 0% of each run, Pallas kernels for 15% -> 16%
where the time goes in v4:
time: 79.3 us; the launch traced here: 78.9 us
  waiting for transfers between devices  37.7 us (48%)
  Pallas kernels  20 us (25%)
  starting transfers between devices  18.8 us (24%)
  local copies, waits for them, and re-layouts  1.35 us (2%)
    ppermute x3, waiting for transfers between devices, outward(): return lax.ppermute(x, 'col', [(1, 0), (2, 3)])  20.3 us
    pallas_call x1, Pallas kernels, sparse_product(): pl.pallas_call(early_kernel, grid=(bc // wide_j,), in_specs=[smem()] * (4...  8.47 us
    ppermute x1, waiting for transfers between devices, end_swap(): return lax.ppermute(x, 'col', [(0, 1), (1, 0), (2, 3), (3, 2)])  8 us
    ppermute x1, starting transfers between devices, end_swap(): return lax.ppermute(x, 'col', [(0, 1), (1, 0), (2, 3), (3, 2)])  5.88 us
    ppermute x2, starting transfers between devices, from_behind(): lax.ppermute(array, axis, [(i, (i + by) % size) for i in range(size)])  4.95 us
    ppermute x1, waiting for transfers between devices, inward(): return lax.ppermute(x, 'col', [(0, 1), (3, 2)])  4.9 us
    pallas_call x1, Pallas kernels, sparse_product(): pl.pallas_call(late_kernel, in_specs=[smem()] * (3 + STEPS - 1) + [whole(...  4.25 us
    ppermute x3, starting transfers between devices, outward(): return lax.ppermute(x, 'col', [(1, 0), (2, 3)])  3.86 us
  transfers between devices with their start and end apart: 14, of which 7 were waited for; matrix products, arithmetic and copies ran while one was open for 0% of the time, Pallas kernels for 16%

profile of v4, /device:TPU:0, one launch (start us, length us, event | category | flops | bytes accessed | tf_op | source)
XLA Modules:
  0.0 78.9 jit_solution(6254209240820927321)
XLA Ops:
  0.0 1.8 %compact.1 = (bf16[2064,128]{1,0:T(8,128)(2,1)S(1)}, bf16[1536,128]{1,0:T(8,128)(2,1)S(1)}, bf16[2048,128]{1,0:T(8,128)(2,1)S(1)}, s32[1]{0:T(128)}) custom-call(s32[4,8]{1,0:T(4,128)} %bitcast.4, bf16[8,4,128,128]{3,2,1,0:T(8,128)(2,1)} %refs_4_.1), custom_call_target="tpu_custom_call" | custom-call | bytes 3145728 | tf_op jit(solution)/shard_map/compact/pallas_call | solution.py:450
  1.8 0.7 collective-permute-start.4
  2.5 5.9 %collective-permute-start.3 = (bf16[2064,128]{1,0:T(8,128)(2,1)S(1)}, bf16[2064,128]{1,0:T(8,128)(2,1)S(1)}, u32[]{:S(2)}, u32[]{:S(2)}) collective-permute-start(bf16[2064,128]{1,0:T(8,128)(2,1)S(1)} %get-tuple-element.167), channel_id=1, source_target_pairs={{0,1},{1,0},{2,3},{3,2},{4,5},{5,4},{6,7},{7,6},{8,9},{9,8},{10,11... | collective-permute-start | bytes 1585160 | tf_op jit(solution)/shard_map/head_end_swap/ppermute | solution.py:422
  8.4 1.9 %collective-permute-start.11 = (bf16[1536,128]{1,0:T(8,128)(2,1)S(1)}, bf16[1536,128]{1,0:T(8,128)(2,1)S(1)}, u32[]{:S(2)}, u32[]{:S(2)}) collective-permute-start(bf16[1536,128]{1,0:T(8,128)(2,1)S(1)} %get-tuple-element.173), channel_id=1, source_target_pairs={{0,1},{3,2},{4,5},{7,6},{8,9},{11,10},{12,13},{15,14},{16,17},{19,... | collective-permute-start | bytes 1179656 | tf_op jit(solution)/shard_map/tail_inward/ppermute | solution.py:425
  10.3 2.5 %collective-permute-start.13 = (bf16[4,8,128,128]{3,2,1,0:T(8,128)(2,1)}, bf16[4,8,128,128]{3,2,1,0:T(8,128)(2,1)}, u32[]{:S(2)}, u32[]{:S(2)}) collective-permute-start(bf16[4,8,128,128]{3,2,1,0:T(8,128)(2,1)} %refs_12_.1), channel_id=1, source_target_pairs={{0,24},{4,28},{8,0},{12,4},{16,8},{20,12},{24,16},{28,20},{1,25},{... | collective-permute-start | bytes 3145736 | tf_op jit(solution)/shard_map/right_two_up/ppermute | solution.py:22
  12.8 0.0 collective-permute-start.14
  12.9 0.0 collective-permute-done.4.refs_1_
  12.9 8.0 %collective-permute-done.3.refs_0_ = bf16[2064,128]{1,0:T(8,128)(2,1)S(1)} collective-permute-done((bf16[2064,128]{1,0:T(8,128)(2,1)S(1)}, bf16[2064,128]{1,0:T(8,128)(2,1)S(1)}, u32[]{:S(2)}, u32[]{:S(2)}) %collective-permute-start.3) | collective-permute-done | bytes 528416 | tf_op jit(solution)/shard_map/head_end_swap/ppermute | solution.py:422
  20.9 0.7 collective-permute-start.6
  21.5 0.1 extend.1
  21.6 0.0 copy-start.15
  21.6 1.3 %collective-permute-start.5 = (bf16[3088,128]{1,0:T(8,128)(2,1)S(1)}, bf16[3088,128]{1,0:T(8,128)(2,1)S(1)}, u32[]{:S(2)}, u32[]{:S(2)}) collective-permute-start(bf16[3088,128]{1,0:T(8,128)(2,1)S(1)} %extend.1), channel_id=1, source_target_pairs={{1,0},{2,3},{5,4},{6,7},{9,8},{10,11},{13,12},{14,15},{17,16},{18,... | collective-permute-start | bytes 2371592 | tf_op jit(solution)/shard_map/second_head_outward/ppermute | solution.py:419
  22.9 4.9 %collective-permute-done.11.refs_0_.more_ref.refs_8_ = bf16[1536,128]{1,0:T(8,128)(2,1)S(1)} collective-permute-done((bf16[1536,128]{1,0:T(8,128)(2,1)S(1)}, bf16[1536,128]{1,0:T(8,128)(2,1)S(1)}, u32[]{:S(2)}, u32[]{:S(2)}) %collective-permute-start.11) | collective-permute-done | bytes 393248 | tf_op jit(solution)/shard_map/tail_inward/ppermute | solution.py:425
  27.8 0.0 copy-done.15
  27.8 2.4 %collective-permute-start.9 = (s32[4,8]{1,0:T(4,128)S(1)}, s32[4,8]{1,0:T(4,128)S(1)}, u32[]{:S(2)}, u32[]{:S(2)}) collective-permute-start(s32[4,8]{1,0:T(4,128)S(1)} %copy-done.15), channel_id=1, source_target_pairs={{0,24},{4,28},{8,0},{12,4},{16,8},{20,12},{24,16},{28,20},{1,25},{... | collective-permute-start | bytes 392 | tf_op jit(solution)/shard_map/right_masks/ppermute | solution.py:22
  30.3 0.0 collective-permute-done.6.refs_4_.refs_0_.refs_10_
  30.3 0.0 copy-done.2
  30.3 0.7 pool.2
  31.0 0.7 collective-permute-start.12
  31.7 3.4 %collective-permute-done.13.refs_0_ = bf16[4,8,128,128]{3,2,1,0:T(8,128)(2,1)} collective-permute-done((bf16[4,8,128,128]{3,2,1,0:T(8,128)(2,1)}, bf16[4,8,128,128]{3,2,1,0:T(8,128)(2,1)}, u32[]{:S(2)}, u32[]{:S(2)}) %collective-permute-start.13) | collective-permute-done | bytes 1048608 | tf_op jit(solution)/shard_map/right_two_up/ppermute | solution.py:22
  35.1 1.3 %collective-permute-start.7 = (bf16[2064,128]{1,0:T(8,128)(2,1)S(1)}, bf16[2064,128]{1,0:T(8,128)(2,1)S(1)}, u32[]{:S(2)}, u32[]{:S(2)}) collective-permute-start(bf16[2064,128]{1,0:T(8,128)(2,1)S(1)} %collective-permute-done.6.refs_4_.refs_0_.refs_10_), channel_id=1, source_target_pairs={{1,0},{2,3},{5,4},{6,7},{9,8},{10,11},{13,12},{14,15},{17,16},{18,... | collective-permute-start | bytes 1585160 | tf_op jit(solution)/shard_map/third_head_outward/ppermute | solution.py:419
  36.4 0.0 collective-permute-done.9.refs_6_.refs_2_.refs_1_
  36.4 0.1 collective-permute-start.8
  36.5 9.1 %collective-permute-done.5.refs_1_.refs_0_.refs_6_ = bf16[3088,128]{1,0:T(8,128)(2,1)S(1)} collective-permute-done((bf16[3088,128]{1,0:T(8,128)(2,1)S(1)}, bf16[3088,128]{1,0:T(8,128)(2,1)S(1)}, u32[]{:S(2)}, u32[]{:S(2)}) %collective-permute-start.5) | collective-permute-done | bytes 790560 | tf_op jit(solution)/shard_map/second_head_outward/ppermute | solution.py:419
  45.6 0.0 collective-permute-start.10
  45.6 0.0 collective-permute-done.8.refs_5_.refs_1_.refs_0_
  45.6 1.1 %collective-permute-done.10.refs_7_.refs_3_.refs_2_ = s32[4,8]{1,0:T(4,128)S(1)} collective-permute-done((s32[4,8]{1,0:T(4,128)S(1)}, s32[4,8]{1,0:T(4,128)S(1)}, u32[]{:S(2)}, u32[]{:S(2)}) %collective-permute-start.10) | collective-permute-done | bytes 160 | tf_op jit(solution)/shard_map/right_masks/ppermute | solution.py:437
  46.7 0.0 collective-permute-done.14.refs_4_.refs_13_.refs_5_
  46.7 6.5 %collective-permute-done.7.refs_2_.refs_7_ = bf16[2064,128]{1,0:T(8,128)(2,1)S(1)} collective-permute-done((bf16[2064,128]{1,0:T(8,128)(2,1)S(1)}, bf16[2064,128]{1,0:T(8,128)(2,1)S(1)}, u32[]{:S(2)}, u32[]{:S(2)}) %collective-permute-start.7) | collective-permute-done | bytes 528416 | tf_op jit(solution)/shard_map/third_head_outward/ppermute | solution.py:419
  53.2 0.0 collective-permute-done.12.more_ref.refs_11_
  53.2 1.5 %pool.3 = (bf16[4,8,128,128]{3,2,1,0:T(8,128)(2,1)}, bf16[2304,128]{1,0:T(8,128)(2,1)}) custom-call(s32[1]{0:T(128)} %get-tuple-element.172.n_ref, bf16[2048,128]{1,0:T(8,128)(2,1)S(1)} %get-tuple-element.170.tail_ref, bf16[2304,128]{1,0:T(8,128)(2,1)S(1)} %collective-permute-done.12.more_ref.refs_11_, ...), custom_call_target="tpu_custom_call", output_to_operand_aliasing={{0}: (3, {})} | custom-call | bytes 1769472 | tf_op jit(solution)/shard_map/pool/pallas_call | solution.py:468
  54.8 0.0 collective-permute-start.16
  54.8 0.0 copy-done
  54.8 0.0 copy-done.7
  54.8 1.3 %collective-permute-start.15 = (bf16[2304,128]{1,0:T(8,128)(2,1)}, bf16[2304,128]{1,0:T(8,128)(2,1)S(1)}, u32[]{:S(2)}, u32[]{:S(2)}) collective-permute-start(bf16[2304,128]{1,0:T(8,128)(2,1)} %get-tuple-element.174), channel_id=1, source_target_pairs={{1,0},{2,3},{5,4},{6,7},{9,8},{10,11},{13,12},{14,15},{17,16},{18,... | collective-permute-start | bytes 1769480 | tf_op jit(solution)/shard_map/pool_outward/ppermute | solution.py:419
  56.1 0.0 copy-start.1
  56.1 0.0 copy-start.3
  56.1 0.0 copy-start.8
  56.1 0.1 pad_add_fusion.where_ref
  56.2 0.0 copy-done.14
  56.2 3.2 %table.1 = (s32[200]{0:T(256)S(1)}, s32[1]{0:T(128)}) custom-call(s32[2]{0:T(128)S(1)} %pad_add_fusion.where_ref, s32[4,8]{1,0:T(4,128)S(1)} %bitcast.5, bf16[2064,128]{1,0:T(8,128)(2,1)S(1)} %get-tuple-element.168.refs_0_.refs_5_, bf16[3088,128]{1,0:T(8,128)(2,1)S(1)} %collective-permute-done.5.refs_1_.refs_0_.refs_6_, ...), custom_call_target="tpu_custom_call" | custom-call | tf_op jit(solution)/shard_map/table/pallas_call | solution.py:514
  59.4 0.0 collective-permute-done.16.refs_15_.refs_7_
  59.4 8.5 %early.1 = (f32[1024,1024]{1,0:T(8,128)S(1)}, bf16[8,8,128,128]{3,2,1,0:T(8,128)(2,1)S(1)}) custom-call(s32[2]{0:T(128)S(1)} %pad_add_fusion.where_ref, s32[4,8]{1,0:T(4,128)S(1)} %bitcast.6, s32[8,8]{1,0:T(8,128)S(1)} %copy-done.13, s32[200]{0:T(256)S(1)} %get-tuple-element.171.table_ref, s32[4,8]{1,0:T(4,128)S(1)} %copy-done.15, ...), custom_call_target="tpu_custom_call" | custom-call | flops 4294967296 | bytes 14680064 | tf_op jit(solution)/shard_map/early/pallas_call | solution.py:535
  67.9 4.7 %collective-permute-done.15.refs_3_ = bf16[2304,128]{1,0:T(8,128)(2,1)S(1)} collective-permute-done((bf16[2304,128]{1,0:T(8,128)(2,1)}, bf16[2304,128]{1,0:T(8,128)(2,1)S(1)}, u32[]{:S(2)}, u32[]{:S(2)}) %collective-permute-start.15) | collective-permute-done | bytes 589856 | tf_op jit(solution)/shard_map/pool_outward/ppermute | solution.py:419
  72.6 4.2 %late.1 = bf16[8,8,128,128]{3,2,1,0:T(8,128)(2,1)S(1)} custom-call(s32[2]{0:T(128)S(1)} %pad_add_fusion.where_ref, s32[8,8]{1,0:T(8,128)S(1)} %copy-done.13, s32[200]{0:T(256)S(1)} %get-tuple-element.171.table_ref, s32[4,8]{1,0:T(4,128)S(1)} %collective-permute-done.8.refs_5_.refs_1_.refs_0_, ...), custom_call_target="tpu_custom_call", output_to_operand_aliasing={{}: (11, {})} | custom-call | bytes 4194304 | tf_op jit(solution)/shard_map/late/pallas_call | solution.py:555
  76.9 0.0 copy-start.4
  76.9 1.3 %copy-done.4 = bf16[8,8,128,128]{3,2,1,0:T(8,128)(2,1)} copy-done((bf16[8,8,128,128]{3,2,1,0:T(8,128)(2,1)}, bf16[8,8,128,128]{3,2,1,0:T(8,128)(2,1)S(1)}, u32[]{:S(2)}) %copy-start.4) | copy-done | bytes 2097176
  78.2 0.7 while.12
  (15 shorter events, 0.0 us)
Async XLA Ops:
  1.8 11.0 %collective-permute-start.4 = (bf16[2064,128]{1,0:T(8,128)(2,1)S(1)}, bf16[2064,128]{1,0:T(8,128)(2,1)S(1)}, u32[]{:S(2)}, u32[]{:S(2)}) collective-permute-start(bf16[2064,128]{1,0:T(8,128)(2,1)S(1)} %get-tuple-element.167), channel_id=1, source_target_pairs={{1,2},{2,1},{5,6},{6,5},{9,10},{10,9},{13,14},{14,13},{17,18},{18,... | collective-permute-start | bytes 1585160 | tf_op jit(solution)/shard_map/head_over_middle/ppermute | solution.py:428
  2.5 18.3 %collective-permute-start.3 = (bf16[2064,128]{1,0:T(8,128)(2,1)S(1)}, bf16[2064,128]{1,0:T(8,128)(2,1)S(1)}, u32[]{:S(2)}, u32[]{:S(2)}) collective-permute-start(bf16[2064,128]{1,0:T(8,128)(2,1)S(1)} %get-tuple-element.167), channel_id=1, source_target_pairs={{0,1},{1,0},{2,3},{3,2},{4,5},{5,4},{6,7},{7,6},{8,9},{9,8},{10,11... | collective-permute-start | bytes 1585160 | tf_op jit(solution)/shard_map/head_end_swap/ppermute | solution.py:422
  8.4 19.4 %collective-permute-start.11 = (bf16[1536,128]{1,0:T(8,128)(2,1)S(1)}, bf16[1536,128]{1,0:T(8,128)(2,1)S(1)}, u32[]{:S(2)}, u32[]{:S(2)}) collective-permute-start(bf16[1536,128]{1,0:T(8,128)(2,1)S(1)} %get-tuple-element.173), channel_id=1, source_target_pairs={{0,1},{3,2},{4,5},{7,6},{8,9},{11,10},{12,13},{15,14},{16,17},{19,... | collective-permute-start | bytes 1179656 | tf_op jit(solution)/shard_map/tail_inward/ppermute | solution.py:425
  10.3 24.7 %collective-permute-start.13 = (bf16[4,8,128,128]{3,2,1,0:T(8,128)(2,1)}, bf16[4,8,128,128]{3,2,1,0:T(8,128)(2,1)}, u32[]{:S(2)}, u32[]{:S(2)}) collective-permute-start(bf16[4,8,128,128]{3,2,1,0:T(8,128)(2,1)} %refs_12_.1), channel_id=1, source_target_pairs={{0,24},{4,28},{8,0},{12,4},{16,8},{20,12},{24,16},{28,20},{1,25},{... | collective-permute-start | bytes 3145736 | tf_op jit(solution)/shard_map/right_two_up/ppermute | solution.py:22
  12.8 33.9 %collective-permute-start.14 = (bf16[4,8,128,128]{3,2,1,0:T(8,128)(2,1)}, bf16[4,8,128,128]{3,2,1,0:T(8,128)(2,1)S(1)}, u32[]{:S(2)}, u32[]{:S(2)}) collective-permute-start(bf16[4,8,128,128]{3,2,1,0:T(8,128)(2,1)} %refs_12_.1), channel_id=1, source_target_pairs={{4,0},{16,4},{12,8},{24,12},{20,16},{0,20},{28,24},{8,28},{5,1},{1... | collective-permute-start | bytes 3145736 | tf_op jit(solution)/shard_map/right_odd_up/ppermute | solution.py:434
  20.9 9.4 %collective-permute-start.6 = (bf16[2064,128]{1,0:T(8,128)(2,1)S(1)}, bf16[2064,128]{1,0:T(8,128)(2,1)S(1)}, u32[]{:S(2)}, u32[]{:S(2)}) collective-permute-start(bf16[2064,128]{1,0:T(8,128)(2,1)S(1)} %get-tuple-element.168.refs_0_.refs_5_), channel_id=1, source_target_pairs={{1,2},{2,1},{5,6},{6,5},{9,10},{10,9},{13,14},{14,13},{17,18},{18,... | collective-permute-start | bytes 1585160 | tf_op jit(solution)/shard_map/end_head_over_middle/ppermute | solution.py:428
  21.6 6.2 %copy-start.15 = (s32[4,8]{1,0:T(4,128)S(1)}, s32[4,8]{1,0:T(4,128)}, u32[]{:S(2)}) copy-start(s32[4,8]{1,0:T(4,128)} %refs_0_.1) | copy-start | bytes 388
  21.6 24.0 %collective-permute-start.5 = (bf16[3088,128]{1,0:T(8,128)(2,1)S(1)}, bf16[3088,128]{1,0:T(8,128)(2,1)S(1)}, u32[]{:S(2)}, u32[]{:S(2)}) collective-permute-start(bf16[3088,128]{1,0:T(8,128)(2,1)S(1)} %extend.1), channel_id=1, source_target_pairs={{1,0},{2,3},{5,4},{6,7},{9,8},{10,11},{13,12},{14,15},{17,16},{18,... | collective-permute-start | bytes 2371592 | tf_op jit(solution)/shard_map/second_head_outward/ppermute | solution.py:419
  27.8 2.5 %copy-start.2 = (bf16[1536,128]{1,0:T(8,128)(2,1)}, bf16[1536,128]{1,0:T(8,128)(2,1)S(1)}, u32[]{:S(2)}) copy-start(bf16[1536,128]{1,0:T(8,128)(2,1)S(1)} %collective-permute-done.11.refs_0_.more_ref.refs_8_) | copy-start | bytes 1179652
  27.8 8.6 %collective-permute-start.9 = (s32[4,8]{1,0:T(4,128)S(1)}, s32[4,8]{1,0:T(4,128)S(1)}, u32[]{:S(2)}, u32[]{:S(2)}) collective-permute-start(s32[4,8]{1,0:T(4,128)S(1)} %copy-done.15), channel_id=1, source_target_pairs={{0,24},{4,28},{8,0},{12,4},{16,8},{20,12},{24,16},{28,20},{1,25},{... | collective-permute-start | bytes 392 | tf_op jit(solution)/shard_map/right_masks/ppermute | solution.py:22
  31.0 22.2 %collective-permute-start.12 = (bf16[2304,128]{1,0:T(8,128)(2,1)S(1)}, bf16[2304,128]{1,0:T(8,128)(2,1)S(1)}, u32[]{:S(2)}, u32[]{:S(2)}) collective-permute-start(bf16[2304,128]{1,0:T(8,128)(2,1)S(1)} %pool.2), channel_id=1, source_target_pairs={{1,2},{2,1},{5,6},{6,5},{9,10},{10,9},{13,14},{14,13},{17,18},{18,... | collective-permute-start | bytes 1769480 | tf_op jit(solution)/shard_map/pool_over_middle/ppermute | solution.py:428
  35.1 18.1 %collective-permute-start.7 = (bf16[2064,128]{1,0:T(8,128)(2,1)S(1)}, bf16[2064,128]{1,0:T(8,128)(2,1)S(1)}, u32[]{:S(2)}, u32[]{:S(2)}) collective-permute-start(bf16[2064,128]{1,0:T(8,128)(2,1)S(1)} %collective-permute-done.6.refs_4_.refs_0_.refs_10_), channel_id=1, source_target_pairs={{1,0},{2,3},{5,4},{6,7},{9,8},{10,11},{13,12},{14,15},{17,16},{18,... | collective-permute-start | bytes 1585160 | tf_op jit(solution)/shard_map/third_head_outward/ppermute | solution.py:419
  36.4 9.2 %collective-permute-start.8 = (s32[4,8]{1,0:T(4,128)S(1)}, s32[4,8]{1,0:T(4,128)S(1)}, u32[]{:S(2)}, u32[]{:S(2)}) collective-permute-start(s32[4,8]{1,0:T(4,128)S(1)} %copy-done.15), channel_id=1, source_target_pairs={{4,0},{16,4},{12,8},{24,12},{20,16},{0,20},{28,24},{8,28},{5,1},{1... | collective-permute-start | bytes 392 | tf_op jit(solution)/shard_map/right_masks/ppermute | solution.py:434
  45.6 1.2 %collective-permute-start.10 = (s32[4,8]{1,0:T(4,128)S(1)}, s32[4,8]{1,0:T(4,128)S(1)}, u32[]{:S(2)}, u32[]{:S(2)}) collective-permute-start(s32[4,8]{1,0:T(4,128)S(1)} %collective-permute-done.9.refs_6_.refs_2_.refs_1_), channel_id=1, source_target_pairs={{0,4},{4,0},{8,12},{12,8},{16,20},{20,16},{24,28},{28,24},{1,5},{5... | collective-permute-start | bytes 392 | tf_op jit(solution)/shard_map/right_masks/ppermute | solution.py:437
  45.6 10.6 %copy-start.14 = (s32[8,4]{0,1:T(4,128)S(1)}, s32[8,4]{0,1:T(4,128)}, u32[]{:S(2)}) copy-start(s32[8,4]{0,1:T(4,128)} %param.8) | copy-start | bytes 388
  46.7 8.0 %copy-start.7 = (bf16[4,8,128,128]{3,2,1,0:T(8,128)(2,1)}, bf16[4,8,128,128]{3,2,1,0:T(8,128)(2,1)S(1)}, u32[]{:S(2)}) copy-start(bf16[4,8,128,128]{3,2,1,0:T(8,128)(2,1)S(1)} %collective-permute-done.14.refs_4_.refs_13_.refs_5_) | copy-start | bytes 3145732
  53.2 1.6 %copy-start = (bf16[2304,128]{1,0:T(8,128)(2,1)}, bf16[2304,128]{1,0:T(8,128)(2,1)S(1)}, u32[]{:S(2)}) copy-start(bf16[2304,128]{1,0:T(8,128)(2,1)S(1)} %collective-permute-done.12.more_ref.refs_11_) | copy-start | bytes 1769476
  54.8 4.6 %copy-start.13 = (s32[8,8]{1,0:T(8,128)S(1)}, s32[8,8]{1,0:T(8,128)}, u32[]{:S(2)}) copy-start(s32[8,8]{1,0:T(8,128)} %c_ref.3) | copy-start | bytes 772
  54.8 4.6 %collective-permute-start.16 = (bf16[4,8,128,128]{3,2,1,0:T(8,128)(2,1)}, bf16[4,8,128,128]{3,2,1,0:T(8,128)(2,1)}, u32[]{:S(2)}, u32[]{:S(2)}) collective-permute-start(bf16[4,8,128,128]{3,2,1,0:T(8,128)(2,1)} %get-tuple-element.302.refs_14_.refs_6_), channel_id=1, source_target_pairs={{0,4},{4,0},{8,12},{12,8},{16,20},{20,16},{24,28},{28,24},{1,5},{5... | collective-permute-start | bytes 3145736 | tf_op jit(solution)/shard_map/right_core_swap/ppermute | solution.py:437
  54.8 17.8 %collective-permute-start.15 = (bf16[2304,128]{1,0:T(8,128)(2,1)}, bf16[2304,128]{1,0:T(8,128)(2,1)S(1)}, u32[]{:S(2)}, u32[]{:S(2)}) collective-permute-start(bf16[2304,128]{1,0:T(8,128)(2,1)} %get-tuple-element.174), channel_id=1, source_target_pairs={{1,0},{2,3},{5,4},{6,7},{9,8},{10,11},{13,12},{14,15},{17,16},{18,... | collective-permute-start | bytes 1769480 | tf_op jit(solution)/shard_map/pool_outward/ppermute | solution.py:419
  56.1 3.3 %copy-start.1 = (bf16[2304,128]{1,0:T(8,128)(2,1)S(1)}, bf16[2304,128]{1,0:T(8,128)(2,1)}, u32[]{:S(2)}) copy-start(bf16[2304,128]{1,0:T(8,128)(2,1)} %copy-done) | copy-start | bytes 1769476
  56.1 3.3 %copy-start.3 = (bf16[1536,128]{1,0:T(8,128)(2,1)S(1)}, bf16[1536,128]{1,0:T(8,128)(2,1)}, u32[]{:S(2)}) copy-start(bf16[1536,128]{1,0:T(8,128)(2,1)} %copy-done.2) | copy-start | bytes 1179652
  56.1 3.3 %copy-start.8 = (bf16[4,8,128,128]{3,2,1,0:T(8,128)(2,1)S(1)}, bf16[4,8,128,128]{3,2,1,0:T(8,128)(2,1)}, u32[]{:S(2)}) copy-start(bf16[4,8,128,128]{3,2,1,0:T(8,128)(2,1)} %copy-done.7) | copy-start | bytes 3145732
  72.6 5.6 %copy-start.10 = (bf16[8,4,128,128]{3,2,1,0:T(8,128)(2,1)S(1)}, bf16[8,4,128,128]{3,2,1,0:T(8,128)(2,1)}, u32[]{:S(2)}) copy-start(bf16[8,4,128,128]{3,2,1,0:T(8,128)(2,1)} %refs_4_.1) | copy-start | bytes 3145732
  76.9 1.3 %copy-start.4 = (bf16[8,8,128,128]{3,2,1,0:T(8,128)(2,1)}, bf16[8,8,128,128]{3,2,1,0:T(8,128)(2,1)S(1)}, u32[]{:S(2)}) copy-start(bf16[8,8,128,128]{3,2,1,0:T(8,128)(2,1)S(1)} %late.1) | copy-start | bytes 6291460

commit v5 on v4

--- a/solution.py
+++ b/solution.py
@@ -8,7 +8,7 @@
 from jax.sharding import PartitionSpec as P
 
 STEPS = 4
-T_TAIL, T_SECOND, T_RIGHT = 7, 5, 2
+T_TAIL, T_SECOND, T_THIRD, T_RIGHT = 7, 4, 12, 1
 NOTE = 16
 MIB = 1024 * 1024
 
@@ -204,7 +204,7 @@
 
 
 def table_kernel(blocks, where_ref, own_ref, *refs):
-    notes, (table_ref, over_ref, note_ref, wide_ref, mask_ref, sems, sem) = refs[:5], refs[5:]
+    notes, (table_ref, over_ref, note_ref, wide_ref, mask_ref, sems, sem) = refs[:5], refs[6:]
     copies = [
         pltpu.make_async_copy(
             ref.at[pl.ds(ref.shape[0] - NOTE, NOTE), :], note_ref.at[pl.ds(m * NOTE, NOTE), :], sems.at[m]
@@ -350,33 +350,83 @@
             out_ref[i, j] = filtered(c_ref, i, j0 + j, total[i * blk : (i + 1) * blk, j * blk : (j + 1) * blk])
 
 
-def late_kernel(where_ref, c_ref, table_ref, *refs):
+def rows_kernel(where_ref, table_ref, *refs):
     b_masks, refs = refs[: STEPS - 1], refs[STEPS - 1 :]
-    late_ref, acc_ref, b_refs, refs = refs[0], refs[1], refs[2 : 1 + STEPS], refs[2 + STEPS :]
-    out_ref, row_ref, touched_ref, sems = refs
-    br, bc, blk, _ = out_ref.shape
+    b_refs, (rows_ref, b_ref, need_ref, sems) = refs[: STEPS - 1], refs[STEPS:]
+    _, bc, blk, _ = b_ref.shape
     kb = b_refs[0].shape[0]
+    br = (table_ref.shape[0] // 5 - 8) // kb
     _, _, _, pool = slots(kb * br)
     first = 3 * (kb * br + 8)
     at_end = jnp.logical_or(where_ref[0] == 0, where_ref[0] == 3)
 
+    def clear(r, carry):
+        need_ref[r] = 0
+        return carry
+
+    def mark(b, carry):
+        place = table_ref[first + b]
+
+        @pl.when(place < STEPS * kb * br)
+        def _():
+            need_ref[place // br - kb] = 1
+
+        return carry
+
+    lax.fori_loop(0, (STEPS - 1) * kb, clear, 0)
+    lax.fori_loop(0, jnp.where(at_end, pool, 0), mark, 0)
+    copies = [
+        pltpu.make_async_copy(b_refs[r // kb].at[r % kb], b_ref.at[r], sems.at[r]) for r in range((STEPS - 1) * kb)
+    ]
+
+    def when(r, act):
+        @pl.when(need_ref[r] > 0)
+        def _():
+            act()
+
+    for r, copy in enumerate(copies):
+        when(r, copy.start)
+    for r, copy in enumerate(copies):
+        when(r, copy.wait)
+    for slab, mask_ref in enumerate(b_masks):
+
+        def fill(k, carry):
+            r = slab * kb + k
+
+            @pl.when(need_ref[r] > 0)
+            def _():
+                for j in range(bc):
+                    keep = mask_ref[k, j].astype(jnp.float32).astype(jnp.bfloat16)
+                    rows_ref[pl.ds(pl.multiple_of(r * blk, blk), blk), j * blk : (j + 1) * blk] = b_ref[r, j] * keep
+
+            return carry
+
+        lax.fori_loop(0, kb, fill, 0)
+
+
+def late_kernel(where_ref, c_ref, table_ref, late_ref, acc_ref, rows_ref, _, out_ref, row_ref, touched_ref, sems):
+    br, bc, blk, _ = out_ref.shape
+    kb = rows_ref.shape[0] // blk // (STEPS - 1)
+    _, _, _, pool = slots(kb * br)
+    first = 3 * (kb * br + 8)
+    at_end = jnp.logical_or(where_ref[0] == 0, where_ref[0] == 3)
+
     def clear(i, carry):
         touched_ref[i] = 0
         return carry
 
     def add(b, carry):
         place = table_ref[first + b]
-        for slab, (b_ref, mask_ref) in enumerate(zip(b_refs, b_masks)):
-
-            @pl.when(place // (kb * br) == slab + 1)
-            def _():
-                i, k = place % br, (place // br) % kb
-                touched_ref[i] = 1
-                keep = [mask_ref[k, j].astype(jnp.float32).astype(jnp.bfloat16) for j in range(bc)]
-                columns = jnp.concatenate([b_ref[k, j] * keep[j] for j in range(bc)], axis=1)
-                acc_ref[pl.ds(pl.multiple_of(i * blk, blk), blk), :] += jnp.dot(
-                    late_ref[pl.ds(pl.multiple_of(b * blk, blk), blk), :], columns, preferred_element_type=jnp.float32
-                )
+
+        @pl.when(place < STEPS * kb * br)
+        def _():
+            i, r = place % br, place // br - kb
+            touched_ref[i] = 1
+            acc_ref[pl.ds(pl.multiple_of(i * blk, blk), blk), :] += jnp.dot(
+                late_ref[pl.ds(pl.multiple_of(b * blk, blk), blk), :],
+                rows_ref[pl.ds(pl.multiple_of(r * blk, blk), blk), :],
+                preferred_element_type=jnp.float32,
+            )
 
         return carry
 
@@ -463,20 +513,18 @@
         name="compact",
     )(by_column, a_blocks)
 
-    def pooled(skip, more, gate, seen):
+    def pooled(skip, more, seen):
         own = blocks - skip
-        outs = pl.pallas_call(
+        return pl.pallas_call(
             functools.partial(pool_kernel, skip),
-            in_specs=[smem(), whole(), whole()] + [anywhere()] * (len(gate) + len(seen)),
-            out_specs=[anywhere()] * len(gate) + [whole()],
-            out_shape=[jax.ShapeDtypeStruct(g.shape, g.dtype) for g in gate] + [listed(pool)],
+            in_specs=[smem(), whole(), whole()] + [anywhere()] * len(seen),
+            out_specs=whole(),
+            out_shape=listed(pool),
             scratch_shapes=[pltpu.VMEM((own * blk + more.shape[0], blk), a_blocks.dtype)],
-            input_output_aliases={3 + g: g for g in range(len(gate))},
             compiler_params=params(),
             cost_estimate=cost(0, 6 * pool * blk * blk),
             name="pool",
-        )(n, own_tail, more, *gate, *seen)
-        return outs[-1], outs[:-1]
+        )(n, own_tail, more, *seen)
 
     with jax.named_scope("head_over_middle"):
         mid_head = over_middle(own_head)
@@ -484,7 +532,6 @@
         near_head = end_swap(own_head)
     with jax.named_scope("tail_inward"):
         near_tail = inward(own_inner)
-    near_head, mid_head = passed([near_head, mid_head])
     with jax.named_scope("second_head_outward"):
         second_head = outward(
             pl.pallas_call(
@@ -501,11 +548,12 @@
         end_head = over_middle(near_head)
     with jax.named_scope("third_head_outward"):
         third_head = outward(end_head)
-    mid_pool, _ = pooled(head, near_tail, [], [end_head, token([near_tail], T_TAIL)])
+    mid_pool = pooled(head, near_tail, [end_head, token([near_tail], T_TAIL)])
     with jax.named_scope("pool_over_middle"):
         mid_pool = over_middle(mid_pool)
-    here = [token([second_head], T_SECOND), third_head, token([second], T_RIGHT), odd_one] + b_masks[1:]
-    out_pool, (second,) = pooled(lead, mid_pool, [second], here)
+    here = [token([second_head], T_SECOND), token([second], T_RIGHT), odd_one] + b_masks[1:]
+    mid_pool, second = passed([mid_pool, second], here)
+    out_pool = pooled(lead, mid_pool, [])
     with jax.named_scope("pool_outward"):
         out_pool = outward(out_pool)
     with jax.named_scope("right_core_swap"):
@@ -513,7 +561,7 @@
 
     table, over = pl.pallas_call(
         functools.partial(table_kernel, blocks),
-        in_specs=[smem(), smem()] + [anywhere()] * 5,
+        in_specs=[smem(), smem()] + [anywhere()] * 6,
         out_specs=[smem(), smem()],
         out_shape=[jax.ShapeDtypeStruct((5 * (blocks + 8),), jnp.int32), jax.ShapeDtypeStruct((1,), jnp.int32)],
         scratch_shapes=[
@@ -525,7 +573,7 @@
         ],
         compiler_params=params(),
         name="table",
-    )(where, by_column, near_head, second_head, third_head, mid_head, end_head)
+    )(where, by_column, near_head, second_head, third_head, mid_head, end_head, token([third_head], T_THIRD))
 
     def fixed(x):
         return pl.BlockSpec(x.shape, lambda g: (0,) * x.ndim)
@@ -552,21 +600,40 @@
         name="early",
     )(where, by_column, c_mask, table, *b_masks, a_blocks, *arrived, *right)
 
-    out = pl.pallas_call(
-        late_kernel,
-        in_specs=[smem()] * (3 + STEPS - 1) + [whole()] * (1 + STEPS) + [anywhere()],
-        out_specs=anywhere(),
-        out_shape=jax.ShapeDtypeStruct((br, bc, blk, blk), jnp.bfloat16),
+    rows_shape = jax.ShapeDtypeStruct(((STEPS - 1) * kb * blk, bc * blk), jnp.bfloat16)
+    met = pl.pallas_call(
+        rows_kernel,
+        in_specs=[smem()] * (2 + STEPS - 1) + [anywhere()] * STEPS,
+        out_specs=whole(),
+        out_shape=rows_shape,
         scratch_shapes=[
-            pltpu.VMEM((br, bc, blk, blk), jnp.bfloat16),
-            pltpu.SMEM((br,), jnp.int32),
-            pltpu.SemaphoreType.DMA((br,)),
+            pltpu.VMEM(((STEPS - 1) * kb, bc, blk, blk), jnp.bfloat16),
+            pltpu.SMEM(((STEPS - 1) * kb,), jnp.int32),
+            pltpu.SemaphoreType.DMA(((STEPS - 1) * kb,)),
         ],
-        input_output_aliases={3 + STEPS - 1 + 1 + STEPS: 0},
         compiler_params=params(12),
-        cost_estimate=cost(0, 4 << 20),
-        name="late",
-    )(where, c_mask, table, *b_masks[1:], out_pool, acc, *right[1:], out)
+        cost_estimate=cost(0, 1 << 20),
+        name="rows",
+    )(where, table, *b_masks[1:], *right[1:], acc)
+
+    def rest(out, acc, late, met):
+        return pl.pallas_call(
+            late_kernel,
+            in_specs=[smem()] * 3 + [whole()] * 3 + [anywhere()],
+            out_specs=anywhere(),
+            out_shape=jax.ShapeDtypeStruct((br, bc, blk, blk), jnp.bfloat16),
+            scratch_shapes=[
+                pltpu.VMEM((br, bc, blk, blk), jnp.bfloat16),
+                pltpu.SMEM((br,), jnp.int32),
+                pltpu.SemaphoreType.DMA((br,)),
+            ],
+            input_output_aliases={6: 0},
+            compiler_params=params(12),
+            cost_estimate=cost(0, 4 << 20),
+            name="late",
+        )(where, c_mask, table, late, acc, met, out)
+
+    out = rest(out, acc, out_pool, met)
 
     def again(state):
         before, trips = state

time: 79.3 us -> 71.5 us (0.902)
  waiting for transfers between devices: 37.7 us -> 27.3 us
  starting transfers between devices: 18.8 us -> 21.2 us
  Pallas kernels: 20 us -> 22.3 us
  local copies, waits for them, and re-layouts: 1.35 us -> 0.03 us
    ppermute x3, waiting for transfers between devices: 20.3 us -> 7.87 us  [outward(): return lax.ppermute(x, 'col', [(1, 0), (2, 3)])]
    pallas_call x1 -> x2, Pallas kernels: 4.25 us -> 6.96 us  [the longest x1 4.74 us: rest(): pl.pallas_call(late_kernel, in_specs=[smem()] * 3 + [whole()] * 3 + [anyw...]
    ppermute x2, waiting for transfers between devices: 3.37 us -> 5.72 us  [from_behind(): lax.ppermute(array, axis, [(i, (i + by) % size) for i in range(size)])]
    ppermute x2, starting transfers between devices: 0.01 us -> 1.47 us  [core_swap(): return lax.ppermute(x, 'row', [(r, r ^ 1) for r in range(rows)])]
    ppermute x1, waiting for transfers between devices: 4.9 us -> 6.27 us  [inward(): return lax.ppermute(x, 'col', [(0, 1), (3, 2)])]
    ppermute x1, waiting for transfers between devices: 8 us -> 6.63 us  [end_swap(): return lax.ppermute(x, 'col', [(0, 1), (1, 0), (2, 3), (3, 2)])]
    unnamed x22 -> x14, local copies, waits for them, and re-layouts: 1.35 us -> 0.03 us
    ppermute x2, waiting for transfers between devices: 1.15 us -> 0.03 us  [core_swap(): return lax.ppermute(x, 'row', [(r, r ^ 1) for r in range(rows)])]
  transfers between devices with their start and end apart: 14 -> 14, of which waited for: 7 -> 6; matrix products, arithmetic and copies ran while one was open for 0% -> 0% of each run, Pallas kernels for 16% -> 22%
where the time goes in v5:
time: 71.5 us; the launch traced here: 71.8 us
  waiting for transfers between devices  27.3 us (38%)
  Pallas kernels  22.3 us (31%)
  starting transfers between devices  21.2 us (30%)
    pallas_call x1, Pallas kernels, sparse_product(): pl.pallas_call(early_kernel, grid=(bc // wide_j,), in_specs=[smem()] * (4...  8.86 us
    ppermute x3, waiting for transfers between devices, outward(): return lax.ppermute(x, 'col', [(1, 0), (2, 3)])  7.87 us
    ppermute x1, waiting for transfers between devices, end_swap(): return lax.ppermute(x, 'col', [(0, 1), (1, 0), (2, 3), (3, 2)])  6.63 us
    ppermute x1, waiting for transfers between devices, inward(): return lax.ppermute(x, 'col', [(0, 1), (3, 2)])  6.27 us
    ppermute x2, starting transfers between devices, from_behind(): lax.ppermute(array, axis, [(i, (i + by) % size) for i in range(size)])  5.94 us
    ppermute x1, starting transfers between devices, end_swap(): return lax.ppermute(x, 'col', [(0, 1), (1, 0), (2, 3), (3, 2)])  5.88 us
    ppermute x2, waiting for transfers between devices, from_behind(): lax.ppermute(array, axis, [(i, (i + by) % size) for i in range(size)])  5.72 us
    pallas_call x1, Pallas kernels, rest(): pl.pallas_call(late_kernel, in_specs=[smem()] * 3 + [whole()] * 3 + [anyw...  4.74 us
  transfers between devices with their start and end apart: 14, of which 6 were waited for; matrix products, arithmetic and copies ran while one was open for 0% of the time, Pallas kernels for 22%

profile of v5, /device:TPU:0, one launch (start us, length us, event | category | flops | bytes accessed | tf_op | source)
XLA Modules:
  0.0 71.8 jit_solution(794275449320347217)
XLA Ops:
  0.0 1.8 %compact.1 = (bf16[2064,128]{1,0:T(8,128)(2,1)S(1)}, bf16[1536,128]{1,0:T(8,128)(2,1)S(1)}, bf16[2048,128]{1,0:T(8,128)(2,1)S(1)}, s32[1]{0:T(128)}) custom-call(s32[4,8]{1,0:T(4,128)} %bitcast.4, bf16[8,4,128,128]{3,2,1,0:T(8,128)(2,1)} %refs_4_.1), custom_call_target="tpu_custom_call" | custom-call | bytes 3145728 | tf_op jit(solution)/shard_map/compact/pallas_call | solution.py:500
  1.8 0.7 collective-permute-start.4
  2.5 5.9 %collective-permute-start.3 = (bf16[2064,128]{1,0:T(8,128)(2,1)S(1)}, bf16[2064,128]{1,0:T(8,128)(2,1)S(1)}, u32[]{:S(2)}, u32[]{:S(2)}) collective-permute-start(bf16[2064,128]{1,0:T(8,128)(2,1)S(1)} %get-tuple-element.165), channel_id=1, source_target_pairs={{0,1},{1,0},{2,3},{3,2},{4,5},{5,4},{6,7},{7,6},{8,9},{9,8},{10,11... | collective-permute-start | bytes 1585160 | tf_op jit(solution)/shard_map/head_end_swap/ppermute | solution.py:472
  8.4 1.9 %collective-permute-start.8 = (bf16[1536,128]{1,0:T(8,128)(2,1)S(1)}, bf16[1536,128]{1,0:T(8,128)(2,1)S(1)}, u32[]{:S(2)}, u32[]{:S(2)}) collective-permute-start(bf16[1536,128]{1,0:T(8,128)(2,1)S(1)} %get-tuple-element.169), channel_id=1, source_target_pairs={{0,1},{3,2},{4,5},{7,6},{8,9},{11,10},{12,13},{15,14},{16,17},{19,... | collective-permute-start | bytes 1179656 | tf_op jit(solution)/shard_map/tail_inward/ppermute | solution.py:475
  10.3 2.5 %collective-permute-start.10 = (bf16[4,8,128,128]{3,2,1,0:T(8,128)(2,1)}, bf16[4,8,128,128]{3,2,1,0:T(8,128)(2,1)}, u32[]{:S(2)}, u32[]{:S(2)}) collective-permute-start(bf16[4,8,128,128]{3,2,1,0:T(8,128)(2,1)} %refs_12_.1), channel_id=1, source_target_pairs={{0,24},{4,28},{8,0},{12,4},{16,8},{20,12},{24,16},{28,20},{1,25},{... | collective-permute-start | bytes 3145736 | tf_op jit(solution)/shard_map/right_two_up/ppermute | solution.py:22
  12.8 0.0 collective-permute-start.11
  12.9 0.0 collective-permute-done.4.head_ref.refs_3_.refs_9_
  12.9 0.1 extend.1
  12.9 0.0 copy-start.10
  12.9 1.3 %collective-permute-start.5 = (bf16[3088,128]{1,0:T(8,128)(2,1)S(1)}, bf16[3088,128]{1,0:T(8,128)(2,1)S(1)}, u32[]{:S(2)}, u32[]{:S(2)}) collective-permute-start(bf16[3088,128]{1,0:T(8,128)(2,1)S(1)} %extend.1), channel_id=1, source_target_pairs={{1,0},{2,3},{5,4},{6,7},{9,8},{10,11},{13,12},{14,15},{17,16},{18,... | collective-permute-start | bytes 2371592 | tf_op jit(solution)/shard_map/second_head_outward/ppermute | solution.py:469
  14.2 6.6 %collective-permute-done.3.refs_0_.refs_5_ = bf16[2064,128]{1,0:T(8,128)(2,1)S(1)} collective-permute-done((bf16[2064,128]{1,0:T(8,128)(2,1)S(1)}, bf16[2064,128]{1,0:T(8,128)(2,1)S(1)}, u32[]{:S(2)}, u32[]{:S(2)}) %collective-permute-start.3) | collective-permute-done | bytes 528416 | tf_op jit(solution)/shard_map/head_end_swap/ppermute | solution.py:472
  20.9 0.7 collective-permute-start.6
  21.5 6.3 %collective-permute-done.8.refs_0_.more_ref.refs_8_ = bf16[1536,128]{1,0:T(8,128)(2,1)S(1)} collective-permute-done((bf16[1536,128]{1,0:T(8,128)(2,1)S(1)}, bf16[1536,128]{1,0:T(8,128)(2,1)S(1)}, u32[]{:S(2)}, u32[]{:S(2)}) %collective-permute-start.8) | collective-permute-done | bytes 393248 | tf_op jit(solution)/shard_map/tail_inward/ppermute | solution.py:475
  27.8 0.0 collective-permute-done.6.refs_4_.refs_0_.refs_10_
  27.8 0.7 %pool.2 = bf16[2304,128]{1,0:T(8,128)(2,1)S(1)} custom-call(s32[1]{0:T(128)} %get-tuple-element.168.n_ref, bf16[2048,128]{1,0:T(8,128)(2,1)S(1)} %get-tuple-element.166.tail_ref, bf16[1536,128]{1,0:T(8,128)(2,1)S(1)} %collective-permute-done.8.refs_0_.more_ref.refs_8_, bf16[2064,128]{1,0:T(8,128)(2,1)S(1)} %collective-permute-done.6.refs_4_.refs_0_.refs_10_, ...), custom_call_target="tpu_custom_call" | custom-call | bytes 1769472 | tf_op jit(solution)/shard_map/pool/pallas_call | solution.py:518
  28.6 0.7 collective-permute-start.9
  29.3 1.3 %collective-permute-start.7 = (bf16[2064,128]{1,0:T(8,128)(2,1)S(1)}, bf16[2064,128]{1,0:T(8,128)(2,1)S(1)}, u32[]{:S(2)}, u32[]{:S(2)}) collective-permute-start(bf16[2064,128]{1,0:T(8,128)(2,1)S(1)} %collective-permute-done.6.refs_4_.refs_0_.refs_10_), channel_id=1, source_target_pairs={{1,0},{2,3},{5,4},{6,7},{9,8},{10,11},{13,12},{14,15},{17,16},{18,... | collective-permute-start | bytes 1585160 | tf_op jit(solution)/shard_map/third_head_outward/ppermute | solution.py:469
  30.6 0.1 pad_add_fusion.where_ref
  30.6 4.4 %collective-permute-done.10.refs_0_.refs_1_ = bf16[4,8,128,128]{3,2,1,0:T(8,128)(2,1)} collective-permute-done((bf16[4,8,128,128]{3,2,1,0:T(8,128)(2,1)}, bf16[4,8,128,128]{3,2,1,0:T(8,128)(2,1)}, u32[]{:S(2)}, u32[]{:S(2)}) %collective-permute-start.10) | collective-permute-done | bytes 1048608 | tf_op jit(solution)/shard_map/right_two_up/ppermute | solution.py:22
  35.1 0.0 copy-done.10
  35.1 3.4 %collective-permute-start.13 = (s32[4,8]{1,0:T(4,128)S(1)}, s32[4,8]{1,0:T(4,128)S(1)}, u32[]{:S(2)}, u32[]{:S(2)}) collective-permute-start(s32[4,8]{1,0:T(4,128)S(1)} %copy-done.10), channel_id=1, source_target_pairs={{0,24},{4,28},{8,0},{12,4},{16,8},{20,12},{24,16},{28,20},{1,25},{... | collective-permute-start | bytes 392 | tf_op jit(solution)/shard_map/right_masks/ppermute | solution.py:22
  38.5 1.3 %collective-permute-done.13.refs_6_.refs_2_.refs_1_ = s32[4,8]{1,0:T(4,128)S(1)} collective-permute-done((s32[4,8]{1,0:T(4,128)S(1)}, s32[4,8]{1,0:T(4,128)S(1)}, u32[]{:S(2)}, u32[]{:S(2)}) %collective-permute-start.13) | collective-permute-done | bytes 160 | tf_op jit(solution)/shard_map/right_masks/ppermute | solution.py:22
  39.8 0.0 collective-permute-start.12
  39.8 0.0 collective-permute-done.5.refs_1_.refs_0_.refs_6_
  39.8 0.5 collective-permute-start.14
  40.3 0.8 %collective-permute-done.12.refs_5_.refs_1_.refs_0_ = s32[4,8]{1,0:T(4,128)S(1)} collective-permute-done((s32[4,8]{1,0:T(4,128)S(1)}, s32[4,8]{1,0:T(4,128)S(1)}, u32[]{:S(2)}, u32[]{:S(2)}) %collective-permute-start.12) | collective-permute-done | bytes 160 | tf_op jit(solution)/shard_map/right_masks/ppermute | solution.py:484
  41.1 0.0 collective-permute-done.14.refs_7_.refs_3_.refs_2_
  41.2 0.0 collective-permute-done.11.refs_4_.refs_13_.refs_3_
  41.2 0.0 collective-permute-done.9.refs_0_
  41.2 0.7 %pool.3 = bf16[2304,128]{1,0:T(8,128)(2,1)S(1)} custom-call(s32[1]{0:T(128)} %get-tuple-element.168.n_ref, bf16[2048,128]{1,0:T(8,128)(2,1)S(1)} %get-tuple-element.166.tail_ref, bf16[2304,128]{1,0:T(8,128)(2,1)S(1)} %get-tuple-element.170.more_ref.refs_11_), custom_call_target="tpu_custom_call" | custom-call | bytes 1769472 | tf_op jit(solution)/shard_map/pool/pallas_call | solution.py:518
  41.9 1.3 %collective-permute-start.15 = (bf16[2304,128]{1,0:T(8,128)(2,1)S(1)}, bf16[2304,128]{1,0:T(8,128)(2,1)S(1)}, u32[]{:S(2)}, u32[]{:S(2)}) collective-permute-start(bf16[2304,128]{1,0:T(8,128)(2,1)S(1)} %pool.3), channel_id=1, source_target_pairs={{1,0},{2,3},{5,4},{6,7},{9,8},{10,11},{13,12},{14,15},{17,16},{18,... | collective-permute-start | bytes 1769480 | tf_op jit(solution)/shard_map/pool_outward/ppermute | solution.py:469
  43.2 0.0 copy-start.9
  43.2 1.0 %collective-permute-start.16 = (bf16[4,8,128,128]{3,2,1,0:T(8,128)(2,1)}, bf16[4,8,128,128]{3,2,1,0:T(8,128)(2,1)S(1)}, u32[]{:S(2)}, u32[]{:S(2)}) collective-permute-start(bf16[4,8,128,128]{3,2,1,0:T(8,128)(2,1)} %get-tuple-element.298.refs_14_.refs_4_), channel_id=1, source_target_pairs={{0,4},{4,0},{8,12},{12,8},{16,20},{20,16},{24,28},{28,24},{1,5},{5... | collective-permute-start | bytes 3145736 | tf_op jit(solution)/shard_map/right_core_swap/ppermute | solution.py:487
  44.2 7.9 %collective-permute-done.7.refs_0_.refs_2_.refs_7_ = bf16[2064,128]{1,0:T(8,128)(2,1)S(1)} collective-permute-done((bf16[2064,128]{1,0:T(8,128)(2,1)S(1)}, bf16[2064,128]{1,0:T(8,128)(2,1)S(1)}, u32[]{:S(2)}, u32[]{:S(2)}) %collective-permute-start.7) | collective-permute-done | bytes 528416 | tf_op jit(solution)/shard_map/third_head_outward/ppermute | solution.py:469
  52.1 0.0 copy-done.9
  52.1 0.0 copy-start.8
  52.1 3.1 %table.1 = (s32[200]{0:T(256)S(1)}, s32[1]{0:T(128)}) custom-call(s32[2]{0:T(128)S(1)} %pad_add_fusion.where_ref, s32[4,8]{1,0:T(4,128)S(1)} %bitcast.5, bf16[2064,128]{1,0:T(8,128)(2,1)S(1)} %collective-permute-done.3.refs_0_.refs_5_, bf16[3088,128]{1,0:T(8,128)(2,1)S(1)} %collective-permute-done.5.refs_1_.refs_0_.refs_6_, ...), custom_call_target="tpu_custom_call" | custom-call | tf_op jit(solution)/shard_map/table/pallas_call | solution.py:562
  55.2 0.0 collective-permute-done.16.refs_15_.refs_5_
  55.2 0.0 copy-start.2
  55.2 0.0 copy-done.4
  55.2 0.0 copy-done.6
  55.2 0.0 copy-done.8
  55.3 8.9 %early.1 = (f32[1024,1024]{1,0:T(8,128)S(1)}, bf16[8,8,128,128]{3,2,1,0:T(8,128)(2,1)}) custom-call(s32[2]{0:T(128)S(1)} %pad_add_fusion.where_ref, s32[4,8]{1,0:T(4,128)S(1)} %bitcast.6, s32[8,8]{1,0:T(8,128)S(1)} %copy-done.8, s32[200]{0:T(256)S(1)} %get-tuple-element.167.table_ref, s32[4,8]{1,0:T(4,128)S(1)} %copy-done.10, ...), custom_call_target="tpu_custom_call" | custom-call | flops 4294967296 | bytes 14680064 | tf_op jit(solution)/shard_map/early/pallas_call | solution.py:583
  64.1 0.0 copy-done
  64.1 2.2 %rows.1.rows_ref = bf16[1536,1024]{1,0:T(8,128)(2,1)S(1)} custom-call(s32[2]{0:T(128)S(1)} %pad_add_fusion.where_ref, s32[200]{0:T(256)S(1)} %get-tuple-element.167.table_ref, s32[4,8]{1,0:T(4,128)S(1)} %collective-permute-done.12.refs_5_.refs_1_.refs_0_, s32[4,8]{1,0:T(4,128)S(1)} %collective-permute-done.13.refs_6_.refs_2_.refs_1_, ...), custom_call_target="tpu_custom_call" | custom-call | bytes 1048576 | tf_op jit(solution)/shard_map/rows/pallas_call | solution.py:604
  66.4 0.0 collective-permute-done.15.late_ref
  66.4 4.7 %late.1 = bf16[8,8,128,128]{3,2,1,0:T(8,128)(2,1)} custom-call(s32[2]{0:T(128)S(1)} %pad_add_fusion.where_ref, s32[8,8]{1,0:T(8,128)S(1)} %copy-done.8, s32[200]{0:T(256)S(1)} %get-tuple-element.167.table_ref, bf16[2304,128]{1,0:T(8,128)(2,1)S(1)} %collective-permute-done.15.late_ref, ...), custom_call_target="tpu_custom_call", output_to_operand_aliasing={{}: (6, {})} | custom-call | bytes 4194304 | tf_op jit(solution)/shard_map/late/pallas_call | solution.py:620
  71.1 0.7 while.12
  (9 shorter events, 0.0 us)
Async XLA Ops:
  1.8 11.0 %collective-permute-start.4 = (bf16[2064,128]{1,0:T(8,128)(2,1)S(1)}, bf16[2064,128]{1,0:T(8,128)(2,1)S(1)}, u32[]{:S(2)}, u32[]{:S(2)}) collective-permute-start(bf16[2064,128]{1,0:T(8,128)(2,1)S(1)} %get-tuple-element.165), channel_id=1, source_target_pairs={{1,2},{2,1},{5,6},{6,5},{9,10},{10,9},{13,14},{14,13},{17,18},{18,... | collective-permute-start | bytes 1585160 | tf_op jit(solution)/shard_map/head_over_middle/ppermute | solution.py:478
  2.5 18.3 %collective-permute-start.3 = (bf16[2064,128]{1,0:T(8,128)(2,1)S(1)}, bf16[2064,128]{1,0:T(8,128)(2,1)S(1)}, u32[]{:S(2)}, u32[]{:S(2)}) collective-permute-start(bf16[2064,128]{1,0:T(8,128)(2,1)S(1)} %get-tuple-element.165), channel_id=1, source_target_pairs={{0,1},{1,0},{2,3},{3,2},{4,5},{5,4},{6,7},{7,6},{8,9},{9,8},{10,11... | collective-permute-start | bytes 1585160 | tf_op jit(solution)/shard_map/head_end_swap/ppermute | solution.py:472
  8.4 19.4 %collective-permute-start.8 = (bf16[1536,128]{1,0:T(8,128)(2,1)S(1)}, bf16[1536,128]{1,0:T(8,128)(2,1)S(1)}, u32[]{:S(2)}, u32[]{:S(2)}) collective-permute-start(bf16[1536,128]{1,0:T(8,128)(2,1)S(1)} %get-tuple-element.169), channel_id=1, source_target_pairs={{0,1},{3,2},{4,5},{7,6},{8,9},{11,10},{12,13},{15,14},{16,17},{19,... | collective-permute-start | bytes 1179656 | tf_op jit(solution)/shard_map/tail_inward/ppermute | solution.py:475
  10.3 24.7 %collective-permute-start.10 = (bf16[4,8,128,128]{3,2,1,0:T(8,128)(2,1)}, bf16[4,8,128,128]{3,2,1,0:T(8,128)(2,1)}, u32[]{:S(2)}, u32[]{:S(2)}) collective-permute-start(bf16[4,8,128,128]{3,2,1,0:T(8,128)(2,1)} %refs_12_.1), channel_id=1, source_target_pairs={{0,24},{4,28},{8,0},{12,4},{16,8},{20,12},{24,16},{28,20},{1,25},{... | collective-permute-start | bytes 3145736 | tf_op jit(solution)/shard_map/right_two_up/ppermute | solution.py:22
  12.8 28.3 %collective-permute-start.11 = (bf16[4,8,128,128]{3,2,1,0:T(8,128)(2,1)}, bf16[4,8,128,128]{3,2,1,0:T(8,128)(2,1)S(1)}, u32[]{:S(2)}, u32[]{:S(2)}) collective-permute-start(bf16[4,8,128,128]{3,2,1,0:T(8,128)(2,1)} %refs_12_.1), channel_id=1, source_target_pairs={{4,0},{16,4},{12,8},{24,12},{20,16},{0,20},{28,24},{8,28},{5,1},{1... | collective-permute-start | bytes 3145736 | tf_op jit(solution)/shard_map/right_odd_up/ppermute | solution.py:484
  12.9 22.2 %copy-start.10 = (s32[4,8]{1,0:T(4,128)S(1)}, s32[4,8]{1,0:T(4,128)}, u32[]{:S(2)}) copy-start(s32[4,8]{1,0:T(4,128)} %refs_0_.1) | copy-start | bytes 388
  12.9 26.9 %collective-permute-start.5 = (bf16[3088,128]{1,0:T(8,128)(2,1)S(1)}, bf16[3088,128]{1,0:T(8,128)(2,1)S(1)}, u32[]{:S(2)}, u32[]{:S(2)}) collective-permute-start(bf16[3088,128]{1,0:T(8,128)(2,1)S(1)} %extend.1), channel_id=1, source_target_pairs={{1,0},{2,3},{5,4},{6,7},{9,8},{10,11},{13,12},{14,15},{17,16},{18,... | collective-permute-start | bytes 2371592 | tf_op jit(solution)/shard_map/second_head_outward/ppermute | solution.py:469
  20.9 7.0 %collective-permute-start.6 = (bf16[2064,128]{1,0:T(8,128)(2,1)S(1)}, bf16[2064,128]{1,0:T(8,128)(2,1)S(1)}, u32[]{:S(2)}, u32[]{:S(2)}) collective-permute-start(bf16[2064,128]{1,0:T(8,128)(2,1)S(1)} %collective-permute-done.3.refs_0_.refs_5_), channel_id=1, source_target_pairs={{1,2},{2,1},{5,6},{6,5},{9,10},{10,9},{13,14},{14,13},{17,18},{18,... | collective-permute-start | bytes 1585160 | tf_op jit(solution)/shard_map/end_head_over_middle/ppermute | solution.py:478
  28.6 12.6 %collective-permute-start.9 = (bf16[2304,128]{1,0:T(8,128)(2,1)S(1)}, bf16[2304,128]{1,0:T(8,128)(2,1)S(1)}, u32[]{:S(2)}, u32[]{:S(2)}) collective-permute-start(bf16[2304,128]{1,0:T(8,128)(2,1)S(1)} %pool.2), channel_id=1, source_target_pairs={{1,2},{2,1},{5,6},{6,5},{9,10},{10,9},{13,14},{14,13},{17,18},{18,... | collective-permute-start | bytes 1769480 | tf_op jit(solution)/shard_map/pool_over_middle/ppermute | solution.py:478
  29.3 22.8 %collective-permute-start.7 = (bf16[2064,128]{1,0:T(8,128)(2,1)S(1)}, bf16[2064,128]{1,0:T(8,128)(2,1)S(1)}, u32[]{:S(2)}, u32[]{:S(2)}) collective-permute-start(bf16[2064,128]{1,0:T(8,128)(2,1)S(1)} %collective-permute-done.6.refs_4_.refs_0_.refs_10_), channel_id=1, source_target_pairs={{1,0},{2,3},{5,4},{6,7},{9,8},{10,11},{13,12},{14,15},{17,16},{18,... | collective-permute-start | bytes 1585160 | tf_op jit(solution)/shard_map/third_head_outward/ppermute | solution.py:469
  35.1 4.8 %collective-permute-start.13 = (s32[4,8]{1,0:T(4,128)S(1)}, s32[4,8]{1,0:T(4,128)S(1)}, u32[]{:S(2)}, u32[]{:S(2)}) collective-permute-start(s32[4,8]{1,0:T(4,128)S(1)} %copy-done.10), channel_id=1, source_target_pairs={{0,24},{4,28},{8,0},{12,4},{16,8},{20,12},{24,16},{28,20},{1,25},{... | collective-permute-start | bytes 392 | tf_op jit(solution)/shard_map/right_masks/ppermute | solution.py:22
  39.8 1.3 %collective-permute-start.12 = (s32[4,8]{1,0:T(4,128)S(1)}, s32[4,8]{1,0:T(4,128)S(1)}, u32[]{:S(2)}, u32[]{:S(2)}) collective-permute-start(s32[4,8]{1,0:T(4,128)S(1)} %copy-done.10), channel_id=1, source_target_pairs={{4,0},{16,4},{12,8},{24,12},{20,16},{0,20},{28,24},{8,28},{5,1},{1... | collective-permute-start | bytes 392 | tf_op jit(solution)/shard_map/right_masks/ppermute | solution.py:484
  39.8 1.3 %collective-permute-start.14 = (s32[4,8]{1,0:T(4,128)S(1)}, s32[4,8]{1,0:T(4,128)S(1)}, u32[]{:S(2)}, u32[]{:S(2)}) collective-permute-start(s32[4,8]{1,0:T(4,128)S(1)} %collective-permute-done.13.refs_6_.refs_2_.refs_1_), channel_id=1, source_target_pairs={{0,4},{4,0},{8,12},{12,8},{16,20},{20,16},{24,28},{28,24},{1,5},{5... | collective-permute-start | bytes 392 | tf_op jit(solution)/shard_map/right_masks/ppermute | solution.py:487
  41.2 23.0 %copy-start = (bf16[4,8,128,128]{3,2,1,0:T(8,128)(2,1)}, bf16[4,8,128,128]{3,2,1,0:T(8,128)(2,1)S(1)}, u32[]{:S(2)}) copy-start(bf16[4,8,128,128]{3,2,1,0:T(8,128)(2,1)S(1)} %collective-permute-done.11.refs_4_.refs_13_.refs_3_) | copy-start | bytes 3145732
  41.9 24.5 %collective-permute-start.15 = (bf16[2304,128]{1,0:T(8,128)(2,1)S(1)}, bf16[2304,128]{1,0:T(8,128)(2,1)S(1)}, u32[]{:S(2)}, u32[]{:S(2)}) collective-permute-start(bf16[2304,128]{1,0:T(8,128)(2,1)S(1)} %pool.3), channel_id=1, source_target_pairs={{1,0},{2,3},{5,4},{6,7},{9,8},{10,11},{13,12},{14,15},{17,16},{18,... | collective-permute-start | bytes 1769480 | tf_op jit(solution)/shard_map/pool_outward/ppermute | solution.py:469
  43.2 8.9 %copy-start.9 = (s32[8,4]{0,1:T(4,128)S(1)}, s32[8,4]{0,1:T(4,128)}, u32[]{:S(2)}) copy-start(s32[8,4]{0,1:T(4,128)} %param.8) | copy-start | bytes 388
  43.2 12.0 %collective-permute-start.16 = (bf16[4,8,128,128]{3,2,1,0:T(8,128)(2,1)}, bf16[4,8,128,128]{3,2,1,0:T(8,128)(2,1)S(1)}, u32[]{:S(2)}, u32[]{:S(2)}) collective-permute-start(bf16[4,8,128,128]{3,2,1,0:T(8,128)(2,1)} %get-tuple-element.298.refs_14_.refs_4_), channel_id=1, source_target_pairs={{0,4},{4,0},{8,12},{12,8},{16,20},{20,16},{24,28},{28,24},{1,5},{5... | collective-permute-start | bytes 3145736 | tf_op jit(solution)/shard_map/right_core_swap/ppermute | solution.py:487
  52.1 3.2 %copy-start.4 = (bf16[8,4,128,128]{3,2,1,0:T(8,128)(2,1)S(1)}, bf16[8,4,128,128]{3,2,1,0:T(8,128)(2,1)}, u32[]{:S(2)}) copy-start(bf16[8,4,128,128]{3,2,1,0:T(8,128)(2,1)} %refs_4_.1) | copy-start | bytes 3145732
  52.1 3.2 %copy-start.6 = (bf16[4,8,128,128]{3,2,1,0:T(8,128)(2,1)S(1)}, bf16[4,8,128,128]{3,2,1,0:T(8,128)(2,1)}, u32[]{:S(2)}) copy-start(bf16[4,8,128,128]{3,2,1,0:T(8,128)(2,1)} %refs_12_.1) | copy-start | bytes 3145732
  52.1 3.2 %copy-start.8 = (s32[8,8]{1,0:T(8,128)S(1)}, s32[8,8]{1,0:T(8,128)}, u32[]{:S(2)}) copy-start(s32[8,8]{1,0:T(8,128)} %c_ref.3) | copy-start | bytes 772
  55.2 8.9 %copy-start.2 = (bf16[4,8,128,128]{3,2,1,0:T(8,128)(2,1)}, bf16[4,8,128,128]{3,2,1,0:T(8,128)(2,1)S(1)}, u32[]{:S(2)}) copy-start(bf16[4,8,128,128]{3,2,1,0:T(8,128)(2,1)S(1)} %collective-permute-done.16.refs_15_.refs_5_) | copy-start | bytes 3145732

commit v6 on v5

--- a/solution.py
+++ b/solution.py
@@ -8,7 +8,8 @@
 from jax.sharding import PartitionSpec as P
 
 STEPS = 4
-T_TAIL, T_SECOND, T_THIRD, T_RIGHT = 7, 4, 12, 1
+T_TAIL, T_SECOND, T_THIRD, T_RIGHT = 4, 4, 12, 1
+GROUP = 3
 NOTE = 16
 MIB = 1024 * 1024
 
@@ -192,19 +193,20 @@
     out_ref[size + more :, :] = head_ref[size:, :]
 
 
-def pool_kernel(skip, n_ref, tail_ref, more_ref, *refs):
-    out_ref, line = refs[-2:]
-    blk = out_ref.shape[1]
+def pool_kernel(parts, skip, n_ref, tail_ref, more_ref, *refs):
+    outs, line = refs[-1 - parts : -1], refs[-1]
+    size, blk = outs[0].shape
     first = skip * blk - tail_ref.shape[0]
     own = tail_ref.shape[0] - first
     line[0:own, :] = tail_ref[first:, :]
     at = pl.multiple_of(jnp.maximum(n_ref[0] - skip, 0) * blk, blk)
     line[pl.ds(at, more_ref.shape[0]), :] = more_ref[...]
-    out_ref[...] = line[0 : out_ref.shape[0], :]
-
-
-def table_kernel(blocks, where_ref, own_ref, *refs):
-    notes, (table_ref, over_ref, note_ref, wide_ref, mask_ref, sems, sem) = refs[:5], refs[6:]
+    for part, out_ref in enumerate(outs):
+        out_ref[...] = line[part * size : (part + 1) * size, :]
+
+
+def table_kernel(blocks, where_ref, own_ref, far_ref, *refs):
+    notes, (table_ref, over_ref, note_ref, wide_ref, mask_ref, sems, sem) = refs[:4], refs[4:]
     copies = [
         pltpu.make_async_copy(
             ref.at[pl.ds(ref.shape[0] - NOTE, NOTE), :], note_ref.at[pl.ds(m * NOTE, NOTE), :], sems.at[m]
@@ -215,7 +217,8 @@
         copy.start()
     for copy in copies:
         copy.wait()
-    wide_ref[...] = note_ref[...].astype(jnp.float32).astype(jnp.int32)
+    for m in range(len(notes)):
+        wide_ref[m : m + 1, :] = note_ref[m * NOTE : m * NOTE + 1, :].astype(jnp.float32).astype(jnp.int32)
     down = pltpu.make_async_copy(wide_ref, mask_ref, sem)
     down.start()
     down.wait()
@@ -230,10 +233,16 @@
     def place_of(step):
         return jnp.where(flip, 4 - step, step)
 
-    def fill(base, place, m):
+    def noted(m):
+        return lambda b: mask_ref[m, b]
+
+    def far(b):
+        return jnp.where(at_end, far_ref[b // own_ref.shape[1], b % own_ref.shape[1]], mask_ref[3, b])
+
+    def fill(base, place, live):
         def body(b, count):
             table_ref[count] = place * blocks + b
-            return count + mask_ref[m * NOTE, b]
+            return count + live(b)
 
         count = lax.fori_loop(0, blocks, body, jnp.int32(base), unroll=8)
 
@@ -244,9 +253,9 @@
         lax.fori_loop(count, base + blocks, pad, 0)
         return count - base
 
-    first = fill(0, place_of(near), 0)
-    second = fill(apart, jnp.where(at_end, 2, place_of(4 - near)), jnp.where(at_end, 1, 3))
-    third = fill(2 * apart, jnp.where(at_end, place_of(4 - near), 2), jnp.where(at_end, 2, 4))
+    first = fill(0, place_of(near), noted(0))
+    second = fill(apart, jnp.where(at_end, 2, place_of(4 - near)), noted(jnp.where(at_end, 1, 2)))
+    third = fill(2 * apart, jnp.where(at_end, place_of(4 - near), 2), far)
 
     def append(base, begin, length, at):
         def body(p, at):
@@ -293,7 +302,7 @@
 
 def early_kernel(where_ref, mask_ref, c_ref, table_ref, *refs):
     b_masks, a_ref, refs = refs[:STEPS], refs[STEPS], refs[STEPS + 1 :]
-    near_ref, outs, mids, refs = refs[0], refs[1:3], refs[3:7], refs[7:]
+    near_ref, outs, mids, refs = refs[0], refs[1:3], refs[3:7], refs[7:-5] + refs[-3:]
     b_refs, (acc_ref, out_ref, left_ref) = refs[:STEPS], refs[STEPS:]
     br, kb, blk, _ = a_ref.shape
     blocks = br * kb
@@ -352,7 +361,7 @@
 
 def rows_kernel(where_ref, table_ref, *refs):
     b_masks, refs = refs[: STEPS - 1], refs[STEPS - 1 :]
-    b_refs, (rows_ref, b_ref, need_ref, sems) = refs[: STEPS - 1], refs[STEPS:]
+    b_refs, (rows_ref, b_ref, need_ref, sems) = refs[: STEPS - 1], refs[STEPS - 1 :]
     _, bc, blk, _ = b_ref.shape
     kb = b_refs[0].shape[0]
     br = (table_ref.shape[0] // 5 - 8) // kb
@@ -404,55 +413,70 @@
         lax.fori_loop(0, kb, fill, 0)
 
 
-def late_kernel(where_ref, c_ref, table_ref, late_ref, acc_ref, rows_ref, _, out_ref, row_ref, touched_ref, sems):
+def late_kernel(begin, where_ref, c_ref, table_ref, late_ref, rows_ref, acc_in, _, out_ref, acc_ref, row_ref, last_ref, sems):
+    del acc_in
     br, bc, blk, _ = out_ref.shape
     kb = rows_ref.shape[0] // blk // (STEPS - 1)
-    _, _, _, pool = slots(kb * br)
-    first = 3 * (kb * br + 8)
+    none = STEPS * kb * br
+    size = late_ref.shape[0] // blk
+    first = 3 * (kb * br + 8) + begin
     at_end = jnp.logical_or(where_ref[0] == 0, where_ref[0] == 3)
 
     def clear(i, carry):
-        touched_ref[i] = 0
+        last_ref[i] = -1
         return carry
 
-    def add(b, carry):
+    def mark(b, live):
         place = table_ref[first + b]
 
-        @pl.when(place < STEPS * kb * br)
+        @pl.when(place < none)
         def _():
-            i, r = place % br, place // br - kb
-            touched_ref[i] = 1
-            acc_ref[pl.ds(pl.multiple_of(i * blk, blk), blk), :] += jnp.dot(
-                late_ref[pl.ds(pl.multiple_of(b * blk, blk), blk), :],
-                rows_ref[pl.ds(pl.multiple_of(r * blk, blk), blk), :],
-                preferred_element_type=jnp.float32,
-            )
-
-        return carry
+            last_ref[place % br] = b
+
+        return live + jnp.where(place < none, 1, 0)
 
     def go(i):
         return pltpu.make_async_copy(row_ref.at[i], out_ref.at[i], sems.at[i])
 
-    def send(i, carry):
-        @pl.when(touched_ref[i] > 0)
-        def _():
+    def add(group, carry):
+        b0 = group * GROUP
+        places = [table_ref[first + b0 + x] for x in range(GROUP)]
+        products = []
+        for x, place in enumerate(places):
+            r = jnp.minimum(place // br - kb, (STEPS - 1) * kb - 1)
+            products.append(
+                jnp.dot(
+                    late_ref[pl.ds(pl.multiple_of((b0 + x) * blk, blk), blk), :],
+                    rows_ref[pl.ds(pl.multiple_of(r * blk, blk), blk), :],
+                    preferred_element_type=jnp.float32,
+                )
+            )
+        for x, (place, product) in enumerate(zip(places, products)):
+            i = place % br
             row = pl.multiple_of(i * blk, blk)
-            for j in range(bc):
-                row_ref[i, j] = filtered(c_ref, i, j, acc_ref[pl.ds(row, blk), j * blk : (j + 1) * blk])
-            go(i).start()
+
+            @pl.when(place < none)
+            def _():
+                acc_ref[pl.ds(row, blk), :] += product
+
+            @pl.when(jnp.logical_and(place < none, last_ref[i] == b0 + x))
+            def _():
+                for j in range(bc):
+                    row_ref[i, j] = filtered(c_ref, i, j, acc_ref[pl.ds(row, blk), j * blk : (j + 1) * blk])
+                go(i).start()
 
         return carry
 
     def settle(i, carry):
-        @pl.when(touched_ref[i] > 0)
+        @pl.when(last_ref[i] >= 0)
         def _():
             go(i).wait()
 
         return carry
 
     lax.fori_loop(0, br, clear, 0)
-    lax.fori_loop(0, jnp.where(at_end, pool, 0), add, 0)
-    lax.fori_loop(0, br, send, 0)
+    live = lax.fori_loop(0, jnp.where(at_end, size, 0), mark, jnp.int32(0))
+    lax.fori_loop(0, (live + GROUP - 1) // GROUP, add, 0)
     lax.fori_loop(0, br, settle, 0)
 
 
@@ -513,13 +537,13 @@
         name="compact",
     )(by_column, a_blocks)
 
-    def pooled(skip, more, seen):
+    def pooled(skip, more, seen, parts=1):
         own = blocks - skip
         return pl.pallas_call(
-            functools.partial(pool_kernel, skip),
+            functools.partial(pool_kernel, parts, skip),
             in_specs=[smem(), whole(), whole()] + [anywhere()] * len(seen),
-            out_specs=whole(),
-            out_shape=listed(pool),
+            out_specs=[whole()] * parts,
+            out_shape=[listed(pool // parts)] * parts,
             scratch_shapes=[pltpu.VMEM((own * blk + more.shape[0], blk), a_blocks.dtype)],
             compiler_params=params(),
             cost_estimate=cost(0, 6 * pool * blk * blk),
@@ -548,32 +572,51 @@
         end_head = over_middle(near_head)
     with jax.named_scope("third_head_outward"):
         third_head = outward(end_head)
-    mid_pool = pooled(head, near_tail, [end_head, token([near_tail], T_TAIL)])
+    (mid_pool,) = pooled(head, near_tail, [end_head, token([near_tail], T_TAIL)])
+    with jax.named_scope("far_mask"):
+        far_mask = lax.ppermute(*passed([a_mask.T], [mid_pool]), "col", [(0, 3), (3, 0)])
     with jax.named_scope("pool_over_middle"):
         mid_pool = over_middle(mid_pool)
-    here = [token([second_head], T_SECOND), token([second], T_RIGHT), odd_one] + b_masks[1:]
-    mid_pool, second = passed([mid_pool, second], here)
-    out_pool = pooled(lead, mid_pool, [])
-    with jax.named_scope("pool_outward"):
-        out_pool = outward(out_pool)
-    with jax.named_scope("right_core_swap"):
-        right = [b_blocks, odd_one, second, core_swap(second)]
-
     table, over = pl.pallas_call(
         functools.partial(table_kernel, blocks),
-        in_specs=[smem(), smem()] + [anywhere()] * 6,
+        in_specs=[smem()] * 3 + [anywhere()] * 4,
         out_specs=[smem(), smem()],
         out_shape=[jax.ShapeDtypeStruct((5 * (blocks + 8),), jnp.int32), jax.ShapeDtypeStruct((1,), jnp.int32)],
         scratch_shapes=[
-            pltpu.VMEM((5 * NOTE, blk), jnp.bfloat16),
-            pltpu.VMEM((5 * NOTE, blk), jnp.int32),
-            pltpu.SMEM((5 * NOTE, blk), jnp.int32),
-            pltpu.SemaphoreType.DMA((5,)),
+            pltpu.VMEM((4 * NOTE, blk), jnp.bfloat16),
+            pltpu.VMEM((8, blk), jnp.int32),
+            pltpu.SMEM((8, blk), jnp.int32),
+            pltpu.SemaphoreType.DMA((4,)),
             pltpu.SemaphoreType.DMA,
         ],
         compiler_params=params(),
         name="table",
-    )(where, by_column, near_head, second_head, third_head, mid_head, end_head, token([third_head], T_THIRD))
+    )(where, by_column, far_mask, near_head, second_head, mid_head, end_head)
+
+    here = [table, token([second_head], T_SECOND), token([second], T_RIGHT), odd_one] + b_masks[1:]
+    mid_pool, second = passed([mid_pool, second], here)
+    out_pools = pooled(lead, mid_pool, [])
+    with jax.named_scope("pool_outward"):
+        out_pools = [outward(part) for part in out_pools]
+    with jax.named_scope("right_core_swap"):
+        right = [b_blocks, odd_one, second, core_swap(second)]
+
+    rows_shape = jax.ShapeDtypeStruct(((STEPS - 1) * kb * blk, bc * blk), jnp.bfloat16)
+    met = pl.pallas_call(
+        rows_kernel,
+        in_specs=[smem()] * (2 + STEPS - 1) + [anywhere()] * (STEPS - 1),
+        out_specs=whole(),
+        out_shape=rows_shape,
+        scratch_shapes=[
+            pltpu.VMEM(((STEPS - 1) * kb, bc, blk, blk), jnp.bfloat16),
+            pltpu.SMEM(((STEPS - 1) * kb,), jnp.int32),
+            pltpu.SemaphoreType.DMA(((STEPS - 1) * kb,)),
+        ],
+        compiler_params=params(12),
+        cost_estimate=cost(0, 1 << 20),
+        name="rows",
+    )(where, table, *b_masks[1:], *right[1:])
+    third_here = token([third_head], T_THIRD)
 
     def fixed(x):
         return pl.BlockSpec(x.shape, lambda g: (0,) * x.ndim)
@@ -585,7 +628,8 @@
         grid=(bc // wide_j,),
         in_specs=[smem()] * (4 + STEPS)
         + [fixed(x) for x in [a_blocks] + arrived]
-        + [pl.BlockSpec((kb, wide_j, blk, blk), lambda g: (0, g, 0, 0))] * STEPS,
+        + [pl.BlockSpec((kb, wide_j, blk, blk), lambda g: (0, g, 0, 0))] * STEPS
+        + [anywhere()] * 2,
         out_specs=[
             pl.BlockSpec((br * blk, wide_j * blk), lambda g: (0, g)),
             pl.BlockSpec((br, wide_j, blk, blk), lambda g: (0, g, 0, 0)),
@@ -598,60 +642,43 @@
         compiler_params=params(24),
         cost_estimate=cost(2 * STEPS * br * bc * kb * blk**3, 14 << 20),
         name="early",
-    )(where, by_column, c_mask, table, *b_masks, a_blocks, *arrived, *right)
-
-    rows_shape = jax.ShapeDtypeStruct(((STEPS - 1) * kb * blk, bc * blk), jnp.bfloat16)
-    met = pl.pallas_call(
-        rows_kernel,
-        in_specs=[smem()] * (2 + STEPS - 1) + [anywhere()] * STEPS,
-        out_specs=whole(),
-        out_shape=rows_shape,
-        scratch_shapes=[
-            pltpu.VMEM(((STEPS - 1) * kb, bc, blk, blk), jnp.bfloat16),
-            pltpu.SMEM(((STEPS - 1) * kb,), jnp.int32),
-            pltpu.SemaphoreType.DMA(((STEPS - 1) * kb,)),
-        ],
-        compiler_params=params(12),
-        cost_estimate=cost(0, 1 << 20),
-        name="rows",
-    )(where, table, *b_masks[1:], *right[1:], acc)
-
-    def rest(out, acc, late, met):
-        return pl.pallas_call(
-            late_kernel,
+    )(where, by_column, c_mask, table, *b_masks, a_blocks, *arrived, *right, met, third_here)
+
+    for part, late in enumerate(out_pools):
+        out, acc = pl.pallas_call(
+            functools.partial(late_kernel, part * (pool // len(out_pools))),
             in_specs=[smem()] * 3 + [whole()] * 3 + [anywhere()],
-            out_specs=anywhere(),
-            out_shape=jax.ShapeDtypeStruct((br, bc, blk, blk), jnp.bfloat16),
+            out_specs=[anywhere(), whole()],
+            out_shape=[
+                jax.ShapeDtypeStruct((br, bc, blk, blk), jnp.bfloat16),
+                jax.ShapeDtypeStruct(acc.shape, acc.dtype),
+            ],
             scratch_shapes=[
                 pltpu.VMEM((br, bc, blk, blk), jnp.bfloat16),
                 pltpu.SMEM((br,), jnp.int32),
                 pltpu.SemaphoreType.DMA((br,)),
             ],
-            input_output_aliases={6: 0},
+            input_output_aliases={5: 1, 6: 0},
             compiler_params=params(12),
-            cost_estimate=cost(0, 4 << 20),
+            cost_estimate=cost(0, 1 << 20),
             name="late",
-        )(where, c_mask, table, late, acc, met, out)
-
-    out = rest(out, acc, out_pool, met)
-
-    def again(state):
-        before, trips = state
+        )(where, c_mask, table, late, met, acc, out)
+
+    def again(before):
         left = [live(a_blocks, by_column, by_column=True, after=(before,))]
         for _ in range(1, STEPS):
             left.append(from_behind(left[-1], "col", -1))
         odd = lax.axis_index("row") % 2 == 1
         held = [live(slab, mask, after=(before,)) for slab, mask in zip(right, b_masks)]
         ordered = [held[0], jnp.where(odd, held[3], held[1]), held[2], jnp.where(odd, held[1], held[3])]
-        return filter_sum(dense_sum(left, ordered), c_mask, blk, before), trips - 1
-
-    out, _ = lax.while_loop(lambda state: state[1] > 0, again, (out, over[0]))
-    return out
+        return filter_sum(dense_sum(left, ordered), c_mask, blk, before)
+
+    return lax.cond(over[0] > 0, again, lambda before: before, out)
 
 
 def on_device(a_blocks, a_mask, b_blocks, b_mask, c_mask):
     blocks = a_blocks.shape[0] * a_blocks.shape[1]
-    fits = blocks % 16 == 0 and blocks <= a_blocks.shape[-1]
+    fits = blocks % 32 == 0 and blocks <= a_blocks.shape[-1]
     if lax.axis_size("col") == STEPS and lax.axis_size("row") % 2 == 0 and fits:
         return sparse_product(a_blocks, a_mask, b_blocks, b_mask, c_mask)
     return dense_product(a_blocks, a_mask, b_blocks, b_mask, c_mask)

time: 71.5 us -> 69.9 us (0.978)
  waiting for transfers between devices: 27.3 us -> 23.1 us
  starting transfers between devices: 21.2 us -> 22.7 us
  Pallas kernels: 22.3 us -> 23.7 us
    ppermute x2, waiting for transfers between devices: 5.72 us -> 1.21 us  [from_behind(): lax.ppermute(array, axis, [(i, (i + by) % size) for i in range(size)])]
    ppermute x0 -> x1, waiting for transfers between devices: none -> 4.11 us  [sparse_product(): lax.ppermute(*passed([a_mask.T], [mid_pool]), 'col', [(0, 3), (3, 0)])]
    ppermute x0 -> x1, starting transfers between devices: none -> 3.26 us  [sparse_product(): lax.ppermute(*passed([a_mask.T], [mid_pool]), 'col', [(0, 3), (3, 0)])]
    ppermute x3, waiting for transfers between devices: 7.87 us -> 4.85 us  [outward(): return lax.ppermute(x, 'col', [(1, 0), (2, 3)])]
    ppermute x2, starting transfers between devices: 5.94 us -> 4.89 us  [from_behind(): lax.ppermute(array, axis, [(i, (i + by) % size) for i in range(size)])]
    pallas_call x4, Pallas kernels: 9.32 us -> 10.2 us  [the longest x1 5.26 us: sparse_product(): pl.pallas_call(functools.partial(late_kernel, part * (pool // len(out_poo...]
    ppermute x2, waiting for transfers between devices: 0.8 us -> 0.01 us  [odd_up(): lax.ppermute(x, 'row', [((r + 1 + 2 * (r % 2)) % rows, r) for r in range(...]
    ppermute x2, starting transfers between devices: 1.47 us -> 0.69 us  [core_swap(): return lax.ppermute(x, 'row', [(r, r ^ 1) for r in range(rows)])]
  transfers between devices with their start and end apart: 14 -> 15, of which waited for: 6 -> 6; matrix products, arithmetic and copies ran while one was open for 0% -> 0% of each run, Pallas kernels for 22% -> 23%
where the time goes in v6:
time: 69.9 us; the launch traced here: 70.5 us
  Pallas kernels  23.7 us (34%)
  waiting for transfers between devices  23.1 us (33%)
  starting transfers between devices  22.7 us (32%)
  between operations  0.91 us (1%)
    pallas_call x1, Pallas kernels, sparse_product(): pl.pallas_call(early_kernel, grid=(bc // wide_j,), in_specs=[smem()] * (4...  8.92 us
    ppermute x1, waiting for transfers between devices, end_swap(): return lax.ppermute(x, 'col', [(0, 1), (1, 0), (2, 3), (3, 2)])  6.65 us
    ppermute x1, waiting for transfers between devices, inward(): return lax.ppermute(x, 'col', [(0, 1), (3, 2)])  6.29 us
    ppermute x1, starting transfers between devices, end_swap(): return lax.ppermute(x, 'col', [(0, 1), (1, 0), (2, 3), (3, 2)])  5.88 us
    pallas_call x1, Pallas kernels, sparse_product(): pl.pallas_call(functools.partial(late_kernel, part * (pool // len(out_poo...  5.26 us
    ppermute x2, starting transfers between devices, from_behind(): lax.ppermute(array, axis, [(i, (i + by) % size) for i in range(size)])  4.89 us
    ppermute x3, waiting for transfers between devices, outward(): return lax.ppermute(x, 'col', [(1, 0), (2, 3)])  4.85 us
    ppermute x1, waiting for transfers between devices, sparse_product(): lax.ppermute(*passed([a_mask.T], [mid_pool]), 'col', [(0, 3), (3, 0)])  4.11 us
  transfers between devices with their start and end apart: 15, of which 6 were waited for; matrix products, arithmetic and copies ran while one was open for 0% of the time, Pallas kernels for 23%

profile of v6, /device:TPU:0, one launch (start us, length us, event | category | flops | bytes accessed | tf_op | source)
XLA Modules:
  0.0 70.5 jit_solution(407464127217280335)
XLA Ops:
  0.0 2.2 %compact.1 = (bf16[2064,128]{1,0:T(8,128)(2,1)S(1)}, bf16[1536,128]{1,0:T(8,128)(2,1)}, bf16[2048,128]{1,0:T(8,128)(2,1)S(1)}, s32[1]{0:T(128)}) custom-call(s32[4,8]{1,0:T(4,128)} %bitcast.4, bf16[8,4,128,128]{3,2,1,0:T(8,128)(2,1)} %refs_4_.1), custom_call_target="tpu_custom_call" | custom-call | bytes 3145728 | tf_op jit(solution)/shard_map/compact/pallas_call | solution.py:524
  2.2 0.7 collective-permute-start.7
  2.9 5.9 %collective-permute-start.4 = (bf16[2064,128]{1,0:T(8,128)(2,1)S(1)}, bf16[2064,128]{1,0:T(8,128)(2,1)}, u32[]{:S(2)}, u32[]{:S(2)}) collective-permute-start(bf16[2064,128]{1,0:T(8,128)(2,1)S(1)} %get-tuple-element.59), channel_id=1, source_target_pairs={{0,1},{1,0},{2,3},{3,2},{4,5},{5,4},{6,7},{7,6},{8,9},{9,8},{10,11... | collective-permute-start | bytes 1585160 | tf_op jit(solution)/shard_map/head_end_swap/ppermute | solution.py:496
  8.8 2.4 %collective-permute-start.10 = (bf16[4,8,128,128]{3,2,1,0:T(8,128)(2,1)}, bf16[4,8,128,128]{3,2,1,0:T(8,128)(2,1)}, u32[]{:S(2)}, u32[]{:S(2)}) collective-permute-start(bf16[4,8,128,128]{3,2,1,0:T(8,128)(2,1)} %refs_12_.1), channel_id=1, source_target_pairs={{0,24},{4,28},{8,0},{12,4},{16,8},{20,12},{24,16},{28,20},{1,25},{... | collective-permute-start | bytes 3145736 | tf_op jit(solution)/shard_map/right_two_up/ppermute | solution.py:23
  11.2 2.0 %collective-permute-start.3 = (bf16[1536,128]{1,0:T(8,128)(2,1)}, bf16[1536,128]{1,0:T(8,128)(2,1)S(1)}, u32[]{:S(2)}, u32[]{:S(2)}) collective-permute-start(bf16[1536,128]{1,0:T(8,128)(2,1)} %get-tuple-element.58), channel_id=1, source_target_pairs={{0,1},{3,2},{4,5},{7,6},{8,9},{11,10},{12,13},{15,14},{16,17},{19,... | collective-permute-start | bytes 1179656 | tf_op jit(solution)/shard_map/tail_inward/ppermute | solution.py:499
  13.2 0.0 collective-permute-done.7.head_ref.refs_2_.refs_9_
  13.2 0.1 extend.1
  13.3 1.3 %collective-permute-start.8 = (bf16[3088,128]{1,0:T(8,128)(2,1)S(1)}, bf16[3088,128]{1,0:T(8,128)(2,1)S(1)}, u32[]{:S(2)}, u32[]{:S(2)}) collective-permute-start(bf16[3088,128]{1,0:T(8,128)(2,1)S(1)} %extend.1), channel_id=1, source_target_pairs={{1,0},{2,3},{5,4},{6,7},{9,8},{10,11},{13,12},{14,15},{17,16},{18,... | collective-permute-start | bytes 2371592 | tf_op jit(solution)/shard_map/second_head_outward/ppermute | solution.py:493
  14.6 6.6 %collective-permute-done.4.refs_0_.refs_5_ = bf16[2064,128]{1,0:T(8,128)(2,1)} collective-permute-done((bf16[2064,128]{1,0:T(8,128)(2,1)S(1)}, bf16[2064,128]{1,0:T(8,128)(2,1)}, u32[]{:S(2)}, u32[]{:S(2)}) %collective-permute-start.4) | collective-permute-done | bytes 528416 | tf_op jit(solution)/shard_map/head_end_swap/ppermute | solution.py:496
  21.2 0.7 collective-permute-start.5
  21.9 0.1 collective-permute-start.11
  22.0 0.0 copy-start.5
  22.0 6.3 %collective-permute-done.3.refs_0_.more_ref.refs_8_ = bf16[1536,128]{1,0:T(8,128)(2,1)S(1)} collective-permute-done((bf16[1536,128]{1,0:T(8,128)(2,1)}, bf16[1536,128]{1,0:T(8,128)(2,1)S(1)}, u32[]{:S(2)}, u32[]{:S(2)}) %collective-permute-start.3) | collective-permute-done | bytes 393248 | tf_op jit(solution)/shard_map/tail_inward/ppermute | solution.py:499
  28.3 2.4 %collective-permute-start.13 = (s32[4,8]{1,0:T(4,128)}, s32[4,8]{1,0:T(4,128)S(1)}, u32[]{:S(2)}, u32[]{:S(2)}) collective-permute-start(s32[4,8]{1,0:T(4,128)} %refs_0_.1), channel_id=1, source_target_pairs={{0,24},{4,28},{8,0},{12,4},{16,8},{20,12},{24,16},{28,20},{1,25},{... | collective-permute-start | bytes 392 | tf_op jit(solution)/shard_map/right_masks/ppermute | solution.py:23
  30.8 0.0 collective-permute-done.5.refs_0_.refs_3_.refs_10_
  30.8 0.0 copy-start.11
  30.8 0.8 %pool.2.refs_1_ = bf16[2304,128]{1,0:T(8,128)(2,1)S(1)} custom-call(s32[1]{0:T(128)} %get-tuple-element.56.n_ref, bf16[2048,128]{1,0:T(8,128)(2,1)S(1)} %get-tuple-element.57.tail_ref, bf16[1536,128]{1,0:T(8,128)(2,1)S(1)} %collective-permute-done.3.refs_0_.more_ref.refs_8_, bf16[2064,128]{1,0:T(8,128)(2,1)S(1)} %collective-permute-done.5.refs_0_.refs_3_.refs_10_, ...), custom_call_target="tpu_custom_call" | custom-call | bytes 1769472 | tf_op jit(solution)/shard_map/pool/pallas_call | solution.py:542
  31.6 0.7 collective-permute-start.9
  32.3 1.2 %collective-permute-done.13.refs_7_.refs_1_.refs_2_ = s32[4,8]{1,0:T(4,128)S(1)} collective-permute-done((s32[4,8]{1,0:T(4,128)}, s32[4,8]{1,0:T(4,128)S(1)}, u32[]{:S(2)}, u32[]{:S(2)}) %collective-permute-start.13) | collective-permute-done | bytes 160 | tf_op jit(solution)/shard_map/right_masks/ppermute | solution.py:23
  33.5 1.3 %collective-permute-start.17 = (bf16[2064,128]{1,0:T(8,128)(2,1)S(1)}, bf16[2064,128]{1,0:T(8,128)(2,1)S(1)}, u32[]{:S(2)}, u32[]{:S(2)}) collective-permute-start(bf16[2064,128]{1,0:T(8,128)(2,1)S(1)} %collective-permute-done.5.refs_0_.refs_3_.refs_10_), channel_id=1, source_target_pairs={{1,0},{2,3},{5,4},{6,7},{9,8},{10,11},{13,12},{14,15},{17,16},{18,... | collective-permute-start | bytes 1585160 | tf_op jit(solution)/shard_map/third_head_outward/ppermute | solution.py:493
  34.8 0.1 pad_add_fusion.where_ref
  34.8 0.0 copy-done.5
  34.8 0.0 collective-permute-done.10.refs_0_.refs_1_
  34.9 3.3 %collective-permute-start.6 = (s32[4,8]{1,0:T(4,128)S(1)}, s32[4,8]{1,0:T(4,128)S(1)}, u32[]{:S(2)}, u32[]{:S(2)}) collective-permute-start(s32[4,8]{1,0:T(4,128)S(1)} %passed.2), channel_id=1, source_target_pairs={{0,3},{3,0},{4,7},{7,4},{8,11},{11,8},{12,15},{15,12},{16,19},{19,... | collective-permute-start | bytes 392 | tf_op jit(solution)/shard_map/far_mask/ppermute | solution.py:577
  38.1 4.1 %collective-permute-done.6.far_ref = s32[4,8]{1,0:T(4,128)S(1)} collective-permute-done((s32[4,8]{1,0:T(4,128)S(1)}, s32[4,8]{1,0:T(4,128)S(1)}, u32[]{:S(2)}, u32[]{:S(2)}) %collective-permute-start.6) | collective-permute-done | bytes 160 | tf_op jit(solution)/shard_map/far_mask/ppermute | solution.py:577
  42.2 0.0 copy-done.11
  42.2 0.0 collective-permute-start.12
  42.2 0.0 collective-permute-done.8.refs_1_.refs_0_.refs_6_
  42.2 0.5 collective-permute-start.14
  42.8 3.3 %table.1 = (s32[200]{0:T(256)S(1)}, s32[1]{0:T(128)}) custom-call(s32[2]{0:T(128)S(1)} %pad_add_fusion.where_ref, s32[4,8]{1,0:T(4,128)S(1)} %bitcast.6, s32[4,8]{1,0:T(4,128)S(1)} %collective-permute-done.6.far_ref, bf16[2064,128]{1,0:T(8,128)(2,1)} %collective-permute-done.4.refs_0_.refs_5_, ...), custom_call_target="tpu_custom_call" | custom-call | tf_op jit(solution)/shard_map/table/pallas_call | solution.py:580
  46.8 0.0 collective-permute-done.12.refs_6_.refs_0_.refs_1_
  46.8 0.0 collective-permute-done.14.refs_8_.refs_2_.refs_3_
  46.8 0.0 collective-permute-done.11.refs_5_.refs_3_.refs_13_
  46.8 0.0 collective-permute-done.9.refs_0_
  46.8 0.8 %pool.3 = bf16[2304,128]{1,0:T(8,128)(2,1)S(1)} custom-call(s32[1]{0:T(128)} %get-tuple-element.56.n_ref, bf16[2048,128]{1,0:T(8,128)(2,1)S(1)} %get-tuple-element.57.tail_ref, bf16[2304,128]{1,0:T(8,128)(2,1)S(1)} %get-tuple-element.62.more_ref.refs_11_), custom_call_target="tpu_custom_call" | custom-call | bytes 1769472 | tf_op jit(solution)/shard_map/pool/pallas_call | solution.py:542
  47.6 1.3 %collective-permute-start.15 = (bf16[2304,128]{1,0:T(8,128)(2,1)S(1)}, bf16[2304,128]{1,0:T(8,128)(2,1)S(1)}, u32[]{:S(2)}, u32[]{:S(2)}) collective-permute-start(bf16[2304,128]{1,0:T(8,128)(2,1)S(1)} %pool.3), channel_id=1, source_target_pairs={{1,0},{2,3},{5,4},{6,7},{9,8},{10,11},{13,12},{14,15},{17,16},{18,... | collective-permute-start | bytes 1769480 | tf_op jit(solution)/shard_map/pool_outward/ppermute | solution.py:493
  48.9 0.2 collective-permute-start.16
  49.1 3.6 %collective-permute-done.17.refs_0_.refs_7_ = bf16[2064,128]{1,0:T(8,128)(2,1)S(1)} collective-permute-done((bf16[2064,128]{1,0:T(8,128)(2,1)S(1)}, bf16[2064,128]{1,0:T(8,128)(2,1)S(1)}, u32[]{:S(2)}, u32[]{:S(2)}) %collective-permute-start.17) | collective-permute-done | bytes 528416 | tf_op jit(solution)/shard_map/third_head_outward/ppermute | solution.py:493
  52.7 0.0 copy-start
  52.7 0.0 copy-start.3
  52.7 0.0 collective-permute-done.16.refs_5_.refs_15_
  52.7 2.4 %rows.1.refs_16_.rows_ref = bf16[1536,1024]{1,0:T(8,128)(2,1)S(1)} custom-call(s32[2]{0:T(128)S(1)} %pad_add_fusion.where_ref, s32[200]{0:T(256)S(1)} %get-tuple-element.61.refs_2_.table_ref, s32[4,8]{1,0:T(4,128)S(1)} %collective-permute-done.12.refs_6_.refs_0_.refs_1_, s32[4,8]{1,0:T(4,128)S(1)} %collective-permute-done.13.refs_7_.refs_1_.refs_2_, ...), custom_call_target="tpu_custom_call" | custom-call | bytes 1048576 | tf_op jit(solution)/shard_map/rows/pallas_call | solution.py:605
  55.0 0.0 copy-done
  55.0 0.0 copy-done.3
  55.1 0.0 copy-done.10
  55.1 8.9 %early.1 = (f32[1024,1024]{1,0:T(8,128)S(1)}, bf16[8,8,128,128]{3,2,1,0:T(8,128)(2,1)}) custom-call(s32[2]{0:T(128)S(1)} %pad_add_fusion.where_ref, s32[4,8]{1,0:T(4,128)S(1)} %bitcast.7, s32[8,8]{1,0:T(8,128)S(1)} %copy-done.10, s32[200]{0:T(256)S(1)} %get-tuple-element.61.refs_2_.table_ref, s32[4,8]{1,0:T(4,128)S(1)} %copy-done.11, ...), custom_call_target="tpu_custom_call" | custom-call | flops 4294967296 | bytes 14680064 | tf_op jit(solution)/shard_map/early/pallas_call | solution.py:626
  64.0 1.3 %collective-permute-done.15.late_ref = bf16[2304,128]{1,0:T(8,128)(2,1)S(1)} collective-permute-done((bf16[2304,128]{1,0:T(8,128)(2,1)S(1)}, bf16[2304,128]{1,0:T(8,128)(2,1)S(1)}, u32[]{:S(2)}, u32[]{:S(2)}) %collective-permute-start.15) | collective-permute-done | bytes 589856 | tf_op jit(solution)/shard_map/pool_outward/ppermute | solution.py:493
  65.3 5.3 %late.1 = (bf16[8,8,128,128]{3,2,1,0:T(8,128)(2,1)}, f32[1024,1024]{1,0:T(8,128)S(1)}) custom-call(s32[2]{0:T(128)S(1)} %pad_add_fusion.where_ref, s32[8,8]{1,0:T(8,128)S(1)} %copy-done.10, s32[200]{0:T(256)S(1)} %get-tuple-element.61.refs_2_.table_ref, ...), custom_call_target="tpu_custom_call", output_to_operand_aliasing={{1}: (5, {}), {0}: (6, {})} | custom-call | bytes 1048576 | tf_op jit(solution)/shard_map/late/pallas_call | solution.py:648
  (9 shorter events, 0.0 us)
Async XLA Ops:
  2.2 11.0 %collective-permute-start.7 = (bf16[2064,128]{1,0:T(8,128)(2,1)S(1)}, bf16[2064,128]{1,0:T(8,128)(2,1)S(1)}, u32[]{:S(2)}, u32[]{:S(2)}) collective-permute-start(bf16[2064,128]{1,0:T(8,128)(2,1)S(1)} %get-tuple-element.59), channel_id=1, source_target_pairs={{1,2},{2,1},{5,6},{6,5},{9,10},{10,9},{13,14},{14,13},{17,18},{18,... | collective-permute-start | bytes 1585160 | tf_op jit(solution)/shard_map/head_over_middle/ppermute | solution.py:502
  2.9 18.3 %collective-permute-start.4 = (bf16[2064,128]{1,0:T(8,128)(2,1)S(1)}, bf16[2064,128]{1,0:T(8,128)(2,1)}, u32[]{:S(2)}, u32[]{:S(2)}) collective-permute-start(bf16[2064,128]{1,0:T(8,128)(2,1)S(1)} %get-tuple-element.59), channel_id=1, source_target_pairs={{0,1},{1,0},{2,3},{3,2},{4,5},{5,4},{6,7},{7,6},{8,9},{9,8},{10,11... | collective-permute-start | bytes 1585160 | tf_op jit(solution)/shard_map/head_end_swap/ppermute | solution.py:496
  8.8 26.1 %collective-permute-start.10 = (bf16[4,8,128,128]{3,2,1,0:T(8,128)(2,1)}, bf16[4,8,128,128]{3,2,1,0:T(8,128)(2,1)}, u32[]{:S(2)}, u32[]{:S(2)}) collective-permute-start(bf16[4,8,128,128]{3,2,1,0:T(8,128)(2,1)} %refs_12_.1), channel_id=1, source_target_pairs={{0,24},{4,28},{8,0},{12,4},{16,8},{20,12},{24,16},{28,20},{1,25},{... | collective-permute-start | bytes 3145736 | tf_op jit(solution)/shard_map/right_two_up/ppermute | solution.py:23
  11.2 17.1 %collective-permute-start.3 = (bf16[1536,128]{1,0:T(8,128)(2,1)}, bf16[1536,128]{1,0:T(8,128)(2,1)S(1)}, u32[]{:S(2)}, u32[]{:S(2)}) collective-permute-start(bf16[1536,128]{1,0:T(8,128)(2,1)} %get-tuple-element.58), channel_id=1, source_target_pairs={{0,1},{3,2},{4,5},{7,6},{8,9},{11,10},{12,13},{15,14},{16,17},{19,... | collective-permute-start | bytes 1179656 | tf_op jit(solution)/shard_map/tail_inward/ppermute | solution.py:499
  13.3 28.9 %collective-permute-start.8 = (bf16[3088,128]{1,0:T(8,128)(2,1)S(1)}, bf16[3088,128]{1,0:T(8,128)(2,1)S(1)}, u32[]{:S(2)}, u32[]{:S(2)}) collective-permute-start(bf16[3088,128]{1,0:T(8,128)(2,1)S(1)} %extend.1), channel_id=1, source_target_pairs={{1,0},{2,3},{5,4},{6,7},{9,8},{10,11},{13,12},{14,15},{17,16},{18,... | collective-permute-start | bytes 2371592 | tf_op jit(solution)/shard_map/second_head_outward/ppermute | solution.py:493
  21.2 9.5 %collective-permute-start.5 = (bf16[2064,128]{1,0:T(8,128)(2,1)}, bf16[2064,128]{1,0:T(8,128)(2,1)S(1)}, u32[]{:S(2)}, u32[]{:S(2)}) collective-permute-start(bf16[2064,128]{1,0:T(8,128)(2,1)} %collective-permute-done.4.refs_0_.refs_5_), channel_id=1, source_target_pairs={{1,2},{2,1},{5,6},{6,5},{9,10},{10,9},{13,14},{14,13},{17,18},{18,... | collective-permute-start | bytes 1585160 | tf_op jit(solution)/shard_map/end_head_over_middle/ppermute | solution.py:502
  21.9 24.9 %collective-permute-start.11 = (bf16[4,8,128,128]{3,2,1,0:T(8,128)(2,1)}, bf16[4,8,128,128]{3,2,1,0:T(8,128)(2,1)}, u32[]{:S(2)}, u32[]{:S(2)}) collective-permute-start(bf16[4,8,128,128]{3,2,1,0:T(8,128)(2,1)} %refs_12_.1), channel_id=1, source_target_pairs={{4,0},{16,4},{12,8},{24,12},{20,16},{0,20},{28,24},{8,28},{5,1},{1... | collective-permute-start | bytes 3145736 | tf_op jit(solution)/shard_map/right_odd_up/ppermute | solution.py:508
  22.0 12.8 %copy-start.5 = (s32[8,4]{0,1:T(4,128)S(1)}, s32[8,4]{0,1:T(4,128)}, u32[]{:S(2)}) copy-start(s32[8,4]{0,1:T(4,128)} %param.8) | copy-start | bytes 388
  28.3 5.2 %collective-permute-start.13 = (s32[4,8]{1,0:T(4,128)}, s32[4,8]{1,0:T(4,128)S(1)}, u32[]{:S(2)}, u32[]{:S(2)}) collective-permute-start(s32[4,8]{1,0:T(4,128)} %refs_0_.1), channel_id=1, source_target_pairs={{0,24},{4,28},{8,0},{12,4},{16,8},{20,12},{24,16},{28,20},{1,25},{... | collective-permute-start | bytes 392 | tf_op jit(solution)/shard_map/right_masks/ppermute | solution.py:23
  30.8 11.5 %copy-start.11 = (s32[4,8]{1,0:T(4,128)S(1)}, s32[4,8]{1,0:T(4,128)}, u32[]{:S(2)}) copy-start(s32[4,8]{1,0:T(4,128)} %refs_0_.1) | copy-start | bytes 388
  31.6 15.2 %collective-permute-start.9 = (bf16[2304,128]{1,0:T(8,128)(2,1)S(1)}, bf16[2304,128]{1,0:T(8,128)(2,1)S(1)}, u32[]{:S(2)}, u32[]{:S(2)}) collective-permute-start(bf16[2304,128]{1,0:T(8,128)(2,1)S(1)} %pool.2.refs_1_), channel_id=1, source_target_pairs={{1,2},{2,1},{5,6},{6,5},{9,10},{10,9},{13,14},{14,13},{17,18},{18,... | collective-permute-start | bytes 1769480 | tf_op jit(solution)/shard_map/pool_over_middle/ppermute | solution.py:502
  33.5 19.2 %collective-permute-start.17 = (bf16[2064,128]{1,0:T(8,128)(2,1)S(1)}, bf16[2064,128]{1,0:T(8,128)(2,1)S(1)}, u32[]{:S(2)}, u32[]{:S(2)}) collective-permute-start(bf16[2064,128]{1,0:T(8,128)(2,1)S(1)} %collective-permute-done.5.refs_0_.refs_3_.refs_10_), channel_id=1, source_target_pairs={{1,0},{2,3},{5,4},{6,7},{9,8},{10,11},{13,12},{14,15},{17,16},{18,... | collective-permute-start | bytes 1585160 | tf_op jit(solution)/shard_map/third_head_outward/ppermute | solution.py:493
  34.9 7.4 %collective-permute-start.6 = (s32[4,8]{1,0:T(4,128)S(1)}, s32[4,8]{1,0:T(4,128)S(1)}, u32[]{:S(2)}, u32[]{:S(2)}) collective-permute-start(s32[4,8]{1,0:T(4,128)S(1)} %passed.2), channel_id=1, source_target_pairs={{0,3},{3,0},{4,7},{7,4},{8,11},{11,8},{12,15},{15,12},{16,19},{19,... | collective-permute-start | bytes 392 | tf_op jit(solution)/shard_map/far_mask/ppermute | solution.py:577
  42.2 4.5 %collective-permute-start.12 = (s32[4,8]{1,0:T(4,128)S(1)}, s32[4,8]{1,0:T(4,128)S(1)}, u32[]{:S(2)}, u32[]{:S(2)}) collective-permute-start(s32[4,8]{1,0:T(4,128)S(1)} %copy-done.11), channel_id=1, source_target_pairs={{4,0},{16,4},{12,8},{24,12},{20,16},{0,20},{28,24},{8,28},{5,1},{1... | collective-permute-start | bytes 392 | tf_op jit(solution)/shard_map/right_masks/ppermute | solution.py:508
  42.2 4.5 %collective-permute-start.14 = (s32[4,8]{1,0:T(4,128)S(1)}, s32[4,8]{1,0:T(4,128)S(1)}, u32[]{:S(2)}, u32[]{:S(2)}) collective-permute-start(s32[4,8]{1,0:T(4,128)S(1)} %collective-permute-done.13.refs_7_.refs_1_.refs_2_), channel_id=1, source_target_pairs={{0,4},{4,0},{8,12},{12,8},{16,20},{20,16},{24,28},{28,24},{1,5},{5... | collective-permute-start | bytes 392 | tf_op jit(solution)/shard_map/right_masks/ppermute | solution.py:511
  47.6 17.7 %collective-permute-start.15 = (bf16[2304,128]{1,0:T(8,128)(2,1)S(1)}, bf16[2304,128]{1,0:T(8,128)(2,1)S(1)}, u32[]{:S(2)}, u32[]{:S(2)}) collective-permute-start(bf16[2304,128]{1,0:T(8,128)(2,1)S(1)} %pool.3), channel_id=1, source_target_pairs={{1,0},{2,3},{5,4},{6,7},{9,8},{10,11},{13,12},{14,15},{17,16},{18,... | collective-permute-start | bytes 1769480 | tf_op jit(solution)/shard_map/pool_outward/ppermute | solution.py:493
  48.9 3.8 %collective-permute-start.16 = (bf16[4,8,128,128]{3,2,1,0:T(8,128)(2,1)}, bf16[4,8,128,128]{3,2,1,0:T(8,128)(2,1)S(1)}, u32[]{:S(2)}, u32[]{:S(2)}) collective-permute-start(bf16[4,8,128,128]{3,2,1,0:T(8,128)(2,1)} %get-tuple-element.63.refs_4_.refs_14_), channel_id=1, source_target_pairs={{0,4},{4,0},{8,12},{12,8},{16,20},{20,16},{24,28},{28,24},{1,5},{5... | collective-permute-start | bytes 3145736 | tf_op jit(solution)/shard_map/right_core_swap/ppermute | solution.py:511
  52.7 2.4 %copy-start = (bf16[8,4,128,128]{3,2,1,0:T(8,128)(2,1)S(1)}, bf16[8,4,128,128]{3,2,1,0:T(8,128)(2,1)}, u32[]{:S(2)}) copy-start(bf16[8,4,128,128]{3,2,1,0:T(8,128)(2,1)} %refs_4_.1) | copy-start | bytes 3145732
  52.7 2.4 %copy-start.3 = (bf16[4,8,128,128]{3,2,1,0:T(8,128)(2,1)S(1)}, bf16[4,8,128,128]{3,2,1,0:T(8,128)(2,1)}, u32[]{:S(2)}) copy-start(bf16[4,8,128,128]{3,2,1,0:T(8,128)(2,1)} %refs_12_.1) | copy-start | bytes 3145732
  52.7 2.4 %copy-start.10 = (s32[8,8]{1,0:T(8,128)S(1)}, s32[8,8]{1,0:T(8,128)}, u32[]{:S(2)}) copy-start(s32[8,8]{1,0:T(8,128)} %c_ref.3) | copy-start | bytes 772

commit v7 on v6

--- a/solution.py
+++ b/solution.py
@@ -8,7 +8,7 @@
 from jax.sharding import PartitionSpec as P
 
 STEPS = 4
-T_TAIL, T_SECOND, T_THIRD, T_RIGHT = 4, 4, 12, 1
+T_TAIL, T_SECOND, T_THIRD, T_RIGHT = 4, 3, 12, 1
 GROUP = 3
 NOTE = 16
 MIB = 1024 * 1024
@@ -550,10 +550,10 @@
             name="pool",
         )(n, own_tail, more, *seen)
 
+    with jax.named_scope("head_end_swap"):
+        near_head = end_swap(own_head)
     with jax.named_scope("head_over_middle"):
         mid_head = over_middle(own_head)
-    with jax.named_scope("head_end_swap"):
-        near_head = end_swap(own_head)
     with jax.named_scope("tail_inward"):
         near_tail = inward(own_inner)
     with jax.named_scope("second_head_outward"):
@@ -572,7 +572,7 @@
         end_head = over_middle(near_head)
     with jax.named_scope("third_head_outward"):
         third_head = outward(end_head)
-    (mid_pool,) = pooled(head, near_tail, [end_head, token([near_tail], T_TAIL)])
+    (mid_pool,) = pooled(head, near_tail, [end_head, token([near_tail], T_TAIL), second_mask, odd_mask])
     with jax.named_scope("far_mask"):
         far_mask = lax.ppermute(*passed([a_mask.T], [mid_pool]), "col", [(0, 3), (3, 0)])
     with jax.named_scope("pool_over_middle"):

time: 69.9 us -> 69 us (0.987); the launches traced: 70.5 us -> 68 us
  waiting for transfers between devices: 23.1 us -> 17 us
  starting transfers between devices: 22.7 us -> 27.5 us
  Pallas kernels: 23.7 us -> 21.8 us
    ppermute x1, waiting for transfers between devices: 6.29 us -> 1.52 us  [inward(): return lax.ppermute(x, 'col', [(0, 1), (3, 2)])]
    ppermute x1, starting transfers between devices: 1.98 us -> 6.28 us  [inward(): return lax.ppermute(x, 'col', [(0, 1), (3, 2)])]
    ppermute x1, waiting for transfers between devices: 6.65 us -> 2.94 us  [end_swap(): return lax.ppermute(x, 'col', [(0, 1), (1, 0), (2, 3), (3, 2)])]
    ppermute x1, starting transfers between devices: 5.88 us -> 3.09 us  [end_swap(): return lax.ppermute(x, 'col', [(0, 1), (1, 0), (2, 3), (3, 2)])]
    ppermute x2, waiting for transfers between devices: 1.21 us -> 3.56 us  [from_behind(): lax.ppermute(array, axis, [(i, (i + by) % size) for i in range(size)])]
    ppermute x2, starting transfers between devices: 0.06 us -> 2.16 us  [odd_up(): lax.ppermute(x, 'row', [((r + 1 + 2 * (r % 2)) % rows, r) for r in range(...]
    pallas_call x1, Pallas kernels: 5.26 us -> 3.45 us  [sparse_product(): pl.pallas_call(functools.partial(late_kernel, part * (pool // len(out_poo...]
    ppermute x2, waiting for transfers between devices: 0.01 us -> 1.51 us  [odd_up(): lax.ppermute(x, 'row', [((r + 1 + 2 * (r % 2)) % rows, r) for r in range(...]
  transfers between devices with their start and end apart: 15 -> 15, of which waited for: 6 -> 7; matrix products, arithmetic and copies ran while one was open for 0% -> 0% of each run, Pallas kernels for 23% -> 24%
where the time goes in v7:
time: 69 us; the launch traced here: 68 us
  starting transfers between devices  27.5 us (40%)
  Pallas kernels  21.8 us (32%)
  waiting for transfers between devices  17 us (25%)
  between operations  1.01 us (1%)
    pallas_call x1, Pallas kernels, sparse_product(): pl.pallas_call(early_kernel, grid=(bc // wide_j,), in_specs=[smem()] * (4...  9.17 us
    ppermute x1, starting transfers between devices, inward(): return lax.ppermute(x, 'col', [(0, 1), (3, 2)])  6.28 us
    ppermute x2, starting transfers between devices, from_behind(): lax.ppermute(array, axis, [(i, (i + by) % size) for i in range(size)])  4.95 us
    ppermute x1, starting transfers between devices, sparse_product(): lax.ppermute(*passed([a_mask.T], [mid_pool]), 'col', [(0, 3), (3, 0)])  4.5 us
    ppermute x3, waiting for transfers between devices, outward(): return lax.ppermute(x, 'col', [(1, 0), (2, 3)])  4.46 us
    ppermute x3, starting transfers between devices, outward(): return lax.ppermute(x, 'col', [(1, 0), (2, 3)])  3.88 us
    ppermute x2, waiting for transfers between devices, from_behind(): lax.ppermute(array, axis, [(i, (i + by) % size) for i in range(size)])  3.56 us
    pallas_call x1, Pallas kernels, sparse_product(): pl.pallas_call(functools.partial(table_kernel, blocks), in_specs=[smem()]...  3.5 us
  transfers between devices with their start and end apart: 15, of which 7 were waited for; matrix products, arithmetic and copies ran while one was open for 0% of the time, Pallas kernels for 24%

profile of v7, /device:TPU:0, one launch (start us, length us, event | category | flops | bytes accessed | tf_op | source)
XLA Modules:
  0.0 68.0 jit_solution(1240388572741152993)
XLA Ops:
  0.0 1.8 %compact.1 = (bf16[2064,128]{1,0:T(8,128)(2,1)S(1)}, bf16[1536,128]{1,0:T(8,128)(2,1)S(1)}, bf16[2048,128]{1,0:T(8,128)(2,1)S(1)}, s32[1]{0:T(128)}) custom-call(s32[4,8]{1,0:T(4,128)} %bitcast.4, bf16[8,4,128,128]{3,2,1,0:T(8,128)(2,1)} %refs_4_.1), custom_call_target="tpu_custom_call" | custom-call | bytes 3145728 | tf_op jit(solution)/shard_map/compact/pallas_call | solution.py:524
  1.8 3.1 %collective-permute-start.4 = (bf16[2064,128]{1,0:T(8,128)(2,1)S(1)}, bf16[2064,128]{1,0:T(8,128)(2,1)S(1)}, u32[]{:S(2)}, u32[]{:S(2)}) collective-permute-start(bf16[2064,128]{1,0:T(8,128)(2,1)S(1)} %get-tuple-element.59), channel_id=1, source_target_pairs={{0,1},{1,0},{2,3},{3,2},{4,5},{5,4},{6,7},{7,6},{8,9},{9,8},{10,11... | collective-permute-start | bytes 1585160 | tf_op jit(solution)/shard_map/head_end_swap/ppermute | solution.py:496
  4.9 0.7 %collective-permute-start.9 = (bf16[2064,128]{1,0:T(8,128)(2,1)S(1)}, bf16[2064,128]{1,0:T(8,128)(2,1)S(1)}, u32[]{:S(2)}, u32[]{:S(2)}) collective-permute-start(bf16[2064,128]{1,0:T(8,128)(2,1)S(1)} %get-tuple-element.59), channel_id=1, source_target_pairs={{1,2},{2,1},{5,6},{6,5},{9,10},{10,9},{13,14},{14,13},{17,18},{18,... | collective-permute-start | bytes 1585160 | tf_op jit(solution)/shard_map/head_over_middle/ppermute | solution.py:502
  5.6 2.5 %collective-permute-start.12 = (bf16[4,8,128,128]{3,2,1,0:T(8,128)(2,1)}, bf16[4,8,128,128]{3,2,1,0:T(8,128)(2,1)}, u32[]{:S(2)}, u32[]{:S(2)}) collective-permute-start(bf16[4,8,128,128]{3,2,1,0:T(8,128)(2,1)} %refs_12_.1), channel_id=1, source_target_pairs={{0,24},{4,28},{8,0},{12,4},{16,8},{20,12},{24,16},{28,20},{1,25},{... | collective-permute-start | bytes 3145736 | tf_op jit(solution)/shard_map/right_two_up/ppermute | solution.py:23
  8.1 6.3 %collective-permute-start.3 = (bf16[1536,128]{1,0:T(8,128)(2,1)S(1)}, bf16[1536,128]{1,0:T(8,128)(2,1)S(1)}, u32[]{:S(2)}, u32[]{:S(2)}) collective-permute-start(bf16[1536,128]{1,0:T(8,128)(2,1)S(1)} %get-tuple-element.58), channel_id=1, source_target_pairs={{0,1},{3,2},{4,5},{7,6},{8,9},{11,10},{12,13},{15,14},{16,17},{19,... | collective-permute-start | bytes 1179656 | tf_op jit(solution)/shard_map/tail_inward/ppermute | solution.py:499
  14.4 2.9 %collective-permute-done.4.refs_0_.refs_5_ = bf16[2064,128]{1,0:T(8,128)(2,1)S(1)} collective-permute-done((bf16[2064,128]{1,0:T(8,128)(2,1)S(1)}, bf16[2064,128]{1,0:T(8,128)(2,1)S(1)}, u32[]{:S(2)}, u32[]{:S(2)}) %collective-permute-start.4) | collective-permute-done | bytes 528416 | tf_op jit(solution)/shard_map/head_end_swap/ppermute | solution.py:496
  17.3 0.7 %collective-permute-start.5 = (bf16[2064,128]{1,0:T(8,128)(2,1)S(1)}, bf16[2064,128]{1,0:T(8,128)(2,1)S(1)}, u32[]{:S(2)}, u32[]{:S(2)}) collective-permute-start(bf16[2064,128]{1,0:T(8,128)(2,1)S(1)} %collective-permute-done.4.refs_0_.refs_5_), channel_id=1, source_target_pairs={{1,2},{2,1},{5,6},{6,5},{9,10},{10,9},{13,14},{14,13},{17,18},{18,... | collective-permute-start | bytes 1585160 | tf_op jit(solution)/shard_map/end_head_over_middle/ppermute | solution.py:502
  18.0 0.0 collective-permute-done.9.head_ref.refs_2_.refs_9_
  18.0 0.1 extend.1
  18.1 0.0 copy-start.15
  18.1 1.3 %collective-permute-start.10 = (bf16[3088,128]{1,0:T(8,128)(2,1)S(1)}, bf16[3088,128]{1,0:T(8,128)(2,1)}, u32[]{:S(2)}, u32[]{:S(2)}) collective-permute-start(bf16[3088,128]{1,0:T(8,128)(2,1)S(1)} %extend.1), channel_id=1, source_target_pairs={{1,0},{2,3},{5,4},{6,7},{9,8},{10,11},{13,12},{14,15},{17,16},{18,... | collective-permute-start | bytes 2371592 | tf_op jit(solution)/shard_map/second_head_outward/ppermute | solution.py:493
  19.4 0.1 collective-permute-start.7
  19.5 1.5 %collective-permute-done.7.refs_3_.refs_6_.refs_0_.refs_1_ = s32[4,8]{1,0:T(4,128)S(1)} collective-permute-done((s32[4,8]{1,0:T(4,128)}, s32[4,8]{1,0:T(4,128)S(1)}, u32[]{:S(2)}, u32[]{:S(2)}) %collective-permute-start.7) | collective-permute-done | bytes 160 | tf_op jit(solution)/shard_map/right_masks/ppermute | solution.py:508
  21.0 2.1 %collective-permute-start.13 = (bf16[4,8,128,128]{3,2,1,0:T(8,128)(2,1)}, bf16[4,8,128,128]{3,2,1,0:T(8,128)(2,1)}, u32[]{:S(2)}, u32[]{:S(2)}) collective-permute-start(bf16[4,8,128,128]{3,2,1,0:T(8,128)(2,1)} %refs_12_.1), channel_id=1, source_target_pairs={{4,0},{16,4},{12,8},{24,12},{20,16},{0,20},{28,24},{8,28},{5,1},{1... | collective-permute-start | bytes 3145736 | tf_op jit(solution)/shard_map/right_odd_up/ppermute | solution.py:508
  23.1 1.5 %collective-permute-done.3.refs_0_.more_ref.refs_8_ = bf16[1536,128]{1,0:T(8,128)(2,1)S(1)} collective-permute-done((bf16[1536,128]{1,0:T(8,128)(2,1)S(1)}, bf16[1536,128]{1,0:T(8,128)(2,1)S(1)}, u32[]{:S(2)}, u32[]{:S(2)}) %collective-permute-start.3) | collective-permute-done | bytes 393248 | tf_op jit(solution)/shard_map/tail_inward/ppermute | solution.py:499
  24.6 2.4 %collective-permute-start.6 = (s32[4,8]{1,0:T(4,128)}, s32[4,8]{1,0:T(4,128)S(1)}, u32[]{:S(2)}, u32[]{:S(2)}) collective-permute-start(s32[4,8]{1,0:T(4,128)} %refs_0_.1), channel_id=1, source_target_pairs={{0,24},{4,28},{8,0},{12,4},{16,8},{20,12},{24,16},{28,20},{1,25},{... | collective-permute-start | bytes 392 | tf_op jit(solution)/shard_map/right_masks/ppermute | solution.py:23
  27.1 0.0 copy-done
  27.1 3.6 %collective-permute-done.6.refs_2_.refs_7_.refs_1_ = s32[4,8]{1,0:T(4,128)S(1)} collective-permute-done((s32[4,8]{1,0:T(4,128)}, s32[4,8]{1,0:T(4,128)S(1)}, u32[]{:S(2)}, u32[]{:S(2)}) %collective-permute-start.6) | collective-permute-done | bytes 160 | tf_op jit(solution)/shard_map/right_masks/ppermute | solution.py:23
  30.6 0.0 collective-permute-done.5.refs_0_.refs_3_.refs_10_
  30.6 0.6 copy-done.11
  31.2 0.7 %pool.2.refs_1_ = bf16[2304,128]{1,0:T(8,128)(2,1)S(1)} custom-call(s32[1]{0:T(128)} %get-tuple-element.56.n_ref, bf16[2048,128]{1,0:T(8,128)(2,1)S(1)} %get-tuple-element.57.tail_ref, bf16[1536,128]{1,0:T(8,128)(2,1)S(1)} %collective-permute-done.3.refs_0_.more_ref.refs_8_, bf16[2064,128]{1,0:T(8,128)(2,1)S(1)} %collective-permute-done.5.refs_0_.refs_3_.refs_10_, ...), custom_call_target="tpu_custom_call" | custom-call | bytes 1769472 | tf_op jit(solution)/shard_map/pool/pallas_call | solution.py:542
  31.9 0.7 %collective-permute-start.11 = (bf16[2304,128]{1,0:T(8,128)(2,1)S(1)}, bf16[2304,128]{1,0:T(8,128)(2,1)S(1)}, u32[]{:S(2)}, u32[]{:S(2)}) collective-permute-start(bf16[2304,128]{1,0:T(8,128)(2,1)S(1)} %pool.2.refs_1_), channel_id=1, source_target_pairs={{1,2},{2,1},{5,6},{6,5},{9,10},{10,9},{13,14},{14,13},{17,18},{18,... | collective-permute-start | bytes 1769480 | tf_op jit(solution)/shard_map/pool_over_middle/ppermute | solution.py:502
  32.6 1.3 %collective-permute-start.17 = (bf16[2064,128]{1,0:T(8,128)(2,1)S(1)}, bf16[2064,128]{1,0:T(8,128)(2,1)}, u32[]{:S(2)}, u32[]{:S(2)}) collective-permute-start(bf16[2064,128]{1,0:T(8,128)(2,1)S(1)} %collective-permute-done.5.refs_0_.refs_3_.refs_10_), channel_id=1, source_target_pairs={{1,0},{2,3},{5,4},{6,7},{9,8},{10,11},{13,12},{14,15},{17,16},{18,... | collective-permute-start | bytes 1585160 | tf_op jit(solution)/shard_map/third_head_outward/ppermute | solution.py:493
  33.9 0.0 copy-done.15
  34.0 0.0 copy-start.1
  34.0 0.1 pad_add_fusion.where_ref
  34.1 0.0 collective-permute-done.12.refs_0_.refs_1_
  34.1 4.5 %collective-permute-start.8 = (s32[4,8]{1,0:T(4,128)S(1)}, s32[4,8]{1,0:T(4,128)S(1)}, u32[]{:S(2)}, u32[]{:S(2)}) collective-permute-start(s32[4,8]{1,0:T(4,128)S(1)} %passed.2), channel_id=1, source_target_pairs={{0,3},{3,0},{4,7},{7,4},{8,11},{11,8},{12,15},{15,12},{16,19},{19,... | collective-permute-start | bytes 392 | tf_op jit(solution)/shard_map/far_mask/ppermute | solution.py:577
  38.6 3.0 %collective-permute-done.8.far_ref = s32[4,8]{1,0:T(4,128)S(1)} collective-permute-done((s32[4,8]{1,0:T(4,128)S(1)}, s32[4,8]{1,0:T(4,128)S(1)}, u32[]{:S(2)}, u32[]{:S(2)}) %collective-permute-start.8) | collective-permute-done | bytes 160 | tf_op jit(solution)/shard_map/far_mask/ppermute | solution.py:577
  41.6 0.0 copy-done.12
  41.6 0.0 collective-permute-start.14
  41.6 0.0 collective-permute-done.10.refs_1_.refs_0_.refs_6_
  41.6 3.5 %table.1 = (s32[200]{0:T(256)S(1)}, s32[1]{0:T(128)}) custom-call(s32[2]{0:T(128)S(1)} %pad_add_fusion.where_ref, s32[4,8]{1,0:T(4,128)} %bitcast.5, s32[4,8]{1,0:T(4,128)S(1)} %collective-permute-done.8.far_ref, bf16[2064,128]{1,0:T(8,128)(2,1)S(1)} %copy-done.1, bf16[3088,128]{1,0:T(8,128)(2,1)} %collective-permute-done.10.refs_1_.refs_0_.refs_6_, ...), custom_call_target="tpu_custom_call" | custom-call | tf_op jit(solution)/shard_map/table/pallas_call | solution.py:580
  45.8 0.0 collective-permute-done.14.refs_8_.refs_2_.refs_3_
  45.8 0.0 collective-permute-done.13.refs_5_.refs_3_.refs_13_
  45.8 0.0 collective-permute-done.11.refs_0_
  45.8 0.7 %pool.3 = bf16[2304,128]{1,0:T(8,128)(2,1)S(1)} custom-call(s32[1]{0:T(128)} %get-tuple-element.56.n_ref, bf16[2048,128]{1,0:T(8,128)(2,1)S(1)} %get-tuple-element.57.tail_ref, bf16[2304,128]{1,0:T(8,128)(2,1)S(1)} %get-tuple-element.62.more_ref.refs_11_), custom_call_target="tpu_custom_call" | custom-call | bytes 1769472 | tf_op jit(solution)/shard_map/pool/pallas_call | solution.py:542
  46.5 1.3 %collective-permute-start.15 = (bf16[2304,128]{1,0:T(8,128)(2,1)S(1)}, bf16[2304,128]{1,0:T(8,128)(2,1)S(1)}, u32[]{:S(2)}, u32[]{:S(2)}) collective-permute-start(bf16[2304,128]{1,0:T(8,128)(2,1)S(1)} %pool.3), channel_id=1, source_target_pairs={{1,0},{2,3},{5,4},{6,7},{9,8},{10,11},{13,12},{14,15},{17,16},{18,... | collective-permute-start | bytes 1769480 | tf_op jit(solution)/shard_map/pool_outward/ppermute | solution.py:493
  47.8 0.6 collective-permute-start.16
  48.4 3.2 %collective-permute-done.17.refs_0_.refs_7_ = bf16[2064,128]{1,0:T(8,128)(2,1)} collective-permute-done((bf16[2064,128]{1,0:T(8,128)(2,1)S(1)}, bf16[2064,128]{1,0:T(8,128)(2,1)}, u32[]{:S(2)}, u32[]{:S(2)}) %collective-permute-start.17) | collective-permute-done | bytes 528416 | tf_op jit(solution)/shard_map/third_head_outward/ppermute | solution.py:493
  51.6 0.0 copy-start.16
  51.6 0.0 copy-start.19
  51.6 0.0 copy-start.20
  51.6 0.0 collective-permute-done.16.refs_5_.refs_15_
  51.6 2.4 %rows.1.refs_16_.rows_ref = bf16[1536,1024]{1,0:T(8,128)(2,1)S(1)} custom-call(s32[2]{0:T(128)S(1)} %pad_add_fusion.where_ref, s32[200]{0:T(256)S(1)} %get-tuple-element.61.refs_2_.table_ref, s32[4,8]{1,0:T(4,128)S(1)} %copy-done.10, s32[4,8]{1,0:T(4,128)S(1)} %copy-done.12, s32[4,8]{1,0:T(4,128)S(1)} %collective-permute-done.14.refs_8_.refs_2_.refs_3_, ...), custom_call_target="tpu_custom_call" | custom-call | bytes 1048576 | tf_op jit(solution)/shard_map/rows/pallas_call | solution.py:605
  54.0 9.2 %early.1 = (f32[1024,1024]{1,0:T(8,128)S(1)}, bf16[8,8,128,128]{3,2,1,0:T(8,128)(2,1)}) custom-call(s32[2]{0:T(128)S(1)} %pad_add_fusion.where_ref, s32[4,8]{1,0:T(4,128)S(1)} %bitcast.7, s32[8,8]{1,0:T(8,128)S(1)} %copy-done.19, s32[200]{0:T(256)S(1)} %get-tuple-element.61.refs_2_.table_ref, s32[4,8]{1,0:T(4,128)S(1)} %copy-done.20, s32[4,8]{1,0:T(4,128)S(1)} %copy-done.10, ...), custom_call_target="tpu_custom_call" | custom-call | flops 4294967296 | bytes 14680064 | tf_op jit(solution)/shard_map/early/pallas_call | solution.py:626
  63.2 1.3 %collective-permute-done.15.late_ref = bf16[2304,128]{1,0:T(8,128)(2,1)S(1)} collective-permute-done((bf16[2304,128]{1,0:T(8,128)(2,1)S(1)}, bf16[2304,128]{1,0:T(8,128)(2,1)S(1)}, u32[]{:S(2)}, u32[]{:S(2)}) %collective-permute-start.15) | collective-permute-done | bytes 589856 | tf_op jit(solution)/shard_map/pool_outward/ppermute | solution.py:493
  64.5 3.5 %late.1 = (bf16[8,8,128,128]{3,2,1,0:T(8,128)(2,1)}, f32[1024,1024]{1,0:T(8,128)S(1)}) custom-call(s32[2]{0:T(128)S(1)} %pad_add_fusion.where_ref, s32[8,8]{1,0:T(8,128)S(1)} %copy-done.19, s32[200]{0:T(256)S(1)} %get-tuple-element.61.refs_2_.table_ref, ...), custom_call_target="tpu_custom_call", output_to_operand_aliasing={{1}: (5, {}), {0}: (6, {})} | custom-call | bytes 1048576 | tf_op jit(solution)/shard_map/late/pallas_call | solution.py:648
  (27 shorter events, 0.1 us)
Async XLA Ops:
  1.8 15.5 %collective-permute-start.4 = (bf16[2064,128]{1,0:T(8,128)(2,1)S(1)}, bf16[2064,128]{1,0:T(8,128)(2,1)S(1)}, u32[]{:S(2)}, u32[]{:S(2)}) collective-permute-start(bf16[2064,128]{1,0:T(8,128)(2,1)S(1)} %get-tuple-element.59), channel_id=1, source_target_pairs={{0,1},{1,0},{2,3},{3,2},{4,5},{5,4},{6,7},{7,6},{8,9},{9,8},{10,11... | collective-permute-start | bytes 1585160 | tf_op jit(solution)/shard_map/head_end_swap/ppermute | solution.py:496
  4.9 13.1 %collective-permute-start.9 = (bf16[2064,128]{1,0:T(8,128)(2,1)S(1)}, bf16[2064,128]{1,0:T(8,128)(2,1)S(1)}, u32[]{:S(2)}, u32[]{:S(2)}) collective-permute-start(bf16[2064,128]{1,0:T(8,128)(2,1)S(1)} %get-tuple-element.59), channel_id=1, source_target_pairs={{1,2},{2,1},{5,6},{6,5},{9,10},{10,9},{13,14},{14,13},{17,18},{18,... | collective-permute-start | bytes 1585160 | tf_op jit(solution)/shard_map/head_over_middle/ppermute | solution.py:502
  5.6 28.5 %collective-permute-start.12 = (bf16[4,8,128,128]{3,2,1,0:T(8,128)(2,1)}, bf16[4,8,128,128]{3,2,1,0:T(8,128)(2,1)}, u32[]{:S(2)}, u32[]{:S(2)}) collective-permute-start(bf16[4,8,128,128]{3,2,1,0:T(8,128)(2,1)} %refs_12_.1), channel_id=1, source_target_pairs={{0,24},{4,28},{8,0},{12,4},{16,8},{20,12},{24,16},{28,20},{1,25},{... | collective-permute-start | bytes 3145736 | tf_op jit(solution)/shard_map/right_two_up/ppermute | solution.py:23
  8.1 16.5 %collective-permute-start.3 = (bf16[1536,128]{1,0:T(8,128)(2,1)S(1)}, bf16[1536,128]{1,0:T(8,128)(2,1)S(1)}, u32[]{:S(2)}, u32[]{:S(2)}) collective-permute-start(bf16[1536,128]{1,0:T(8,128)(2,1)S(1)} %get-tuple-element.58), channel_id=1, source_target_pairs={{0,1},{3,2},{4,5},{7,6},{8,9},{11,10},{12,13},{15,14},{16,17},{19,... | collective-permute-start | bytes 1179656 | tf_op jit(solution)/shard_map/tail_inward/ppermute | solution.py:499
  17.3 9.7 %copy-start = (bf16[2064,128]{1,0:T(8,128)(2,1)}, bf16[2064,128]{1,0:T(8,128)(2,1)S(1)}, u32[]{:S(2)}) copy-start(bf16[2064,128]{1,0:T(8,128)(2,1)S(1)} %collective-permute-done.4.refs_0_.refs_5_) | copy-start | bytes 1585156
  17.3 13.3 %collective-permute-start.5 = (bf16[2064,128]{1,0:T(8,128)(2,1)S(1)}, bf16[2064,128]{1,0:T(8,128)(2,1)S(1)}, u32[]{:S(2)}, u32[]{:S(2)}) collective-permute-start(bf16[2064,128]{1,0:T(8,128)(2,1)S(1)} %collective-permute-done.4.refs_0_.refs_5_), channel_id=1, source_target_pairs={{1,2},{2,1},{5,6},{6,5},{9,10},{10,9},{13,14},{14,13},{17,18},{18,... | collective-permute-start | bytes 1585160 | tf_op jit(solution)/shard_map/end_head_over_middle/ppermute | solution.py:502
  18.1 15.9 %copy-start.15 = (s32[8,4]{0,1:T(4,128)S(1)}, s32[8,4]{0,1:T(4,128)}, u32[]{:S(2)}) copy-start(s32[8,4]{0,1:T(4,128)} %param.8) | copy-start | bytes 388
  18.1 23.5 %collective-permute-start.10 = (bf16[3088,128]{1,0:T(8,128)(2,1)S(1)}, bf16[3088,128]{1,0:T(8,128)(2,1)}, u32[]{:S(2)}, u32[]{:S(2)}) collective-permute-start(bf16[3088,128]{1,0:T(8,128)(2,1)S(1)} %extend.1), channel_id=1, source_target_pairs={{1,0},{2,3},{5,4},{6,7},{9,8},{10,11},{13,12},{14,15},{17,16},{18,... | collective-permute-start | bytes 2371592 | tf_op jit(solution)/shard_map/second_head_outward/ppermute | solution.py:493
  19.4 1.6 %collective-permute-start.7 = (s32[4,8]{1,0:T(4,128)}, s32[4,8]{1,0:T(4,128)S(1)}, u32[]{:S(2)}, u32[]{:S(2)}) collective-permute-start(s32[4,8]{1,0:T(4,128)} %refs_0_.1), channel_id=1, source_target_pairs={{4,0},{16,4},{12,8},{24,12},{20,16},{0,20},{28,24},{8,28},{5,1},{1... | collective-permute-start | bytes 392 | tf_op jit(solution)/shard_map/right_masks/ppermute | solution.py:508
  21.0 9.6 %copy-start.9 = (s32[4,8]{1,0:T(4,128)}, s32[4,8]{1,0:T(4,128)S(1)}, u32[]{:S(2)}) copy-start(s32[4,8]{1,0:T(4,128)S(1)} %collective-permute-done.7.refs_3_.refs_6_.refs_0_.refs_1_) | copy-start | bytes 388
  21.0 24.8 %collective-permute-start.13 = (bf16[4,8,128,128]{3,2,1,0:T(8,128)(2,1)}, bf16[4,8,128,128]{3,2,1,0:T(8,128)(2,1)}, u32[]{:S(2)}, u32[]{:S(2)}) collective-permute-start(bf16[4,8,128,128]{3,2,1,0:T(8,128)(2,1)} %refs_12_.1), channel_id=1, source_target_pairs={{4,0},{16,4},{12,8},{24,12},{20,16},{0,20},{28,24},{8,28},{5,1},{1... | collective-permute-start | bytes 3145736 | tf_op jit(solution)/shard_map/right_odd_up/ppermute | solution.py:508
  24.6 6.0 %copy-start.2 = (bf16[1536,128]{1,0:T(8,128)(2,1)}, bf16[1536,128]{1,0:T(8,128)(2,1)S(1)}, u32[]{:S(2)}) copy-start(bf16[1536,128]{1,0:T(8,128)(2,1)S(1)} %collective-permute-done.3.refs_0_.more_ref.refs_8_) | copy-start | bytes 1179652
  24.6 6.0 %collective-permute-start.6 = (s32[4,8]{1,0:T(4,128)}, s32[4,8]{1,0:T(4,128)S(1)}, u32[]{:S(2)}, u32[]{:S(2)}) collective-permute-start(s32[4,8]{1,0:T(4,128)} %refs_0_.1), channel_id=1, source_target_pairs={{0,24},{4,28},{8,0},{12,4},{16,8},{20,12},{24,16},{28,20},{1,25},{... | collective-permute-start | bytes 392 | tf_op jit(solution)/shard_map/right_masks/ppermute | solution.py:23
  30.6 0.6 copy-start.11
  31.9 13.9 %collective-permute-start.11 = (bf16[2304,128]{1,0:T(8,128)(2,1)S(1)}, bf16[2304,128]{1,0:T(8,128)(2,1)S(1)}, u32[]{:S(2)}, u32[]{:S(2)}) collective-permute-start(bf16[2304,128]{1,0:T(8,128)(2,1)S(1)} %pool.2.refs_1_), channel_id=1, source_target_pairs={{1,2},{2,1},{5,6},{6,5},{9,10},{10,9},{13,14},{14,13},{17,18},{18,... | collective-permute-start | bytes 1769480 | tf_op jit(solution)/shard_map/pool_over_middle/ppermute | solution.py:502
  32.6 18.9 %collective-permute-start.17 = (bf16[2064,128]{1,0:T(8,128)(2,1)S(1)}, bf16[2064,128]{1,0:T(8,128)(2,1)}, u32[]{:S(2)}, u32[]{:S(2)}) collective-permute-start(bf16[2064,128]{1,0:T(8,128)(2,1)S(1)} %collective-permute-done.5.refs_0_.refs_3_.refs_10_), channel_id=1, source_target_pairs={{1,0},{2,3},{5,4},{6,7},{9,8},{10,11},{13,12},{14,15},{17,16},{18,... | collective-permute-start | bytes 1585160 | tf_op jit(solution)/shard_map/third_head_outward/ppermute | solution.py:493
  34.0 7.6 %copy-start.12 = (s32[4,8]{1,0:T(4,128)S(1)}, s32[4,8]{1,0:T(4,128)}, u32[]{:S(2)}) copy-start(s32[4,8]{1,0:T(4,128)} %copy-done.11) | copy-start | bytes 388
  34.0 7.6 %copy-start.1 = (bf16[2064,128]{1,0:T(8,128)(2,1)S(1)}, bf16[2064,128]{1,0:T(8,128)(2,1)}, u32[]{:S(2)}) copy-start(bf16[2064,128]{1,0:T(8,128)(2,1)} %copy-done) | copy-start | bytes 1585156
  34.1 7.5 %collective-permute-start.8 = (s32[4,8]{1,0:T(4,128)S(1)}, s32[4,8]{1,0:T(4,128)S(1)}, u32[]{:S(2)}, u32[]{:S(2)}) collective-permute-start(s32[4,8]{1,0:T(4,128)S(1)} %passed.2), channel_id=1, source_target_pairs={{0,3},{3,0},{4,7},{7,4},{8,11},{11,8},{12,15},{15,12},{16,19},{19,... | collective-permute-start | bytes 392 | tf_op jit(solution)/shard_map/far_mask/ppermute | solution.py:577
  41.6 4.2 %collective-permute-start.14 = (s32[4,8]{1,0:T(4,128)S(1)}, s32[4,8]{1,0:T(4,128)S(1)}, u32[]{:S(2)}, u32[]{:S(2)}) collective-permute-start(s32[4,8]{1,0:T(4,128)S(1)} %copy-done.12), channel_id=1, source_target_pairs={{0,4},{4,0},{8,12},{12,8},{16,20},{20,16},{24,28},{28,24},{1,5},{5... | collective-permute-start | bytes 392 | tf_op jit(solution)/shard_map/right_masks/ppermute | solution.py:511
  45.1 0.7 %copy-start.10 = (s32[4,8]{1,0:T(4,128)S(1)}, s32[4,8]{1,0:T(4,128)}, u32[]{:S(2)}) copy-start(s32[4,8]{1,0:T(4,128)} %copy-done.9) | copy-start | bytes 388
  46.5 18.0 %collective-permute-start.15 = (bf16[2304,128]{1,0:T(8,128)(2,1)S(1)}, bf16[2304,128]{1,0:T(8,128)(2,1)S(1)}, u32[]{:S(2)}, u32[]{:S(2)}) collective-permute-start(bf16[2304,128]{1,0:T(8,128)(2,1)S(1)} %pool.3), channel_id=1, source_target_pairs={{1,0},{2,3},{5,4},{6,7},{9,8},{10,11},{13,12},{14,15},{17,16},{18,... | collective-permute-start | bytes 1769480 | tf_op jit(solution)/shard_map/pool_outward/ppermute | solution.py:493
  47.8 3.8 %collective-permute-start.16 = (bf16[4,8,128,128]{3,2,1,0:T(8,128)(2,1)}, bf16[4,8,128,128]{3,2,1,0:T(8,128)(2,1)S(1)}, u32[]{:S(2)}, u32[]{:S(2)}) collective-permute-start(bf16[4,8,128,128]{3,2,1,0:T(8,128)(2,1)} %get-tuple-element.63.refs_4_.refs_14_), channel_id=1, source_target_pairs={{0,4},{4,0},{8,12},{12,8},{16,20},{20,16},{24,28},{28,24},{1,5},{5... | collective-permute-start | bytes 3145736 | tf_op jit(solution)/shard_map/right_core_swap/ppermute | solution.py:511
  51.6 2.4 %copy-start.3 = (bf16[1536,128]{1,0:T(8,128)(2,1)S(1)}, bf16[1536,128]{1,0:T(8,128)(2,1)}, u32[]{:S(2)}) copy-start(bf16[1536,128]{1,0:T(8,128)(2,1)} %copy-done.2) | copy-start | bytes 1179652
  51.6 2.4 %copy-start.4 = (bf16[8,4,128,128]{3,2,1,0:T(8,128)(2,1)S(1)}, bf16[8,4,128,128]{3,2,1,0:T(8,128)(2,1)}, u32[]{:S(2)}) copy-start(bf16[8,4,128,128]{3,2,1,0:T(8,128)(2,1)} %refs_4_.1) | copy-start | bytes 3145732
  51.6 2.4 %copy-start.7 = (bf16[4,8,128,128]{3,2,1,0:T(8,128)(2,1)S(1)}, bf16[4,8,128,128]{3,2,1,0:T(8,128)(2,1)}, u32[]{:S(2)}) copy-start(bf16[4,8,128,128]{3,2,1,0:T(8,128)(2,1)} %refs_12_.1) | copy-start | bytes 3145732
  51.6 2.4 %copy-start.16 = (s32[8,4]{0,1:T(4,128)S(1)}, s32[8,4]{0,1:T(4,128)}, u32[]{:S(2)}) copy-start(s32[8,4]{0,1:T(4,128)} %param.8) | copy-start | bytes 388
  51.6 2.4 %copy-start.19 = (s32[8,8]{1,0:T(8,128)S(1)}, s32[8,8]{1,0:T(8,128)}, u32[]{:S(2)}) copy-start(s32[8,8]{1,0:T(8,128)} %c_ref.3) | copy-start | bytes 772
  51.6 2.4 %copy-start.20 = (s32[4,8]{1,0:T(4,128)S(1)}, s32[4,8]{1,0:T(4,128)}, u32[]{:S(2)}) copy-start(s32[4,8]{1,0:T(4,128)} %refs_0_.1) | copy-start | bytes 388
